TPU v7x, 32 devices: a whole 2x2x4 slice. The times are simulated.
32 devices in a mesh: dp: 16 (over z, y, x), tensor: 2 (over core).
Axes of the slice: x: 2, y: 2, z: 4, core: 2. Of those that a mesh axis runs over, the one named last changes fastest.
Arguments:
- tokens: bfloat16 [8192, 2048], P(('dp', 'tensor')), may hold values from -6 to 6
- cotangent: bfloat16 [8192, 2048], P(('dp', 'tensor')), may hold values from -6 to 6
- lengths: int32 [16, 4], P('dp'), may hold values from 1 to 509, as said below
- slot_of: int32 [8192], P(('dp', 'tensor')), may hold values from 0 to 8191, as said below
- norm_gains: float32 [2, 2048], replicated, may hold values from 0.5 to 1.5
- w_query: bfloat16 [2048, 2048], P('dp', 'tensor'), may hold values from -0.125 to 0.125
- w_key: bfloat16 [2048, 2048], P('dp', 'tensor'), may hold values from -0.125 to 0.125
- w_value: bfloat16 [2048, 4096], P('dp', 'tensor'), may hold values from -0.125 to 0.125
- w_gate: bfloat16 [2048, 4096], P('dp', 'tensor'), may hold values from -0.125 to 0.125
- w_decay: bfloat16 [2048, 16], P('dp', 'tensor'), may hold values from -0.125 to 0.125
- w_beta: bfloat16 [2048, 16], P('dp', 'tensor'), may hold values from -0.125 to 0.125
- conv_weights: float32 [4, 8192], replicated, may hold values from -3 to 3
- a_log: float32 [16], replicated, may hold values from -8 to -2.5
- dt_bias: float32 [16], replicated, may hold values from -2 to 0
- out_gain: float32 [256], replicated, may hold values from 0.5 to 1.5
- w_out: bfloat16 [4096, 2048], P('tensor', 'dp'), may hold values from -0.1875 to 0.1875
- w_mlp_gate: bfloat16 [2048, 5632], P('dp', 'tensor'), may hold values from -0.125 to 0.125
- w_mlp_up: bfloat16 [2048, 5632], P('dp', 'tensor'), may hold values from -0.125 to 0.125
- w_mlp_down: bfloat16 [5632, 2048], P('tensor', 'dp'), may hold values from -0.15625 to 0.15625
Outputs:
- output: bfloat16 [8192, 2048], P(('dp', 'tensor'))
- tokens_grad: bfloat16 [8192, 2048], P(('dp', 'tensor'))
- norm_gains_grad: float32 [2, 2048], replicated
- w_query_grad: float32 [2048, 2048], P('dp', 'tensor')
- w_key_grad: float32 [2048, 2048], P('dp', 'tensor')
- w_value_grad: float32 [2048, 4096], P('dp', 'tensor')
- w_gate_grad: float32 [2048, 4096], P('dp', 'tensor')
- w_decay_grad: float32 [2048, 16], P('dp', 'tensor')
- w_beta_grad: float32 [2048, 16], P('dp', 'tensor')
- conv_weights_grad: float32 [4, 8192], replicated
- a_log_grad: float32 [16], replicated
- dt_bias_grad: float32 [16], replicated
- out_gain_grad: float32 [256], replicated
- w_out_grad: float32 [4096, 2048], P('tensor', 'dp')
- w_mlp_gate_grad: float32 [2048, 5632], P('dp', 'tensor')
- w_mlp_up_grad: float32 [2048, 5632], P('dp', 'tensor')
- w_mlp_down_grad: float32 [5632, 2048], P('tensor', 'dp')
Inputs may be any that keep to these rules, and one draw needn't show every extreme that they name: `slot_of`: A permutation of the slots; slot s lies on device s // 256 of the dp+tensor order. Each device sends at most 10 of its tokens to any one device, sends exactly 10 to one device and receives exactly 10 from one device. Each group's lengths fill its first slots in order and sum to 260 or more; in every group one sequence covers slots of all its tensor devices; some group holds a sequence of 509.
All inputs are finite; a program needn't handle non-finite values.
Results may differ from a plain program's by a relative error of at most 0.028.
Values may be sent and summed in bfloat16 or wider, within the bound.
No kernel may reach another device: no remote copies, remote signals or barrier semaphores. Data moves between devices by JAX's collectives and lax.ppermute only.
A program may use at most 448 MiB of HBM per device.

v0:
```python
import jax
import jax.numpy as jnp
from jax import lax
from jax.sharding import PartitionSpec as P

HEADS = 16
DK = 128
DV = 256
BLOCK = 64


EPS_ROW = 1e-06
EPS_UNIT = 1e-06
EPS_HEAD = 1e-05
HIGH = lax.Precision.HIGHEST


def matmul(left, right):
    return jnp.dot(left, right, preferred_element_type=jnp.float32)


def outer_sum(left, right):
    return lax.dot_general(
        left, right, (((0,), (0,)), ((), ())), preferred_element_type=jnp.float32
    )


def times_back(left, right):
    return lax.dot_general(
        left, right, (((1,), (1,)), ((), ())), preferred_element_type=jnp.float32
    )


def unit_rows(values):
    return values * lax.rsqrt(jnp.sum(values * values, axis=-1, keepdims=True) + EPS_UNIT)


def rounded(values):
    return lax.optimization_barrier(values.astype(jnp.bfloat16)).astype(jnp.float32)


def group_marks(lengths, group_rows):
    seq_ends = jnp.cumsum(lengths[0])
    begins = seq_ends - lengths[0]
    position = jnp.arange(group_rows, dtype=jnp.int32)
    starts = jnp.any(position[:, None] == begins[None, :], axis=1).astype(jnp.float32)
    live_mask = (position < seq_ends[-1]).astype(jnp.float32)
    segment = jnp.cumsum(starts.astype(jnp.int32))
    return (starts, live_mask, segment)


def norm_back(inputs, scale, gain, grad_out):
    scaled = grad_out * gain
    grad_in = scale * scaled - inputs * scale**3 * jnp.mean(scaled * inputs, axis=1, keepdims=True)
    return (grad_in, jnp.sum(grad_out * inputs * scale, axis=0))


def conv_part(proj_q, proj_k, proj_v, conv_taps, segment):
    joined = jnp.concatenate([proj_q, proj_k, proj_v], axis=1)
    summed = conv_taps[0] * joined
    for offset in range(1, conv_taps.shape[0]):
        shifted = jnp.pad(joined, ((offset, 0), (0, 0)))[:-offset]
        before = jnp.pad(segment, (offset, 0), constant_values=-1)[:-offset]
        summed = (
            summed + conv_taps[offset] * shifted * (before == segment).astype(jnp.float32)[:, None]
        )
    activated = jax.nn.silu(summed)
    row_count = joined.shape[0]
    key_width = proj_q.shape[1]
    queries = unit_rows(activated[:, :key_width].reshape(row_count, -1, DK)) * DK ** (-0.5)
    key_vecs = unit_rows(activated[:, key_width : 2 * key_width].reshape(row_count, -1, DK))
    values = activated[:, 2 * key_width :].reshape(row_count, -1, DV)
    return (queries, key_vecs, values)


def block_rule(memory, pieces):
    queries, key_vecs, values, log_decay, beta_gate, starts = pieces
    block_len = starts.shape[0]
    segment = jnp.cumsum(starts)
    cum_log = jnp.cumsum(log_decay, axis=0).T
    places = jnp.arange(block_len)
    causal = ((places[:, None] >= places[None, :]) & (segment[:, None] == segment[None, :]))[None]
    log_gap = jnp.where(causal, cum_log[:, :, None] - cum_log[:, None, :], 0.0)
    decay_mat = jnp.where(causal, jnp.exp(log_gap), 0.0)
    opening = jnp.where((segment == 0)[None, :], jnp.exp(cum_log), 0.0)
    beta_rows = beta_gate.T
    key_dots = jnp.einsum("ihd,jhd->hij", key_vecs, key_vecs, precision=HIGH)
    strict = (places[:, None] > places[None, :])[None]
    system = jnp.where(strict, beta_rows[:, :, None] * key_dots * decay_mat, 0.0) + jnp.eye(
        block_len, dtype=jnp.float32
    )
    right_side = jnp.concatenate(
        [
            beta_rows[:, :, None] * values.transpose(1, 0, 2),
            (beta_rows * opening)[:, :, None] * key_vecs.transpose(1, 0, 2),
        ],
        axis=2,
    )
    solved = jax.scipy.linalg.solve_triangular(system, right_side, lower=True, unit_diagonal=True)
    value_dim = values.shape[2]
    new_values = solved[:, :, :value_dim] - jnp.einsum(
        "hik,hvk->hiv", solved[:, :, value_dim:], memory, precision=HIGH
    )
    scores = jnp.einsum("ihd,jhd->hij", queries, key_vecs, precision=HIGH) * decay_mat
    outputs = opening[:, :, None] * jnp.einsum(
        "hvk,ihk->hiv", memory, queries, precision=HIGH
    ) + jnp.einsum("hij,hjv->hiv", scores, new_values, precision=HIGH)
    memory = opening[:, -1][:, None, None] * memory + jnp.einsum(
        "hj,hjv,jhk->hvk", decay_mat[:, -1, :], new_values, key_vecs, precision=HIGH
    )
    return (memory, outputs.transpose(1, 0, 2))


def mixer_core(
    queries, key_vecs, values, decay_in, beta_in, gate_in, decay_log, decay_bias, out_gain, starts
):
    row_count = queries.shape[0]
    head_count = queries.shape[1]
    beta_gate = jax.nn.sigmoid(beta_in)
    log_decay = -jnp.exp(decay_log) * jax.nn.softplus(decay_in + decay_bias)
    pieces = tuple(
        (
            member.reshape((row_count // BLOCK, BLOCK) + member.shape[1:])
            for member in (queries, key_vecs, values, log_decay, beta_gate, starts)
        )
    )
    initial = jnp.zeros((head_count, values.shape[2], queries.shape[2]), jnp.float32)
    _, results = lax.scan(block_rule, initial, pieces)
    mixture = results.reshape(row_count, head_count, -1)
    normed = (
        mixture
        * lax.rsqrt(jnp.mean(mixture * mixture, axis=2, keepdims=True) + EPS_HEAD)
        * out_gain
    )
    return (normed * jax.nn.silu(gate_in.reshape(mixture.shape))).reshape(row_count, -1)


def group_of(values):
    return lax.all_gather(values, "tensor", axis=0, tiled=True)


def own_of(values):
    return lax.psum_scatter(
        values.astype(jnp.bfloat16), "tensor", scatter_dimension=0, tiled=True
    ).astype(jnp.float32)


def gather_mixer(w_query, w_key, w_value, w_gate, w_decay, w_beta, w_out):
    return (
        lax.all_gather(w_query, "dp", axis=0, tiled=True),
        lax.all_gather(w_key, "dp", axis=0, tiled=True),
        lax.all_gather(w_value, "dp", axis=0, tiled=True),
        lax.all_gather(w_gate, "dp", axis=0, tiled=True),
        lax.all_gather(w_decay, "dp", axis=0, tiled=True),
        lax.all_gather(w_beta, "dp", axis=0, tiled=True),
        lax.all_gather(w_out, "dp", axis=1, tiled=True),
    )


def gather_mlp(w_mlp_gate, w_mlp_up, w_mlp_down):
    return (
        lax.all_gather(w_mlp_gate, "dp", axis=0, tiled=True),
        lax.all_gather(w_mlp_up, "dp", axis=0, tiled=True),
        lax.all_gather(w_mlp_down, "dp", axis=1, tiled=True),
    )


def route_in(send_tokens, send_cot, send_slot):
    arrived = (
        lax.all_to_all(send_tokens, ("dp", "tensor"), split_axis=0, concat_axis=0, tiled=True),
        lax.all_to_all(send_cot, ("dp", "tensor"), split_axis=0, concat_axis=0, tiled=True),
        lax.all_to_all(send_slot, ("dp", "tensor"), split_axis=0, concat_axis=0, tiled=True),
    )
    return arrived


def route_out(back_out, back_grad):
    returned = (
        lax.all_to_all(back_out, ("dp", "tensor"), split_axis=0, concat_axis=0, tiled=True),
        lax.all_to_all(back_grad, ("dp", "tensor"), split_axis=0, concat_axis=0, tiled=True),
    )
    return returned


def shards(
    tokens,
    cotangent,
    lengths,
    slot_of,
    norm_gains,
    w_query,
    w_key,
    w_value,
    w_gate,
    w_decay,
    w_beta,
    conv_weights,
    a_log,
    dt_bias,
    out_gain,
    w_out,
    w_mlp_gate,
    w_mlp_up,
    w_mlp_down,
):
    row_count = tokens.shape[0]
    feature_dim = tokens.shape[1]
    tensor_ways = lax.axis_size("tensor")
    dp_ways = lax.axis_size("dp")
    device_count = dp_ways * tensor_ways
    tensor_rank = lax.axis_index("tensor")
    group_rows = row_count * tensor_ways
    capacity = row_count // device_count + 2
    bulk_rows = device_count * capacity
    heads_here = HEADS // tensor_ways
    keys_here = heads_here * DK
    vals_here = heads_here * DV
    all_keys = HEADS * DK
    target = slot_of // row_count
    within = slot_of % row_count
    target_hits = (target[:, None] == jnp.arange(device_count, dtype=jnp.int32)[None, :]).astype(
        jnp.int32
    )
    send_rank = jnp.sum(jnp.cumsum(target_hits, axis=0) * target_hits, axis=1) - 1
    outgoing = target * capacity + send_rank
    send_tokens = jnp.zeros((bulk_rows, feature_dim), jnp.bfloat16).at[outgoing].set(tokens)
    send_cot = jnp.zeros((bulk_rows, feature_dim), jnp.bfloat16).at[outgoing].set(cotangent)
    send_slot = jnp.full((bulk_rows,), -1, jnp.int32).at[outgoing].set(within)
    got_tokens, got_cot, got_slot = route_in(send_tokens, send_cot, send_slot)
    landing = jnp.where(got_slot < 0, row_count, got_slot)
    x_own = (
        jnp.zeros((row_count, feature_dim), jnp.bfloat16)
        .at[landing]
        .set(got_tokens, mode="drop")
        .astype(jnp.float32)
    )
    dy_own = (
        jnp.zeros((row_count, feature_dim), jnp.bfloat16)
        .at[landing]
        .set(got_cot, mode="drop")
        .astype(jnp.float32)
    )
    starts, live_mask, segment = group_marks(lengths, group_rows)
    live_own = lax.dynamic_slice_in_dim(live_mask, tensor_rank * row_count, row_count)[:, None]
    conv_taps = jnp.concatenate(
        [
            lax.dynamic_slice_in_dim(conv_weights, tensor_rank * keys_here, keys_here, 1),
            lax.dynamic_slice_in_dim(
                conv_weights, all_keys + tensor_rank * keys_here, keys_here, 1
            ),
            lax.dynamic_slice_in_dim(
                conv_weights, 2 * all_keys + tensor_rank * vals_here, vals_here, 1
            ),
        ],
        axis=1,
    )
    decay_log = lax.dynamic_slice_in_dim(a_log, tensor_rank * heads_here, heads_here)
    decay_bias = lax.dynamic_slice_in_dim(dt_bias, tensor_rank * heads_here, heads_here)
    mixer_set = gather_mixer(w_query, w_key, w_value, w_gate, w_decay, w_beta, w_out)
    scale_one = lax.rsqrt(jnp.mean(x_own * x_own, axis=1, keepdims=True) + EPS_ROW)
    first_in = (x_own * scale_one * norm_gains[0]).astype(jnp.bfloat16)
    first_rows = group_of(first_in)
    projected = [matmul(first_rows, weight) for weight in mixer_set[:6]]

    def conv_fn(proj_q, proj_k, proj_v, taps_in):
        return conv_part(proj_q, proj_k, proj_v, taps_in, segment)

    conv_out, conv_pull = jax.vjp(conv_fn, projected[0], projected[1], projected[2], conv_taps)
    queries = rounded(conv_out[0])
    key_vecs = rounded(conv_out[1])
    values = rounded(conv_out[2])

    def core_fn(
        queries_in, keys_in, values_in, decay_in, beta_in, gate_in, log_in, bias_in, gain_in
    ):
        return mixer_core(
            queries_in,
            keys_in,
            values_in,
            decay_in,
            beta_in,
            gate_in,
            log_in,
            bias_in,
            gain_in,
            starts,
        )

    heads_full, core_pull = jax.vjp(
        core_fn,
        queries,
        key_vecs,
        values,
        projected[4],
        projected[5],
        projected[3],
        decay_log,
        decay_bias,
        out_gain,
    )
    heads_out = heads_full.astype(jnp.bfloat16)
    mix_own = own_of(matmul(heads_out, mixer_set[6]))
    middle = x_own + live_own * mix_own
    mlp_set = gather_mlp(w_mlp_gate, w_mlp_up, w_mlp_down)
    scale_two = lax.rsqrt(jnp.mean(middle * middle, axis=1, keepdims=True) + EPS_ROW)
    second_in = (middle * scale_two * norm_gains[1]).astype(jnp.bfloat16)
    second_rows = group_of(second_in)
    gate_pre = matmul(second_rows, mlp_set[0])
    up_proj = matmul(second_rows, mlp_set[1])
    hidden = (jax.nn.silu(gate_pre) * up_proj).astype(jnp.bfloat16)
    branch_own = own_of(matmul(hidden, mlp_set[2]))
    result_own = (middle + live_own * branch_own).astype(jnp.bfloat16)
    branch_cot = (live_own * dy_own).astype(jnp.bfloat16)
    branch_rows = group_of(branch_cot)
    mlp_back = gather_mlp(w_mlp_gate, w_mlp_up, w_mlp_down)
    grad_hidden = times_back(branch_rows, mlp_back[2])
    sigmoid_gate = jax.nn.sigmoid(gate_pre)
    grad_gate = (
        grad_hidden * up_proj * sigmoid_gate * (1.0 + gate_pre * (1.0 - sigmoid_gate))
    ).astype(jnp.bfloat16)
    grad_up = (grad_hidden * gate_pre * sigmoid_gate).astype(jnp.bfloat16)
    mlp_grads = (
        lax.psum_scatter(outer_sum(second_rows, grad_gate), "dp", scatter_dimension=0, tiled=True),
        lax.psum_scatter(outer_sum(second_rows, grad_up), "dp", scatter_dimension=0, tiled=True),
        lax.psum_scatter(outer_sum(hidden, branch_rows), "dp", scatter_dimension=1, tiled=True),
    )
    grad_second = own_of(times_back(grad_gate, mlp_back[0]) + times_back(grad_up, mlp_back[1]))
    grad_mid_norm, gain_two_grad = norm_back(middle, scale_two, norm_gains[1], grad_second)
    grad_middle = dy_own + grad_mid_norm
    mix_cot = (live_own * grad_middle).astype(jnp.bfloat16)
    mix_rows = group_of(mix_cot)
    mixer_back = gather_mixer(w_query, w_key, w_value, w_gate, w_decay, w_beta, w_out)
    grad_heads = times_back(mix_rows, mixer_back[6])
    core_grads = core_pull(grad_heads)
    conv_grads = conv_pull((core_grads[0], core_grads[1], core_grads[2]))
    proj_grads = (
        conv_grads[0],
        conv_grads[1],
        conv_grads[2],
        core_grads[5],
        core_grads[3],
        core_grads[4],
    )
    proj_grads = tuple((member.astype(jnp.bfloat16) for member in proj_grads))
    grad_first = times_back(proj_grads[0], mixer_back[0])
    for number in range(1, 6):
        grad_first = grad_first + times_back(proj_grads[number], mixer_back[number])
    grad_first = own_of(grad_first)
    grad_x_norm, gain_one_grad = norm_back(x_own, scale_one, norm_gains[0], grad_first)
    grad_tokens = (grad_middle + grad_x_norm).astype(jnp.bfloat16)
    weight_grads = tuple((outer_sum(first_rows, member) for member in proj_grads))
    mixer_grads = (
        lax.psum_scatter(weight_grads[0], "dp", scatter_dimension=0, tiled=True),
        lax.psum_scatter(weight_grads[1], "dp", scatter_dimension=0, tiled=True),
        lax.psum_scatter(weight_grads[2], "dp", scatter_dimension=0, tiled=True),
        lax.psum_scatter(weight_grads[3], "dp", scatter_dimension=0, tiled=True),
        lax.psum_scatter(weight_grads[4], "dp", scatter_dimension=0, tiled=True),
        lax.psum_scatter(weight_grads[5], "dp", scatter_dimension=0, tiled=True),
        lax.psum_scatter(outer_sum(heads_out, mix_rows), "dp", scatter_dimension=1, tiled=True),
    )
    taps_grad = conv_grads[3]
    conv_full = jnp.zeros(conv_weights.shape, jnp.float32)
    conv_full = lax.dynamic_update_slice_in_dim(
        conv_full, taps_grad[:, :keys_here], tensor_rank * keys_here, 1
    )
    conv_full = lax.dynamic_update_slice_in_dim(
        conv_full, taps_grad[:, keys_here : 2 * keys_here], all_keys + tensor_rank * keys_here, 1
    )
    conv_full = lax.dynamic_update_slice_in_dim(
        conv_full, taps_grad[:, 2 * keys_here :], 2 * all_keys + tensor_rank * vals_here, 1
    )
    log_full = lax.dynamic_update_slice_in_dim(
        jnp.zeros((HEADS,), jnp.float32), core_grads[6], tensor_rank * heads_here, 0
    )
    bias_full = lax.dynamic_update_slice_in_dim(
        jnp.zeros((HEADS,), jnp.float32), core_grads[7], tensor_rank * heads_here, 0
    )
    gains_full = jnp.stack([gain_one_grad, gain_two_grad])
    small_sums = lax.psum(
        (gains_full, conv_full, log_full, bias_full, core_grads[8]), ("dp", "tensor")
    )
    picked = jnp.where(got_slot < 0, 0, got_slot)
    back_out, back_grad = route_out(result_own[picked], grad_tokens[picked])
    output = back_out[outgoing]
    tokens_grad = back_grad[outgoing]
    return (
        output,
        tokens_grad,
        small_sums[0],
        mixer_grads[0],
        mixer_grads[1],
        mixer_grads[2],
        mixer_grads[3],
        mixer_grads[4],
        mixer_grads[5],
        small_sums[1],
        small_sums[2],
        small_sums[3],
        small_sums[4],
        mixer_grads[6],
        mlp_grads[0],
        mlp_grads[1],
        mlp_grads[2],
    )


def solution(mesh):
    return jax.shard_map(
        shards,
        mesh=mesh,
        in_specs=(
            P(("dp", "tensor"), None),
            P(("dp", "tensor"), None),
            P("dp", None),
            P(("dp", "tensor")),
            P(),
            P("dp", "tensor"),
            P("dp", "tensor"),
            P("dp", "tensor"),
            P("dp", "tensor"),
            P("dp", "tensor"),
            P("dp", "tensor"),
            P(),
            P(),
            P(),
            P(),
            P("tensor", "dp"),
            P("dp", "tensor"),
            P("dp", "tensor"),
            P("tensor", "dp"),
        ),
        out_specs=(
            P(("dp", "tensor"), None),
            P(("dp", "tensor"), None),
            P(),
            P("dp", "tensor"),
            P("dp", "tensor"),
            P("dp", "tensor"),
            P("dp", "tensor"),
            P("dp", "tensor"),
            P("dp", "tensor"),
            P(),
            P(),
            P(),
            P(),
            P("tensor", "dp"),
            P("dp", "tensor"),
            P("dp", "tensor"),
            P("tensor", "dp"),
        ),
        check_vma=False,
    )
```

profile of v0, /device:TPU:0, one launch (start us, length us, event | category | flops | bytes accessed | tf_op | source)
XLA Modules:
  0.0 5657.0 jit_solution(17267983549170181748)
XLA Ops:
  31.5 46.3 all-to-all-done.1
  88.2 39.4 all_gather.53
  179.9 71.1 %all-gather.17.cloned.1.call-done = bf16[2048,1024]{1,0:T(8,128)(2,1)} async-done(((bf16[128,1024]{1,0:T(8,128)(2,1)}), bf16[2048,1024]{1,0:T(8,128)(2,1)}) %all-gather.17.cloned.1.call-update) | async-done | bytes 4194320 | tf_op jit(solution)/shard_map/all_gather | solution.py:151
  257.5 107.6 %all-gather.19.cloned.1.call-done = bf16[2048,2048]{1,0:T(8,128)(2,1)} async-done(((bf16[128,2048]{1,0:T(8,128)(2,1)}), bf16[2048,2048]{1,0:T(8,128)(2,1)}) %all-gather.19.cloned.1.call-update) | async-done | bytes 8388624 | tf_op jit(solution)/shard_map/all_gather | solution.py:152
  423.6 612.4 %while.96 = (s32[]{:T(128)}, f32[8,256,128]{2,1,0:T(8,128)S(1)}, f32[8,64,8,256]{3,1,2,0:T(8,128)}, pred[8,8,64,64]{3,2,1,0:T(32,128)(4,1)}, f32[8,8,64,64]{3,2,...) while((s32[]{:T(128)}, f32[8,256,128]{2,1,0:T(8,128)S(1)}, ...), condition=%wide.region_16.17_spmd.clone, body=%wide.region_13.16_spmd.clone.sunk | while | flops 959648832 | bytes 23773008 | solution.py:128
  432.9 39.3 custom-call.64
  509.3 39.3 custom-call.64
  585.9 39.3 custom-call.64
  1083.8 69.4 %all-to-all-done.3 = bf16[32,10,2048]{2,1,0:T(8,128)(2,1)S(1)} async-done(((bf16[32,10,2048]{2,1,0:T(8,128)(2,1)}), bf16[32,10,2048]{2,1,0:T(8,128)(2,1)S(1)}, u32[]{:S(2)}, u32[]{:S(2)}) %all-to-all-start.3) | async-done | bytes 1310752 | tf_op jit(solution)/shard_map/all_to_all | solution.py:171
  1164.2 87.2 %all-gather.27.cloned.1.call-done = bf16[2048,2816]{1,0:T(8,128)(2,1)} async-done(((bf16[128,2816]{1,0:T(8,128)(2,1)}), bf16[2048,2816]{1,0:T(8,128)(2,1)}) %all-gather.27.cloned.1.call-update) | async-done | bytes 11534352 | tf_op jit(solution)/shard_map/all_gather | solution.py:162
  1275.1 133.6 %all-gather.29.cloned.1.call-done = bf16[2048,2816]{1,0:T(8,128)(2,1)} async-done(((bf16[128,2816]{1,0:T(8,128)(2,1)}), bf16[2048,2816]{1,0:T(8,128)(2,1)}) %all-gather.29.cloned.1.call-update) | async-done | bytes 11534352 | tf_op jit(solution)/shard_map/all_gather | solution.py:163
  1421.2 171.4 %all-gather.31.cloned.1.call-done = bf16[2816,2048]{1,0:T(8,128)(2,1)} async-done(((bf16[2816,128]{1,0:T(8,128)(2,1)}), bf16[2816,2048]{1,0:T(8,128)(2,1)}) %all-gather.31.cloned.1.call-update) | async-done | bytes 11534352 | tf_op jit(solution)/shard_map/all_gather | solution.py:164
  1699.1 659.8 %while.97 = (s32[]{:T(128)}, f32[8,256,128]{2,1,0:T(8,128)S(1)}, f32[8,64,8,128]{3,2,1,0:T(8,128)}, f32[8,64,8,128]{3,2,1,0:T(8,128)}, f32[8,64,8,256]{3,2,1,0:T...) while((s32[]{:T(128)}, f32[8,256,128]{2,1,0:T(8,128)S(1)}, ...), condition=%wide.region_35.36_spmd.clone, body=%wide.region_26.35_spmd.clone.sunk | while | flops 1943352832 | bytes 34715300 | solution.py:128
  1712.9 39.3 custom-call.65
  1795.3 39.3 custom-call.65
  1877.6 39.3 custom-call.65
  1960.0 39.3 custom-call.65
  2042.4 39.3 custom-call.65
  2124.8 39.3 custom-call.65
  2207.2 39.3 custom-call.65
  2289.6 39.3 custom-call.65
  2588.9 45.5 all-to-all-done.4
  2638.9 70.0 %all-reduce.20 = (f32[2,2048]{1,0:T(2,128)}, f32[16]{0:T(128)}, f32[16]{0:T(128)}, f32[256]{0:T(256)}) all-reduce(f32[2,2048]{1,0:T(2,128)S(1)} %pad_maximum_fusion.2, f32[16]{0:T(128)S(1)} %multiply_dynamic-update-slice_fusion, f32[16]{0:T(128)S(1)} %dynamic_update_slice.303, ...), channel_id=1, replica_groups=mesh['dp'=16,'tensor'=2] {'dp','tensor'}, use_global_device_ids=true, to_apply=%region_42.43 | all-reduce | flops 4384 | bytes 35072 | tf_op jit(solution)/shard_map/psum | solution.py:379
  2716.5 63.8 %reduce-scatter.31.cloned.1.call-done = f32[128,8]{0,1:T(8,128)} async-done(((f32[2048,8]{0,1:T(8,128)}), f32[128,8]{0,1:T(8,128)}) %reduce-scatter.31.cloned.1.call-update) | async-done | bytes 4112 | tf_op jit(solution)/shard_map/reduce_scatter | solution.py:357
  2780.3 176.9 %reduce-scatter.23.cloned.1.call-done = f32[128,1024]{1,0:T(8,128)} async-done(((f32[2048,1024]{1,0:T(8,128)}), f32[128,1024]{1,0:T(8,128)}) %reduce-scatter.23.cloned.1.call-update) | async-done | bytes 524304 | tf_op jit(solution)/shard_map/reduce_scatter | solution.py:353
  2957.2 183.2 %reduce-scatter.25.cloned.1.call-done = f32[128,1024]{1,0:T(8,128)} async-done(((f32[2048,1024]{1,0:T(8,128)}), f32[128,1024]{1,0:T(8,128)}) %reduce-scatter.25.cloned.1.call-update) | async-done | bytes 524304 | tf_op jit(solution)/shard_map/reduce_scatter | solution.py:354
  3140.4 351.7 %reduce-scatter.35.cloned.1.call-done = f32[2048,128]{1,0:T(8,128)} async-done(((f32[2048,2048]{1,0:T(8,128)}), f32[2048,128]{1,0:T(8,128)}) %reduce-scatter.35.cloned.1.call-update) | async-done | bytes 1048592 | tf_op jit(solution)/shard_map/reduce_scatter | solution.py:359
  3492.0 354.9 %reduce-scatter.27.cloned.1.call-done = f32[128,2048]{1,0:T(8,128)} async-done(((f32[2048,2048]{1,0:T(8,128)}), f32[128,2048]{1,0:T(8,128)}) %reduce-scatter.27.cloned.1.call-update) | async-done | bytes 1048592 | tf_op jit(solution)/shard_map/reduce_scatter | solution.py:355
  3846.9 354.8 %reduce-scatter.29.cloned.1.call-done = f32[128,2048]{1,0:T(8,128)} async-done(((f32[2048,2048]{1,0:T(8,128)}), f32[128,2048]{1,0:T(8,128)}) %reduce-scatter.29.cloned.1.call-update) | async-done | bytes 1048592 | tf_op jit(solution)/shard_map/reduce_scatter | solution.py:356
  4201.7 481.5 %reduce-scatter.39.cloned.1.call-done = f32[128,2816]{1,0:T(8,128)} async-done(((f32[2048,2816]{1,0:T(8,128)}), f32[128,2816]{1,0:T(8,128)}) %reduce-scatter.39.cloned.1.call-update) | async-done | bytes 1441808 | tf_op jit(solution)/shard_map/reduce_scatter | solution.py:324
  4683.2 482.6 %reduce-scatter.41.cloned.1.call-done = f32[2816,128]{1,0:T(8,128)} async-done(((f32[2816,2048]{1,0:T(8,128)}), f32[2816,128]{1,0:T(8,128)}) %reduce-scatter.41.cloned.1.call-update) | async-done | bytes 1441808 | tf_op jit(solution)/shard_map/reduce_scatter | solution.py:325
  5165.8 482.6 %reduce-scatter.37.cloned.1.call-done = f32[128,2816]{1,0:T(8,128)} async-done(((f32[2048,2816]{1,0:T(8,128)}), f32[128,2816]{1,0:T(8,128)}) %reduce-scatter.37.cloned.1.call-update) | async-done | bytes 1441808 | tf_op jit(solution)/shard_map/reduce_scatter | solution.py:323
  (1210 shorter events, 1431.7 us)
Async XLA Ops:
  10.9 14.4 all-to-all-start
  25.3 52.5 all-to-all-start.1
  28.9 137.4 %all-gather.13.cloned.1.call-start = ((), (), s32[]{:S(2)}) async-start(), calls=%async_computation.19 | async-start | bytes 3145728 | tf_op jit(solution)/shard_map/all_gather | solution.py:139
  83.3 90.1 %all-gather.15.cloned.1.call-start = ((), (), s32[]{:S(2)}) async-start(), calls=%async_computation.20 | async-start | bytes 4456448 | tf_op jit(solution)/shard_map/all_gather | solution.py:150
  84.0 167.0 %all-gather.17.cloned.1.call-start = ((), (), s32[]{:S(2)}) async-start(), calls=%async_computation.21 | async-start | bytes 4456448 | tf_op jit(solution)/shard_map/all_gather | solution.py:151
  84.8 280.3 %all-gather.19.cloned.1.call-start = ((), (), s32[]{:S(2)}) async-start(), calls=%async_computation.22 | async-start | bytes 8912896 | tf_op jit(solution)/shard_map/all_gather | solution.py:152
  85.4 966.8 %all-gather.21.cloned.1.call-start = ((), (), s32[]{:S(2)}) async-start(), calls=%async_computation.23 | async-start | bytes 8912896 | tf_op jit(solution)/shard_map/all_gather | solution.py:153
  86.0 978.1 %all-gather.23.cloned.1.call-start = ((), (), s32[]{:S(2)}) async-start(), calls=%async_computation.24 | async-start | bytes 8912896 | tf_op jit(solution)/shard_map/all_gather | solution.py:156
  86.5 1071.6 %reduce-scatter.15.cloned.1.call-start = ((), (), s32[]{:S(2)}) async-start(), calls=%async_computation.25 | async-start | bytes 3145728 | tf_op jit(solution)/shard_map/reduce_scatter | solution.py:143
  1074.0 177.4 %all-gather.27.cloned.1.call-start = ((), (), s32[]{:S(2)}) async-start(), calls=%async_computation.27 | async-start | bytes 12255232 | tf_op jit(solution)/shard_map/all_gather | solution.py:162
  1079.5 73.7 %all-to-all-start.3 = ((bf16[32,10,2048]{2,1,0:T(8,128)(2,1)}), bf16[32,10,2048]{2,1,0:T(8,128)(2,1)S(1)}, u32[]{:S(2)}, u32[]{:S(2)}) async-start(bf16[32,10,2048]{2,1,0:T(8,128)(2,1)} %all_to_all.49), calls=%async_computation.5 | async-start | bytes 4194304 | tf_op jit(solution)/shard_map/all_to_all | solution.py:171
  1082.4 180.0 %all-gather.25.cloned.1.call-start = ((), (), s32[]{:S(2)}) async-start(), calls=%async_computation.26 | async-start | bytes 3145728 | tf_op jit(solution)/shard_map/all_gather | solution.py:139
  1162.2 246.5 %all-gather.29.cloned.1.call-start = ((), (), s32[]{:S(2)}) async-start(), calls=%async_computation.28 | async-start | bytes 12255232 | tf_op jit(solution)/shard_map/all_gather | solution.py:163
  1162.8 429.8 %all-gather.31.cloned.1.call-start = ((), (), s32[]{:S(2)}) async-start(), calls=%async_computation.29 | async-start | bytes 12255232 | tf_op jit(solution)/shard_map/all_gather | solution.py:164
  1163.5 439.9 %all-gather.33.cloned.1.call-start = ((), (), s32[]{:S(2)}) async-start(), calls=%async_computation.31 | async-start | bytes 3145728 | tf_op jit(solution)/shard_map/all_gather | solution.py:139
  1164.1 486.7 %reduce-scatter.19.cloned.1.call-start = ((), (), s32[]{:S(2)}) async-start(), calls=%async_computation.32 | async-start | bytes 3145728 | tf_op jit(solution)/shard_map/reduce_scatter | solution.py:143
  1639.9 28.3 all-gather.35.cloned.1.call-start
  1656.3 909.9 %reduce-scatter.21.cloned.1.call-start = ((), (), s32[]{:S(2)}) async-start(), calls=%async_computation.34 | async-start | bytes 3145728 | tf_op jit(solution)/shard_map/reduce_scatter | solution.py:143
  2463.0 105.7 %reduce-scatter.17.cloned.1.call-start = ((), (), s32[]{:S(2)}) async-start(), calls=%async_computation.30 | async-start | bytes 3145728 | tf_op jit(solution)/shard_map/reduce_scatter | solution.py:143
  2473.9 242.6 %all-reduce.23.cloned.1.call-start = ((), (), s32[]{:S(2)}) async-start(), calls=%async_computation.41 | async-start | bytes 262144 | tf_op jit(solution)/shard_map/psum | solution.py:379
  2474.8 241.7 %reduce-scatter.33.cloned.1.call-start = ((), (), s32[]{:S(2)}) async-start(), calls=%async_computation.40 | async-start | bytes 69632 | tf_op jit(solution)/shard_map/reduce_scatter | solution.py:358
  2476.6 303.7 %reduce-scatter.31.cloned.1.call-start = ((), (), s32[]{:S(2)}) async-start(), calls=%async_computation.39 | async-start | bytes 69632 | tf_op jit(solution)/shard_map/reduce_scatter | solution.py:357
  2477.6 479.5 %reduce-scatter.23.cloned.1.call-start = ((), (), s32[]{:S(2)}) async-start(), calls=%async_computation.35 | async-start | bytes 8912896 | tf_op jit(solution)/shard_map/reduce_scatter | solution.py:353
  2484.8 655.5 %reduce-scatter.25.cloned.1.call-start = ((), (), s32[]{:S(2)}) async-start(), calls=%async_computation.36 | async-start | bytes 8912896 | tf_op jit(solution)/shard_map/reduce_scatter | solution.py:354
  2491.8 1000.2 %reduce-scatter.35.cloned.1.call-start = ((), (), s32[]{:S(2)}) async-start(), calls=%async_computation.42 | async-start | bytes 17825792 | tf_op jit(solution)/shard_map/reduce_scatter | solution.py:359
  2505.0 1341.9 %reduce-scatter.27.cloned.1.call-start = ((), (), s32[]{:S(2)}) async-start(), calls=%async_computation.37 | async-start | bytes 17825792 | tf_op jit(solution)/shard_map/reduce_scatter | solution.py:355
  2514.9 1686.7 %reduce-scatter.29.cloned.1.call-start = ((), (), s32[]{:S(2)}) async-start(), calls=%async_computation.38 | async-start | bytes 17825792 | tf_op jit(solution)/shard_map/reduce_scatter | solution.py:356
  2524.9 2158.3 %reduce-scatter.39.cloned.1.call-start = ((), (), s32[]{:S(2)}) async-start(), calls=%async_computation.44 | async-start | bytes 24510464 | tf_op jit(solution)/shard_map/reduce_scatter | solution.py:324
  2539.2 2626.5 %reduce-scatter.41.cloned.1.call-start = ((), (), s32[]{:S(2)}) async-start(), calls=%async_computation.45 | async-start | bytes 24510464 | tf_op jit(solution)/shard_map/reduce_scatter | solution.py:325
  2552.8 3095.5 %reduce-scatter.37.cloned.1.call-start = ((), (), s32[]{:S(2)}) async-start(), calls=%async_computation.43 | async-start | bytes 24510464 | tf_op jit(solution)/shard_map/reduce_scatter | solution.py:323
  2578.9 55.4 all-to-all-start.4
  2634.3 79.3 %all-to-all-start.2 = ((bf16[32,10,2048]{2,1,0:T(8,128)(2,1)}), bf16[32,10,2048]{2,1,0:T(8,128)(2,1)S(1)}, u32[]{:S(2)}, u32[]{:S(2)}) async-start(bf16[32,10,2048]{2,1,0:T(8,128)(2,1)} %all_to_all.46), calls=%async_computation.4 | async-start | bytes 4194304 | tf_op jit(solution)/shard_map/all_to_all | solution.py:179
  (125 other events, 6951.3 us)
Sparse Core Ops, SparseCore 0:
  83.4 9.9 all-gather.12
  96.2 77.1 all-gather.14
  176.2 74.7 all-gather.16
  253.6 111.4 all-gather.18
  367.7 111.0 all-gather.20
  481.4 141.9 all-gather.22
  1074.1 7.8 reduce-scatter.14
  1085.2 166.1 all-gather.26
  1253.6 8.7 all-gather.24
  1265.4 143.3 all-gather.28
  1411.8 180.7 all-gather.30
  1594.6 8.7 all-gather.32
  1640.0 10.7 reduce-scatter.18
  1656.4 11.7 all-gather.34
  2463.1 10.7 reduce-scatter.20
  2476.1 10.7 reduce-scatter.16
  2492.9 130.2 all-reduce.22
  2625.9 76.0 reduce-scatter.32
  2704.9 75.3 reduce-scatter.30
  2783.0 174.1 reduce-scatter.22
  2960.1 180.2 reduce-scatter.24
  3143.2 348.7 reduce-scatter.34
  3494.9 351.9 reduce-scatter.26
  3849.7 351.9 reduce-scatter.28
  4204.6 478.5 reduce-scatter.38
  4685.9 479.7 reduce-scatter.40
  5168.5 479.7 reduce-scatter.36
where the time goes:
time: 5680 us; the launch traced here: 5660 us
  waiting for transfers between devices  3710 us (65%)
  other arithmetic  853 us (15%)
  matrix products  641 us (11%)
  local copies, waits for them, and re-layouts  261 us (5%)
  blocking collectives  146 us (3%)
    another operation x72, other arithmetic, block_rule(): jax.scipy.linalg.solve_triangular(system, right_side, lower=True, unit_di...  638 us
    reduce_scatter x1, waiting for transfers between devices, shards(): lax.psum_scatter(outer_sum(hidden, branch_rows), 'dp', scatter_dimension=...  483 us
    reduce_scatter x1, waiting for transfers between devices, shards(): lax.psum_scatter(outer_sum(second_rows, grad_gate), 'dp', scatter_dimensi...  483 us
    reduce_scatter x1, waiting for transfers between devices, shards(): lax.psum_scatter(outer_sum(second_rows, grad_up), 'dp', scatter_dimension...  482 us
    reduce_scatter x1, waiting for transfers between devices, shards(): lax.psum_scatter(weight_grads[2], 'dp', scatter_dimension=0, tiled=True)  355 us
    reduce_scatter x1, waiting for transfers between devices, shards(): lax.psum_scatter(weight_grads[3], 'dp', scatter_dimension=0, tiled=True)  355 us
    reduce_scatter x1, waiting for transfers between devices, shards(): lax.psum_scatter(outer_sum(heads_out, mix_rows), 'dp', scatter_dimension=...  352 us
    reduce_scatter x1, waiting for transfers between devices, shards(): lax.psum_scatter(weight_grads[1], 'dp', scatter_dimension=0, tiled=True)  183 us
  transfers between devices with their start and end apart: 32, of which 23 were waited for; matrix products, arithmetic and copies ran while one was open for 16% of the time, Pallas kernels for 0%

commit v1 on v0

v1 whole, which is shorter than its diff:
```python
import functools

import jax
import jax.numpy as jnp
from jax import lax
from jax.experimental import pallas as pl
from jax.experimental.pallas import tpu as pltpu
from jax.sharding import PartitionSpec as P

bf = jnp.bfloat16
f32 = jnp.float32
DK = 128
DV = 256
CHUNK = 128
LANES = 128
EPS_ROW = 1e-06
EPS_UNIT = 1e-06
EPS_HEAD = 1e-05
NEG = -1e30


def nn(left, right):
    return lax.dot_general(left.astype(bf), right.astype(bf), (((1,), (0,)), ((), ())), preferred_element_type=f32)


def nt(left, right):
    return lax.dot_general(left.astype(bf), right.astype(bf), (((1,), (1,)), ((), ())), preferred_element_type=f32)


def tn(left, right):
    return lax.dot_general(left.astype(bf), right.astype(bf), (((0,), (0,)), ((), ())), preferred_element_type=f32)


def exact(left, right):
    return lax.dot_general(left, right, (((1,), (0,)), ((), ())), precision=lax.Precision.HIGHEST, preferred_element_type=f32)


def softplus(v):
    return jnp.maximum(v, 0.0) + jnp.log(1.0 + jnp.exp(-jnp.abs(v)))


def sigmoid(v):
    return 1.0 / (1.0 + jnp.exp(-v))


def unit_lower_inverses(systems, places, others):
    eye = (places == others).astype(f32)
    size = 16
    same = (places // size) == (others // size)
    power = [jnp.where(same, a, 0.0) for a in systems]
    inverse = [eye - a for a in power]
    span = 2
    while span < size:
        power = [nn(a, a) for a in power]
        inverse = [t + nn(t, a) for t, a in zip(inverse, power)]
        span *= 2
    while size < places.shape[0]:
        corner = ((places // (2 * size)) == (others // (2 * size))) & ((places // size) != (others // size))
        steps = [nn(jnp.where(corner, a, 0.0), t) for a, t in zip(systems, inverse)]
        inverse = [t - nn(t, s) for t, s in zip(inverse, steps)]
        size *= 2
    return inverse


def conv_channels(padded, taps, marks, columns):
    total = taps[0:1, columns] * padded[8 : 8 + CHUNK, columns]
    for offset in range(1, 4):
        total = total + (taps[offset : offset + 1, columns] * marks[:, offset : offset + 1]) * padded[8 - offset : 8 - offset + CHUNK, columns]
    return total


def decay_terms(decays, head_params):
    biased = decays + head_params[0:1, :]
    log_decay = -head_params[1:2, :] * softplus(biased)
    return biased, log_decay


def chunk_terms(heads, decays, head_params, marks, seg_row, places, others):
    biased, log_decay = decay_terms(decays, head_params)
    lower = (places >= others).astype(f32)
    cum = exact(lower, log_decay)
    cum_rows = cum.T
    beta = sigmoid(decays)
    seg = marks[:, 0:1]
    causal = (places >= others) & (seg == seg_row)
    opening = marks[:, 4:5] > 0.0
    closing = marks[:, 5:6] > 0.0
    terms = []
    for head in range(heads):
        col = cum[:, head : head + 1]
        row = cum_rows[head : head + 1, :]
        decay = jnp.exp(jnp.where(causal, col - row, NEG))
        opened = jnp.exp(jnp.where(opening, col, NEG))
        last = cum[CHUNK - 1 : CHUNK, head : head + 1]
        closed = jnp.exp(jnp.where(closing, last - col, NEG))
        opened_last = opened[CHUNK - 1 : CHUNK, :]
        terms.append((decay, opened, closed, opened_last, beta[:, heads + head : heads + head + 1]))
    return biased, log_decay, beta, terms


def forward_kernel(heads, proj, marks_ref, seg_ref, taps, params, gain, out, kept_state, kept_inverse, state, padded):
    keys = heads * DK
    vals = heads * DV
    conv_width = 2 * keys + vals

    @pl.when(pl.program_id(1) == 0)
    def _():
        state[...] = jnp.zeros_like(state)
        padded[0:8, :] = jnp.zeros((8, conv_width), f32)

    padded[8:, :] = proj[:, :conv_width].astype(f32)
    marks = marks_ref[...]
    places = lax.broadcasted_iota(jnp.int32, (CHUNK, CHUNK), 0)
    others = lax.broadcasted_iota(jnp.int32, (CHUNK, CHUNK), 1)
    decays = proj[:, conv_width + vals :].astype(f32)
    _, _, _, terms = chunk_terms(heads, decays, params[...], marks, seg_ref[0], places, others)
    strict = places > others
    queries, key_vecs, values = [], [], []
    for head in range(heads):
        summed = conv_channels(padded, taps, marks, slice(head * DK, head * DK + DK))
        act = summed * sigmoid(summed)
        queries.append((act * (lax.rsqrt(jnp.sum(act * act, axis=1, keepdims=True) + EPS_UNIT) * DK**-0.5)).astype(bf))
        summed = conv_channels(padded, taps, marks, slice(keys + head * DK, keys + head * DK + DK))
        act = summed * sigmoid(summed)
        key_vecs.append((act * lax.rsqrt(jnp.sum(act * act, axis=1, keepdims=True) + EPS_UNIT)).astype(bf))
    dots = [nt(jnp.concatenate([q, k], axis=0), k) for q, k in zip(queries, key_vecs)]
    systems = [jnp.where(strict, term[4] * term[0] * dot[CHUNK:], 0.0) for term, dot in zip(terms, dots)]
    inverses = unit_lower_inverses(systems, places, others)
    for head in range(heads):
        summed = conv_channels(padded, taps, marks, slice(2 * keys + head * DV, 2 * keys + head * DV + DV))
        values.append((summed * sigmoid(summed)).astype(bf).astype(f32))
    padded[0:8, :] = padded[CHUNK : CHUNK + 8, :]
    before = [state[head] for head in range(heads)]
    for head in range(heads):
        kept_state[0, head] = before[head].astype(bf)
        kept_inverse[:, head * CHUNK : head * CHUNK + CHUNK] = inverses[head].astype(bf)
    reads = [nn(jnp.concatenate([k, q], axis=0), s) for k, q, s in zip(key_vecs, queries, before)]
    rights = [term[4] * (v - term[1] * read[:CHUNK]) for term, v, read in zip(terms, values, reads)]
    news = [nn(t, r) for t, r in zip(inverses, rights)]
    mixed = [
        term[1] * read[CHUNK:] + nn(dot[:CHUNK] * term[0], new)
        for term, read, dot, new in zip(terms, reads, dots, news)
    ]
    for head in range(heads):
        term = terms[head]
        state[head] = term[3] * before[head] + tn(key_vecs[head], term[2] * news[head])
    for head in range(heads):
        gate = proj[:, conv_width + head * DV : conv_width + head * DV + DV].astype(f32)
        mix = mixed[head]
        scale = lax.rsqrt(jnp.mean(mix * mix, axis=1, keepdims=True) + EPS_HEAD)
        out[:, head * DV : head * DV + DV] = (mix * scale * gain[...] * (gate * sigmoid(gate))).astype(bf)


def backward_kernel(heads, proj, prev_rows, grads, marks_ref, seg_ref, taps, params, gain, kept_state, kept_inverse,
                    proj_grad, taps_grad, params_grad, gain_grad, state_grad, padded, summed_grad):
    keys = heads * DK
    vals = heads * DV
    conv_width = 2 * keys + vals
    step = pl.program_id(1)

    @pl.when((pl.program_id(0) == 0) & (step == 0))
    def _():
        taps_grad[...] = jnp.zeros_like(taps_grad)
        params_grad[...] = jnp.zeros_like(params_grad)
        gain_grad[...] = jnp.zeros_like(gain_grad)

    @pl.when(step == 0)
    def _():
        state_grad[...] = jnp.zeros_like(state_grad)
        summed_grad[CHUNK:, :] = jnp.zeros((8, conv_width), f32)

    marks = marks_ref[...]
    padded[0:8, :] = prev_rows[...].astype(f32)[-8:, :conv_width]
    padded[8:, :] = proj[:, :conv_width].astype(f32)
    places = lax.broadcasted_iota(jnp.int32, (CHUNK, CHUNK), 0)
    others = lax.broadcasted_iota(jnp.int32, (CHUNK, CHUNK), 1)
    decays = proj[:, conv_width + vals :].astype(f32)
    biased, log_decay, beta, terms = chunk_terms(heads, decays, params[...], marks, seg_ref[0], places, others)
    strict = places > others
    q_sums, k_sums, v_sums = [], [], []
    q_acts, k_acts, q_scale, k_scale = [], [], [], []
    queries, key_vecs, values = [], [], []
    for head in range(heads):
        summed = conv_channels(padded, taps, marks, slice(head * DK, head * DK + DK))
        act = summed * sigmoid(summed)
        scale = lax.rsqrt(jnp.sum(act * act, axis=1, keepdims=True) + EPS_UNIT)
        queries.append((act * (scale * DK**-0.5)).astype(bf))
        q_sums.append(summed)
        q_acts.append(act)
        q_scale.append(scale)
        summed = conv_channels(padded, taps, marks, slice(keys + head * DK, keys + head * DK + DK))
        act = summed * sigmoid(summed)
        scale = lax.rsqrt(jnp.sum(act * act, axis=1, keepdims=True) + EPS_UNIT)
        key_vecs.append((act * scale).astype(bf))
        k_sums.append(summed)
        k_acts.append(act)
        k_scale.append(scale)
        summed = conv_channels(padded, taps, marks, slice(2 * keys + head * DV, 2 * keys + head * DV + DV))
        values.append((summed * sigmoid(summed)).astype(bf).astype(f32))
        v_sums.append(summed)
    pairs = [jnp.concatenate([q, k], axis=0) for q, k in zip(queries, key_vecs)]
    dots = [nt(pair, k) for pair, k in zip(pairs, key_vecs)]
    before = [kept_state[0, head] for head in range(heads)]
    after_grad = [state_grad[head] for head in range(heads)]
    inverses = [kept_inverse[:, head * CHUNK : head * CHUNK + CHUNK] for head in range(heads)]
    reads = [nn(pair, s) for pair, s in zip(pairs, before)]
    gaps = [v - term[1] * read[CHUNK:] for term, v, read in zip(terms, values, reads)]
    news = [nn(t, term[4] * g) for t, term, g in zip(inverses, terms, gaps)]
    scores = [(dot[:CHUNK] * term[0]) for dot, term in zip(dots, terms)]
    mixed = [term[1] * read[:CHUNK] + nn(score, new) for term, read, score, new in zip(terms, reads, scores, news)]
    mix_grads = []
    gain_row = gain[...]
    for head in range(heads):
        columns = slice(head * DV, head * DV + DV)
        gate_columns = slice(conv_width + head * DV, conv_width + head * DV + DV)
        gate = proj[:, gate_columns].astype(f32)
        grad = grads[:, columns].astype(f32)
        mix = mixed[head]
        scale = lax.rsqrt(jnp.mean(mix * mix, axis=1, keepdims=True) + EPS_HEAD)
        soft = sigmoid(gate)
        normed = mix * scale
        grad_normed = grad * normed
        proj_grad[:, gate_columns] = (grad_normed * gain_row * (soft * (1.0 + gate * (1.0 - soft)))).astype(bf)
        silu = gate * soft
        gain_grad[0:1, :] += jnp.sum(grad_normed * silu, axis=0, keepdims=True)
        inner = grad * silu * gain_row
        mix_grads.append(scale * inner - mix * (scale * scale * scale) * jnp.mean(inner * mix, axis=1, keepdims=True))
    pushes = [nn(k, g) for k, g in zip(key_vecs, after_grad)]
    new_grads = [tn(score, grad) + term[2] * push for score, grad, term, push in zip(scores, mix_grads, terms, pushes)]
    score_grads = [nt(grad, new) for grad, new in zip(mix_grads, news)]
    right_grads = [tn(t, grad) for t, grad in zip(inverses, new_grads)]
    system_grads = [jnp.where(strict, -nt(grad, new), 0.0) for grad, new in zip(right_grads, news)]
    cum_grad = jnp.zeros((CHUNK, LANES), f32)
    beta_grads = jnp.zeros((CHUNK, LANES), f32)
    cross_rows = []
    lanes = lax.broadcasted_iota(jnp.int32, (CHUNK, LANES), 1)
    rows_down = lax.broadcasted_iota(jnp.int32, (CHUNK, 1), 0)
    raised = []
    for head in range(heads):
        decay, opened, closed, opened_last, strength = terms[head]
        read_key = reads[head][CHUNK:]
        read_query = reads[head][:CHUNK]
        gram = dots[head][CHUNK:]
        decayed_score_grad = score_grads[head] * decay
        decayed_system = system_grads[head] * decay
        system_gram = decayed_system * gram
        crossing = decayed_score_grad * dots[head][:CHUNK] + strength * system_gram
        value_grad = strength * right_grads[head]
        beta_grad = jnp.sum(system_gram, axis=1, keepdims=True) + jnp.sum(right_grads[head] * gaps[head], axis=1, keepdims=True)
        open_grad = jnp.sum(mix_grads[head] * read_query - value_grad * read_key, axis=1, keepdims=True)
        close_grad = closed * jnp.sum(news[head] * pushes[head], axis=1, keepdims=True)
        last_grad = jnp.sum(close_grad, axis=0, keepdims=True) + opened_last * jnp.sum(
            jnp.sum(after_grad[head] * before[head].astype(f32), axis=1, keepdims=True), axis=0, keepdims=True
        )
        col = jnp.sum(crossing, axis=1, keepdims=True) + opened * open_grad - close_grad
        col = col + jnp.where(rows_down == CHUNK - 1, last_grad, 0.0)
        cross_rows.append(jnp.sum(crossing, axis=0, keepdims=True))
        cum_grad = jnp.where(lanes == head, col, cum_grad)
        beta_grads = jnp.where(lanes == heads + head, beta_grad, beta_grads)
        raised.append((decayed_score_grad.astype(bf), (strength * decayed_system).astype(bf), value_grad, opened))
    cross = jnp.concatenate(cross_rows + [jnp.zeros((CHUNK - heads, CHUNK), f32)], axis=0).T
    cum_grad = cum_grad - cross
    stacked = [
        jnp.concatenate([(opened * grad).astype(bf), (-opened * value_grad).astype(bf)], axis=0)
        for (_, _, value_grad, opened), grad in zip(raised, mix_grads)
    ]
    through = [nt(x, s) for x, s in zip(stacked, before)]
    grams = [jnp.concatenate([item[0], item[1]], axis=0) for item in raised]
    direct = [nn(g, k) for g, k in zip(grams, key_vecs)]
    turned = [tn(g, pair) for g, pair in zip(grams, pairs)]
    pushed = [nt(terms[head][2] * news[head], after_grad[head]) for head in range(heads)]
    for head in range(heads):
        state_grad[head] = terms[head][3] * after_grad[head] + tn(pairs[head], stacked[head])
    for head in range(heads):
        query_grad = (through[head][:CHUNK] + direct[head][:CHUNK]) * DK**-0.5
        key_grad = through[head][CHUNK:] + direct[head][CHUNK:] + turned[head] + pushed[head]
        for grad, act, scale, summed, start in (
            (query_grad, q_acts[head], q_scale[head], q_sums[head], head * DK),
            (key_grad, k_acts[head], k_scale[head], k_sums[head], keys + head * DK),
        ):
            inner = scale * (grad - act * (scale * scale) * jnp.sum(grad * act, axis=1, keepdims=True))
            soft = sigmoid(summed)
            summed_grad[0:CHUNK, start : start + DK] = inner * (soft * (1.0 + summed * (1.0 - soft)))
        summed = v_sums[head]
        soft = sigmoid(summed)
        start = 2 * keys + head * DV
        summed_grad[0:CHUNK, start : start + DV] = raised[head][2] * (soft * (1.0 + summed * (1.0 - soft)))
    for start in range(0, conv_width, LANES):
        columns = slice(start, start + LANES)
        grad = summed_grad[0:CHUNK, columns]
        total = taps[0:1, columns] * grad
        taps_grad[0:1, columns] += jnp.sum(grad * padded[8 : 8 + CHUNK, columns], axis=0, keepdims=True)
        for offset in range(1, 4):
            later = summed_grad[offset : offset + CHUNK, columns]
            total = total + (taps[offset : offset + 1, columns] * marks[:, 5 + offset : 6 + offset]) * later
            taps_grad[offset : offset + 1, columns] += jnp.sum(
                (grad * marks[:, offset : offset + 1]) * padded[8 - offset : 8 - offset + CHUNK, columns], axis=0, keepdims=True
            )
        proj_grad[:, columns] = total.astype(bf)
    summed_grad[CHUNK:, :] = summed_grad[0:8, :]
    upper = (places <= others).astype(f32)
    log_grad = exact(upper, cum_grad)
    decay_grad = log_grad * (-params[1:2, :]) * sigmoid(biased)
    both = decay_grad + beta_grads * beta * (1.0 - beta)
    proj_grad[:, conv_width + vals :] = both.astype(bf)
    params_grad[0:1, :] += jnp.sum(log_grad * log_decay, axis=0, keepdims=True)
    params_grad[1:2, :] += jnp.sum(decay_grad, axis=0, keepdims=True)


def mixer_forward(proj, marks, seg_rows, taps, params, gain, group_rows):
    rows, width = proj.shape
    heads = (width - LANES) // (2 * DK + 2 * DV)
    groups = rows // group_rows
    chunks = group_rows // CHUNK
    conv_width = heads * (2 * DK + DV)
    at = lambda g, c: (g * chunks + c, 0)
    return pl.pallas_call(
        functools.partial(forward_kernel, heads),
        grid=(groups, chunks),
        in_specs=[
            pl.BlockSpec((CHUNK, width), at),
            pl.BlockSpec((CHUNK, LANES), at),
            pl.BlockSpec((1, 1, CHUNK), lambda g, c: (g * chunks + c, 0, 0)),
            pl.BlockSpec((4, conv_width), lambda g, c: (0, 0)),
            pl.BlockSpec((8, LANES), lambda g, c: (0, 0)),
            pl.BlockSpec((1, DV), lambda g, c: (0, 0)),
        ],
        out_specs=[
            pl.BlockSpec((CHUNK, heads * DV), at),
            pl.BlockSpec((1, heads, DK, DV), lambda g, c: (g * chunks + c, 0, 0, 0)),
            pl.BlockSpec((CHUNK, heads * CHUNK), at),
        ],
        out_shape=[
            jax.ShapeDtypeStruct((rows, heads * DV), bf),
            jax.ShapeDtypeStruct((groups * chunks, heads, DK, DV), bf),
            jax.ShapeDtypeStruct((rows, heads * CHUNK), bf),
        ],
        scratch_shapes=[pltpu.VMEM((heads, DK, DV), f32), pltpu.VMEM((CHUNK + 8, conv_width), f32)],
        compiler_params=pltpu.CompilerParams(vmem_limit_bytes=48 * 2**20),
        cost_estimate=pl.CostEstimate(flops=rows * heads * 1500000, bytes_accessed=rows * width * 8, transcendentals=0),
        name="mixer_forward",
    )(proj, marks, seg_rows, taps, params, gain)


def mixer_backward(proj, grads, marks, seg_rows, taps, params, gain, states, inverses, group_rows):
    rows, width = proj.shape
    heads = (width - LANES) // (2 * DK + 2 * DV)
    groups = rows // group_rows
    chunks = group_rows // CHUNK
    conv_width = heads * (2 * DK + DV)
    at = lambda g, c: (g * chunks + chunks - 1 - c, 0)
    prev = lambda g, c: (jnp.maximum((g * chunks + chunks - 1 - c) * (CHUNK // 16) - 1, 0), 0)
    return pl.pallas_call(
        functools.partial(backward_kernel, heads),
        grid=(groups, chunks),
        in_specs=[
            pl.BlockSpec((CHUNK, width), at),
            pl.BlockSpec((16, width), prev),
            pl.BlockSpec((CHUNK, heads * DV), at),
            pl.BlockSpec((CHUNK, LANES), at),
            pl.BlockSpec((1, 1, CHUNK), lambda g, c: (g * chunks + chunks - 1 - c, 0, 0)),
            pl.BlockSpec((4, conv_width), lambda g, c: (0, 0)),
            pl.BlockSpec((8, LANES), lambda g, c: (0, 0)),
            pl.BlockSpec((1, DV), lambda g, c: (0, 0)),
            pl.BlockSpec((1, heads, DK, DV), lambda g, c: (g * chunks + chunks - 1 - c, 0, 0, 0)),
            pl.BlockSpec((CHUNK, heads * CHUNK), at),
        ],
        out_specs=[
            pl.BlockSpec((CHUNK, width), at),
            pl.BlockSpec((4, conv_width), lambda g, c: (0, 0)),
            pl.BlockSpec((8, LANES), lambda g, c: (0, 0)),
            pl.BlockSpec((8, DV), lambda g, c: (0, 0)),
        ],
        out_shape=[
            jax.ShapeDtypeStruct((rows, width), bf),
            jax.ShapeDtypeStruct((4, conv_width), f32),
            jax.ShapeDtypeStruct((8, LANES), f32),
            jax.ShapeDtypeStruct((8, DV), f32),
        ],
        scratch_shapes=[
            pltpu.VMEM((heads, DK, DV), f32),
            pltpu.VMEM((CHUNK + 8, conv_width), f32),
            pltpu.VMEM((CHUNK + 8, conv_width), f32),
        ],
        compiler_params=pltpu.CompilerParams(vmem_limit_bytes=48 * 2**20),
        cost_estimate=pl.CostEstimate(flops=rows * heads * 3000000, bytes_accessed=rows * width * 12, transcendentals=0),
        name="mixer_backward",
    )(proj, proj, grads, marks, seg_rows, taps, params, gain, states, inverses)


def group_marks(lengths, group_rows):
    groups, count = lengths.shape
    position = jnp.arange(group_rows, dtype=jnp.int32)[None, :]
    segment = jnp.zeros((groups, group_rows), jnp.int32)
    end = jnp.zeros((groups, 1), jnp.int32)
    for number in range(count):
        segment = segment + (position >= end).astype(jnp.int32)
        end = end + lengths[:, number : number + 1]
    live = (position < end).astype(f32)
    padded = jnp.pad(segment, ((0, 0), (CHUNK, CHUNK)))
    later = lambda offset: padded[:, CHUNK + offset : CHUNK + offset + group_rows]
    chunked = segment.reshape(groups, group_rows // CHUNK, CHUNK)
    before = padded[:, CHUNK - 1 : CHUNK - 1 + group_rows].reshape(chunked.shape)[:, :, :1]
    columns = [segment]
    columns += [later(-offset) == segment for offset in (1, 2, 3)]
    columns += [(chunked == before).reshape(segment.shape), (chunked == chunked[:, :, -1:]).reshape(segment.shape)]
    columns += [later(offset) == segment for offset in (1, 2, 3)]
    marks = jnp.stack([c.astype(f32) for c in columns], axis=-1).reshape(groups * group_rows, len(columns))
    marks = jnp.pad(marks, ((0, 0), (0, LANES - len(columns))))
    seg_rows = segment.astype(f32).reshape(groups * group_rows // CHUNK, 1, CHUNK)
    return marks, seg_rows, live


RING = (0, 1, 3, 2)


def matmul(left, right):
    return jnp.dot(left, right, preferred_element_type=f32)


def outer_sum(left, right):
    return lax.dot_general(left, right, (((0,), (0,)), ((), ())), preferred_element_type=f32)


def times_back(left, right):
    return lax.dot_general(left, right, (((1,), (1,)), ((), ())), preferred_element_type=f32)


def norm_back(inputs, scale, gain, grad_out):
    scaled = grad_out * gain
    grad_in = scale * scaled - inputs * scale**3 * jnp.mean(scaled * inputs, axis=1, keepdims=True)
    return (grad_in, jnp.sum(grad_out * inputs * scale, axis=0))


class Layout:
    def __init__(self):
        self.ways = lax.axis_size("dp")
        self.spans = self.ways // 8
        dp = lax.axis_index("dp")
        self.core = lax.axis_index("tensor")
        self.dp = dp
        self.turn = (dp // 4) % 2
        self.far = dp // 8
        near = dp % 4
        self.spot = near ^ (near >> 1)

    def ring(self, values, step):
        pairs = []
        for number in range(self.ways):
            near = number % 4
            pairs.append((number, number - near + RING[((near ^ (near >> 1)) + step) % 4]))
        return lax.ppermute(values, "dp", pairs)

    def flip(self, values, bit):
        return lax.ppermute(values, "dp", [(n, n ^ bit) for n in range(self.ways)])

    def turned(self, values):
        return self.flip(values, 4)

    def crossed(self, values):
        return lax.ppermute(values, "tensor", [(0, 1), (1, 0)])

    def far_bits(self):
        bit = 8
        while bit < self.ways:
            yield bit
            bit *= 2

    def sources(self):
        places = jnp.arange(self.ways, dtype=jnp.int32)
        step = places // (2 * self.spans)
        jump = (places // 2) % self.spans
        spot = (self.spot + step) % 4
        return ((self.far ^ jump) * 2 + places % 2) * 4 + (spot ^ (spot >> 1))

    def ordered(self, first, second, flag):
        return jnp.where(
            flag == 0, jnp.concatenate([first, second], axis=0), jnp.concatenate([second, first], axis=0)
        )

    def halves(self, weight):
        half = weight.shape[1] // 2
        keep = lax.dynamic_slice_in_dim(weight, self.turn * half, half, 1)
        give = lax.dynamic_slice_in_dim(weight, (1 - self.turn) * half, half, 1)
        return keep, give

    def spread(self, weights):
        pairs = [self.halves(weight) for weight in weights]
        keep = jnp.concatenate([pair[0] for pair in pairs], axis=1)
        give = jnp.concatenate([pair[1] for pair in pairs], axis=1)
        short = -keep.shape[1] % LANES
        if short:
            keep = jnp.pad(keep, ((0, 0), (0, short)))
            give = jnp.pad(give, ((0, 0), (0, short)))
        chunk = self.ordered(keep, self.turned(give), self.turn)
        for bit in self.far_bits():
            chunk = jnp.concatenate([chunk, self.flip(chunk, bit)], axis=0)
        half = chunk.shape[0] // 2
        ahead = self.ring(chunk, -1)
        behind = self.ring(chunk, 1)
        top = self.ring(ahead[:half], -1)
        bottom = self.ring(behind[half:], 1)
        return jnp.concatenate([chunk, ahead, top, bottom, behind], axis=0)

    def collect(self, grad):
        width = grad.shape[1]
        pieces = grad.reshape(4, -1, width)
        half = pieces.shape[1] // 2
        up = self.ring(pieces[2, :half].astype(bf), 1)
        down = self.ring(pieces[2, half:].astype(bf), -1)
        up = self.ring(jnp.concatenate([pieces[1, :half] + up, pieces[1, half:]], axis=0).astype(bf), 1)
        down = self.ring(jnp.concatenate([pieces[3, :half], pieces[3, half:] + down], axis=0).astype(bf), -1)
        own = pieces[0] + up + down
        for bit in reversed(list(self.far_bits())):
            half = own.shape[0] // 2
            own = own[:half] + self.flip(own[half:].astype(bf), bit)
        half = own.shape[0] // 2
        mine = lax.dynamic_slice_in_dim(own, self.turn * half, half, 0)
        other = lax.dynamic_slice_in_dim(own, (1 - self.turn) * half, half, 0)
        return mine, self.turned(other.astype(bf)).astype(f32)

    def columns(self, mine, theirs, start, stop):
        return jnp.where(
            self.turn == 0,
            jnp.concatenate([mine[:, start:stop], theirs[:, start:stop]], axis=1),
            jnp.concatenate([theirs[:, start:stop], mine[:, start:stop]], axis=1),
        )

    def rows_of(self, own):
        across = self.crossed(own)
        there = self.turned(own)
        return across, there, self.crossed(there)

    def own_of(self, mine, give):
        total = mine + self.crossed(give.astype(bf))
        return total[0] + self.turned(total[1].astype(bf))

    def everywhere(self, values):
        bit = 1
        while bit < self.ways:
            values = values + self.flip(values, bit)
            bit *= 2
        return values + self.crossed(values)


def flat(parts):
    joined = jnp.concatenate([part.reshape(-1) for part in parts])
    return jnp.pad(joined, (0, -joined.shape[0] % (8 * LANES))).reshape(-1, LANES)


def shards(
    tokens, cotangent, lengths, slot_of, norm_gains, w_query, w_key, w_value, w_gate, w_decay, w_beta,
    conv_weights, a_log, dt_bias, out_gain, w_out, w_mlp_gate, w_mlp_up, w_mlp_down,
):
    lay = Layout()
    row_count, features = tokens.shape
    tensor_ways = lax.axis_size("tensor")
    device_count = lay.ways * tensor_ways
    group_rows = row_count * tensor_ways
    capacity = row_count // device_count + 2
    bulk_rows = device_count * capacity
    all_heads = a_log.shape[0]
    heads = all_heads // (2 * tensor_ways)
    keys_here = heads * DK
    vals_here = heads * DV
    all_keys = all_heads * DK
    conv_width = 2 * keys_here + vals_here
    share = lay.core * 2 + lay.turn

    target = slot_of // row_count
    within = slot_of % row_count
    hits = target[:, None] == jnp.arange(device_count, dtype=jnp.int32)[None, :]
    places = jnp.arange(row_count, dtype=jnp.int32)
    earlier = (places[:, None] >= places[None, :]).astype(bf)
    rank = jnp.sum(matmul(earlier, hits.astype(bf)) * hits.astype(f32), axis=1).astype(jnp.int32) - 1
    outgoing = target * capacity + rank
    sending = (jnp.arange(bulk_rows, dtype=jnp.int32)[:, None] == outgoing[None, :]).astype(bf)
    slot_mark = jnp.broadcast_to((within + 1).astype(bf)[:, None], (row_count, LANES))
    send_tokens = matmul(sending, jnp.concatenate([tokens, slot_mark], axis=1)).astype(bf)
    send_cot = matmul(sending, cotangent).astype(bf)

    def exchange(values):
        return lax.all_to_all(values, ("dp", "tensor"), split_axis=0, concat_axis=0, tiled=True)

    got_tokens = exchange(send_tokens)
    got_slot = got_tokens[:, features].astype(jnp.int32)
    landing = (places[:, None] + 1 == got_slot[None, :]).astype(bf)
    sources = lay.sources()
    block = features // lay.ways
    feature = jnp.arange(features, dtype=jnp.int32)
    turning = (feature[:, None] == (sources[:, None] * block + jnp.arange(block, dtype=jnp.int32)[None, :]).reshape(1, -1)).astype(bf)
    x_own = matmul(matmul(landing, got_tokens[:, :features]).astype(bf), turning)
    numbers = jnp.arange(lay.ways, dtype=jnp.int32)
    picking = (sources[:, None] == numbers[None, :]).astype(f32)

    def reordered_gain(gain):
        return jnp.sum(picking[:, :, None] * gain.reshape(1, lay.ways, block), axis=1).reshape(features)

    def straight_gain(grad):
        return jnp.sum(picking[:, :, None] * grad.reshape(lay.ways, 1, block), axis=0).reshape(features)

    gains = (reordered_gain(norm_gains[0]), reordered_gain(norm_gains[1]))

    pair_lengths = jnp.concatenate([lengths, lay.turned(lengths)], axis=0)
    marks, seg_rows, live = group_marks(pair_lengths, group_rows)
    live_own = lax.dynamic_slice_in_dim(live[0], lay.core * row_count, row_count)[:, None]
    starts = (share * keys_here, all_keys + share * keys_here, 2 * all_keys + share * vals_here)
    sizes = (keys_here, keys_here, vals_here)
    taps = jnp.concatenate(
        [lax.dynamic_slice_in_dim(conv_weights, start, size, 1) for start, size in zip(starts, sizes)], axis=1
    )
    log_here = lax.dynamic_slice_in_dim(a_log, share * heads, heads)
    bias_here = lax.dynamic_slice_in_dim(dt_bias, share * heads, heads)
    params = jnp.pad(jnp.stack([bias_here, jnp.exp(log_here)]), ((0, 6), (0, LANES - heads)))
    gain_row = out_gain[None, :]

    weights_in = lay.spread([w_query, w_key, w_value, w_gate, w_decay, w_beta])
    weights_out = lay.spread([w_out.T])
    weights_gate = lay.spread([w_mlp_gate])
    weights_up = lay.spread([w_mlp_up])
    weights_down = lay.spread([w_mlp_down.T])

    def group_order(own):
        across, there, beyond = lay.rows_of(own)
        return jnp.concatenate([lay.ordered(own, across, lay.core), lay.ordered(there, beyond, lay.core)], axis=0)

    def own_of_groups(partial):
        partial = partial.reshape(2, 2, row_count, features)
        mine = lax.dynamic_index_in_dim(partial, lay.core, 1, keepdims=False)
        give = lax.dynamic_index_in_dim(partial, 1 - lay.core, 1, keepdims=False)
        return lay.own_of(mine, give)

    def own_of_rows(partial):
        partial = partial.reshape(2, 2, row_count, features)
        return lay.own_of(partial[:, 0], partial[:, 1])

    def any_order(own):
        across, there, beyond = lay.rows_of(own)
        return jnp.concatenate([own, across, there, beyond], axis=0)

    scale_one = lax.rsqrt(jnp.mean(x_own * x_own, axis=1, keepdims=True) + EPS_ROW)
    first_rows = group_order((x_own * scale_one * gains[0]).astype(bf))
    proj = matmul(first_rows, weights_in)
    heads_out, states, inverses = mixer_forward(proj, marks, seg_rows, taps, params, gain_row, group_rows)
    middle = x_own + live_own * own_of_groups(times_back(heads_out, weights_out))
    scale_two = lax.rsqrt(jnp.mean(middle * middle, axis=1, keepdims=True) + EPS_ROW)
    second_rows = any_order((middle * scale_two * gains[1]).astype(bf))

    got_cot = exchange(send_cot)
    dy_own = matmul(matmul(landing, got_cot).astype(bf), turning)
    branch_rows = any_order((live_own * dy_own).astype(bf))

    gate_pre = matmul(second_rows, weights_gate)
    up_proj = matmul(second_rows, weights_up)
    hidden = (jax.nn.silu(gate_pre) * up_proj).astype(bf)
    grad_hidden = matmul(branch_rows, weights_down)
    soft = jax.nn.sigmoid(gate_pre)
    grad_gate = (grad_hidden * up_proj * soft * (1.0 + gate_pre * (1.0 - soft))).astype(bf)
    grad_up = (grad_hidden * gate_pre * soft).astype(bf)
    down_grad = lay.collect(outer_sum(branch_rows, hidden))
    gate_grad = lay.collect(outer_sum(second_rows, grad_gate))
    up_grad = lay.collect(outer_sum(second_rows, grad_up))
    branch_own = own_of_rows(times_back(hidden, weights_down))
    result_own = (middle + live_own * branch_own).astype(bf)
    grad_second = own_of_rows(times_back(grad_gate, weights_gate) + times_back(grad_up, weights_up))
    grad_mid_norm, gain_two_grad = norm_back(middle, scale_two, gains[1], grad_second)
    grad_middle = dy_own + grad_mid_norm
    mix_rows = group_order((live_own * grad_middle).astype(bf))
    grad_heads = matmul(mix_rows, weights_out).astype(bf)
    out_grad = lay.collect(outer_sum(mix_rows, heads_out))
    proj_grad, taps_grad, params_grad, gain_grad = mixer_backward(
        proj, grad_heads, marks, seg_rows, taps, params, gain_row, states, inverses, group_rows
    )
    in_grad = lay.collect(outer_sum(first_rows, proj_grad))
    grad_first = own_of_groups(times_back(proj_grad, weights_in))
    grad_x_norm, gain_one_grad = norm_back(x_own, scale_one, gains[0], grad_first)
    grad_tokens = (grad_middle + grad_x_norm).astype(bf)

    def sent_back(own):
        straight = times_back(own, turning).astype(bf)
        back = exchange(outer_sum(landing, straight).astype(bf))
        return outer_sum(sending, back).astype(bf)

    output = sent_back(result_own)
    tokens_grad = sent_back(grad_tokens)

    conv_full = jnp.zeros(conv_weights.shape, f32)
    begin = 0
    for start, size in zip(starts, sizes):
        conv_full = lax.dynamic_update_slice_in_dim(conv_full, taps_grad[:, begin : begin + size], start, 1)
        begin += size
    log_full = lax.dynamic_update_slice_in_dim(jnp.zeros_like(a_log), params_grad[0, :heads], share * heads, 0)
    bias_full = lax.dynamic_update_slice_in_dim(jnp.zeros_like(dt_bias), params_grad[1, :heads], share * heads, 0)

    early = lay.everywhere(flat([conv_full, straight_gain(gain_two_grad), gain_grad[0], log_full, bias_full])).reshape(-1)
    late = lay.everywhere(flat([straight_gain(gain_one_grad)])).reshape(-1)[:features]
    conv_size = conv_full.size
    cuts = [conv_size, conv_size + features, conv_size + features + DV, conv_size + features + DV + all_heads]
    norm_grad = jnp.stack([late, early[cuts[0] : cuts[1]]])

    in_columns = []
    begin = 0
    for size in (keys_here, keys_here, vals_here, vals_here, heads, heads):
        in_columns.append(lay.columns(*in_grad, begin, begin + size))
        begin += size
    hidden_here = weights_gate.shape[1]
    return (
        output,
        tokens_grad,
        norm_grad,
        *in_columns,
        early[:conv_size].reshape(conv_full.shape),
        early[cuts[2] : cuts[3]],
        early[cuts[3] : cuts[3] + all_heads],
        early[cuts[1] : cuts[2]],
        lay.columns(*out_grad, 0, vals_here).T,
        lay.columns(*gate_grad, 0, hidden_here),
        lay.columns(*up_grad, 0, hidden_here),
        lay.columns(*down_grad, 0, hidden_here).T,
    )


def solution(mesh):
    return jax.shard_map(
        shards,
        mesh=mesh,
        in_specs=(
            P(("dp", "tensor"), None),
            P(("dp", "tensor"), None),
            P("dp", None),
            P(("dp", "tensor")),
            P(),
            P("dp", "tensor"),
            P("dp", "tensor"),
            P("dp", "tensor"),
            P("dp", "tensor"),
            P("dp", "tensor"),
            P("dp", "tensor"),
            P(),
            P(),
            P(),
            P(),
            P("tensor", "dp"),
            P("dp", "tensor"),
            P("dp", "tensor"),
            P("tensor", "dp"),
        ),
        out_specs=(
            P(("dp", "tensor"), None),
            P(("dp", "tensor"), None),
            P(),
            P("dp", "tensor"),
            P("dp", "tensor"),
            P("dp", "tensor"),
            P("dp", "tensor"),
            P("dp", "tensor"),
            P("dp", "tensor"),
            P(),
            P(),
            P(),
            P(),
            P("tensor", "dp"),
            P("dp", "tensor"),
            P("dp", "tensor"),
            P("tensor", "dp"),
        ),
        check_vma=False,
    )
```

time: 5680 us -> 1420 us (0.25)
  waiting for transfers between devices: 3710 us -> 681 us
  other arithmetic: 853 us -> 142 us
  matrix products: 641 us -> 219 us
  blocking collectives: 146 us -> 0 us
  local copies, waits for them, and re-layouts: 261 us -> 184 us
  Pallas kernels: 0 us -> 76.8 us
  starting transfers between devices: 25.8 us -> 101 us
    reduce_scatter x14 -> x0, waiting for transfers between devices: 2940 us -> none  [the longest x1 483 us: shards(): lax.psum_scatter(outer_sum(hidden, branch_rows), 'dp', scatter_dimension=...]
    ppermute x0 -> x91, waiting for transfers between devices: none -> 670 us  [the longest x37 433 us: flip(): return lax.ppermute(values, 'dp', [(n, n ^ bit) for n in range(self.ways)])]
    another operation x134 -> x12, other arithmetic: 657 us -> 34.9 us  [the longest x72 638 us: block_rule(): jax.scipy.linalg.solve_triangular(system, right_side, lower=True, unit_di...]
    all_gather x12 -> x0, waiting for transfers between devices: 598 us -> none  [the longest x1 171 us: gather_mlp(): lax.all_gather(w_mlp_down, 'dp', axis=1, tiled=True)]
    dot_general x162 -> x10, matrix products: 431 us -> 83.5 us  [matmul(): return jnp.dot(left, right, preferred_element_type=f32)]
    all_to_all x5 -> x4, waiting for transfers between devices: 163 us -> 11.4 us  [exchange(): lax.all_to_all(values, ('dp', 'tensor'), split_axis=0, concat_axis=0, til...]
    dynamic_update_slice x153 -> x5, local copies, waits for them, and re-layouts: 82.5 us -> 0.21 us  [the longest x1 0.09 us: shards(): lax.dynamic_update_slice_in_dim(jnp.zeros_like(dt_bias), params_grad[1, :...]
    ppermute x0 -> x91, starting transfers between devices: none -> 81.7 us  [the longest x40 44.6 us: ring(): return lax.ppermute(values, 'dp', pairs)]
  transfers between devices with their start and end apart: 32 -> 95, of which waited for: 23 -> 35; matrix products, arithmetic and copies ran while one was open for 16% -> 32% of each run, Pallas kernels for 0% -> 5%
where the time goes in v1:
time: 1420 us; the launch traced here: 1410 us
  waiting for transfers between devices  681 us (48%)
  matrix products  219 us (15%)
  local copies, waits for them, and re-layouts  184 us (13%)
  other arithmetic  142 us (10%)
  starting transfers between devices  101 us (7%)
  Pallas kernels  76.8 us (5%)
    ppermute x37, waiting for transfers between devices, flip(): return lax.ppermute(values, 'dp', [(n, n ^ bit) for n in range(self.ways)])  433 us
    ppermute x40, waiting for transfers between devices, ring(): return lax.ppermute(values, 'dp', pairs)  237 us
    dot_general x10, matrix products, matmul(): return jnp.dot(left, right, preferred_element_type=f32)  83.5 us
    dot_general x9, matrix products, outer_sum(): lax.dot_general(left, right, (((0,), (0,)), ((), ())), preferred_element_...  79.9 us
    unnamed x270, local copies, waits for them, and re-layouts  70.6 us
    dot_general x5, matrix products, times_back(): lax.dot_general(left, right, (((1,), (1,)), ((), ())), preferred_element_...  55.6 us
    pallas_call x1, Pallas kernels, mixer_backward(): pl.pallas_call(functools.partial(backward_kernel, heads), grid=(groups, c...  49.5 us
    ppermute x40, starting transfers between devices, ring(): return lax.ppermute(values, 'dp', pairs)  44.6 us
  transfers between devices with their start and end apart: 95, of which 35 were waited for; matrix products, arithmetic and copies ran while one was open for 32% of the time, Pallas kernels for 5%

profile of v1, /device:TPU:0, one launch (start us, length us, event | category | flops | bytes accessed | tf_op | source)
XLA Modules:
  0.0 1407.2 jit_solution(11341959951103179263)
XLA Ops:
  58.5 10.8 collective-permute-done
  85.7 18.7 %collective-permute-done.33 = bf16[128,1408]{0,1:T(8,128)(2,1)} collective-permute-done((bf16[128,1408]{0,1:T(8,128)(2,1)}, bf16[128,1408]{0,1:T(8,128)(2,1)}, u32[]{:S(2)}, u32[]{:S(2)}) %collective-permute-start.33) | collective-permute-done | bytes 360480 | tf_op jit(solution)/shard_map/ppermute | solution.py:455
  106.8 69.9 %collective-permute-done.5 = bf16[256,3200]{1,0:T(8,128)(2,1)} collective-permute-done((bf16[256,3200]{1,0:T(8,128)(2,1)}, bf16[256,3200]{1,0:T(8,128)(2,1)}, u32[]{:S(2)}, u32[]{:S(2)}) %collective-permute-start.5) | collective-permute-done | bytes 1638432 | tf_op jit(solution)/shard_map/ppermute | solution.py:455
  187.7 15.6 %collective-permute-done.11 = bf16[256,1024]{0,1:T(8,128)(2,1)S(1)} collective-permute-done((bf16[256,1024]{0,1:T(8,128)(2,1)S(1)}, bf16[256,1024]{0,1:T(8,128)(2,1)S(1)}, u32[]{:S(2)}, u32[]{:S(2)}) %collective-permute-start.11) | collective-permute-done | bytes 524320 | tf_op jit(solution)/shard_map/ppermute | solution.py:455
  233.2 23.8 %collective-permute-done.28 = bf16[256,1408]{0,1:T(8,128)(2,1)} collective-permute-done((bf16[256,1408]{0,1:T(8,128)(2,1)}, bf16[256,1408]{0,1:T(8,128)(2,1)}, u32[]{:S(2)}, u32[]{:S(2)}) %collective-permute-start.28) | collective-permute-done | bytes 720928 | tf_op jit(solution)/shard_map/ppermute | solution.py:455
  257.3 35.2 %collective-permute-done.12 = bf16[512,1024]{0,1:T(8,128)(2,1)} collective-permute-done((bf16[512,1024]{0,1:T(8,128)(2,1)}, bf16[512,1024]{0,1:T(8,128)(2,1)}, u32[]{:S(2)}, u32[]{:S(2)}) %collective-permute-start.12) | collective-permute-done | bytes 1048608 | tf_op jit(solution)/shard_map/ppermute | solution.py:452
  312.7 15.7 %collective-permute-done.2 = bf16[256,2048]{1,0:T(8,128)(2,1)S(1)} collective-permute-done((bf16[256,2048]{1,0:T(8,128)(2,1)S(1)}, bf16[256,2048]{1,0:T(8,128)(2,1)S(1)}, u32[]{:S(2)}, u32[]{:S(2)}) %collective-permute-start.2) | collective-permute-done | bytes 1048608 | tf_op jit(solution)/shard_map/ppermute | solution.py:455
  347.9 50.3 %collective-permute-done.7 = bf16[256,3200]{1,0:T(8,128)(2,1)S(1)} collective-permute-done((bf16[256,3200]{1,0:T(8,128)(2,1)S(1)}, bf16[256,3200]{1,0:T(8,128)(2,1)S(1)}, u32[]{:S(2)}, u32[]{:S(2)}) %collective-permute-start.7) | collective-permute-done | bytes 1638432 | tf_op jit(solution)/shard_map/ppermute | solution.py:452
  407.2 21.0 %fusion.21.proj.prev_rows = f32[1024,3200]{1,0:T(8,128)} fusion(bf16[2048,3200]{1,0:T(8,128)(2,1)} %constant_dynamic-update-slice_fusion, bf16[512,2048]{1,0:T(8,128)(2,1)S(1)} %maximum_select_fusion.1, bf16[512,2048]{1,0:T(8,128)(2,1)S(1)} %maximum_select_fusion), kind=kOutput, calls=%fused_computation.51 | convolution fusion | flops 13430161408 | bytes 30408704 | tf_op jit(solution)/shard_map/dot_general | solution.py:418
  428.3 27.4 %mixer_forward.1 = (bf16[1024,1024]{1,0:T(8,128)(2,1)S(1)}, bf16[8,4,128,256]{3,2,1,0:T(8,128)(2,1)S(1)}, bf16[1024,512]{1,0:T(8,128)(2,1)S(1)}) custom-call(f32[1024,3200]{1,0:T(8,128)} %fusion.21.proj.prev_rows, f32[1024,128]{1,0:T(8,128)S(1)} %pad.26.marks_ref, f32[8,1,128]{2,1,0:T(1,128)S(1)} %fusion.126.seg_ref, f32[4,2048]{1,0:T(4,128)S(1)} %pad_maximum_fusion.27.taps, ...), custom_call_target="tpu_custom_call" | custom-call | flops 6144000000 | bytes 26214400 | tf_op jit(solution)/shard_map/mixer_forward/pallas_call | solution.py:317
  485.6 12.4 collective-permute-done.25
  547.4 20.1 %collective-permute-done.42 = bf16[256,2048]{1,0:T(8,128)(2,1)S(1)} collective-permute-done((bf16[256,2048]{1,0:T(8,128)(2,1)S(1)}, bf16[256,2048]{1,0:T(8,128)(2,1)S(1)}, u32[]{:S(2)}, u32[]{:S(2)}) %collective-permute-start.42) | collective-permute-done | bytes 1048608 | tf_op jit(solution)/shard_map/ppermute | solution.py:455
  583.7 11.1 fusion.81
  596.8 13.7 fusion.150
  610.5 17.3 %multiply_convert_fusion.1 = (bf16[1024,1408]{1,0:T(8,128)(2,1)}, bf16[1024,1408]{1,0:T(8,128)(2,1)}, bf16[1024,1408]{1,0:T(8,128)(2,1)}) fusion(f32[1024,1408]{1,0:T(8,128)} %fusion.81, f32[1024,1408]{1,0:T(8,128)} %fusion.150, bf16[2048,1408]{0,1:T(8,128)(2,1)} %constant_dynamic-update-slice_fusion.12, bf16[256,2048]{1,0:T(8,128)(2,1)} %copy-done.100, ...), kind=kOutput, calls=%fused_computation.12 | convolution fusion | flops 5945425920 | bytes 30146560 | tf_op jit(solution)/shard_map/dot_general | solution.py:418
  684.3 11.3 fusion.148
  703.7 11.6 fusion.80
  727.3 13.0 collective-permute-done.81
  768.5 18.3 %collective-permute-done.76 = bf16[512,1408]{1,0:T(8,128)(2,1)} collective-permute-done((bf16[512,1408]{1,0:T(8,128)(2,1)S(1)}, bf16[512,1408]{1,0:T(8,128)(2,1)}, u32[]{:S(2)}, u32[]{:S(2)}) %collective-permute-start.76) | collective-permute-done | bytes 1441824 | tf_op jit(solution)/shard_map/ppermute | solution.py:452
  792.2 25.5 %collective-permute-done.82 = bf16[512,1408]{1,0:T(8,128)(2,1)} collective-permute-done((bf16[512,1408]{1,0:T(8,128)(2,1)}, bf16[512,1408]{1,0:T(8,128)(2,1)}, u32[]{:S(2)}, u32[]{:S(2)}) %collective-permute-start.82) | collective-permute-done | bytes 1441824 | tf_op jit(solution)/shard_map/ppermute | solution.py:452
  824.1 23.0 %collective-permute-done.88 = bf16[512,1408]{1,0:T(8,128)(2,1)} collective-permute-done((bf16[512,1408]{1,0:T(8,128)(2,1)}, bf16[512,1408]{1,0:T(8,128)(2,1)}, u32[]{:S(2)}, u32[]{:S(2)}) %collective-permute-start.88) | collective-permute-done | bytes 1441824 | tf_op jit(solution)/shard_map/ppermute | solution.py:452
  861.4 41.5 %collective-permute-done.83 = bf16[256,1408]{1,0:T(8,128)(2,1)S(1)} collective-permute-done((bf16[256,1408]{1,0:T(8,128)(2,1)S(1)}, bf16[256,1408]{1,0:T(8,128)(2,1)S(1)}, u32[]{:S(2)}, u32[]{:S(2)}) %collective-permute-start.83) | collective-permute-done | bytes 720928 | tf_op jit(solution)/shard_map/ppermute | solution.py:455
  905.7 12.7 collective-permute-done.89
  942.3 25.0 %collective-permute-done.90 = bf16[128,1408]{1,0:T(8,128)(2,1)} collective-permute-done((bf16[128,1408]{1,0:T(8,128)(2,1)}, bf16[128,1408]{1,0:T(8,128)(2,1)}, u32[]{:S(2)}, u32[]{:S(2)}) %collective-permute-start.90) | collective-permute-done | bytes 360480 | tf_op jit(solution)/shard_map/ppermute | solution.py:455
  990.5 49.5 %mixer_backward.1 = (bf16[1024,3200]{1,0:T(8,128)(2,1)}, f32[4,2048]{1,0:T(4,128)S(1)}, f32[8,128]{1,0:T(8,128)S(1)}, f32[8,256]{1,0:T(8,128)S(1)}) custom-call(f32[1024,3200]{1,0:T(8,128)} %fusion.21.proj.prev_rows, f32[1024,3200]{1,0:T(8,128)} %fusion.21.proj.prev_rows, bf16[1024,1024]{1,0:T(8,128)(2,1)S(1)} %fusion.38.grads, ...), custom_call_target="tpu_custom_call" | custom-call | flops 12288000000 | bytes 39321600 | tf_op jit(solution)/shard_map/mixer_backward/pallas_call | solution.py:353
  1039.9 20.6 %fusion.170 = f32[1024,2048]{1,0:T(8,128)} fusion(bf16[1024,3200]{1,0:T(8,128)(2,1)} %get-tuple-element.27, bf16[2048,3200]{1,0:T(8,128)(2,1)} %constant_dynamic-update-slice_fusion), kind=kOutput, calls=%fused_computation.424 | convolution fusion | flops 13421772800 | bytes 28049408 | tf_op jit(solution)/shard_map/dot_general | solution.py:426
  1060.5 20.7 %fusion.20 = f32[2048,3200]{1,0:T(8,128)} fusion(bf16[1024,3200]{1,0:T(8,128)(2,1)} %get-tuple-element.27, bf16[512,2048]{1,0:T(8,128)(2,1)S(1)} %copy-done.39, bf16[512,2048]{1,0:T(8,128)(2,1)S(1)} %copy-done.37), kind=kOutput, calls=%fused_computation.50 | convolution fusion | flops 13430161408 | bytes 36962304 | tf_op jit(solution)/shard_map/dot_general | solution.py:422
  1104.8 37.3 %collective-permute-done.67 = bf16[256,1024]{1,0:T(8,128)(2,1)S(1)} collective-permute-done((bf16[256,1024]{1,0:T(8,128)(2,1)S(1)}, bf16[256,1024]{1,0:T(8,128)(2,1)S(1)}, u32[]{:S(2)}, u32[]{:S(2)}) %collective-permute-start.67) | collective-permute-done | bytes 524320 | tf_op jit(solution)/shard_map/ppermute | solution.py:452
  1175.5 13.4 collective-permute-done.50
  1200.9 41.4 %collective-permute-done.56 = f32[280,128]{1,0:T(8,128)S(1)} collective-permute-done((f32[280,128]{1,0:T(8,128)S(1)}, f32[280,128]{1,0:T(8,128)S(1)}, u32[]{:S(2)}, u32[]{:S(2)}) %collective-permute-start.56) | collective-permute-done | bytes 143392 | tf_op jit(solution)/shard_map/ppermute | solution.py:455
  1282.3 77.8 %collective-permute-done.54 = f32[16,128]{1,0:T(8,128)S(1)} collective-permute-done((f32[16,128]{1,0:T(8,128)S(1)}, f32[16,128]{1,0:T(8,128)S(1)}, u32[]{:S(2)}, u32[]{:S(2)}) %collective-permute-start.54) | collective-permute-done | bytes 8224 | tf_op jit(solution)/shard_map/ppermute | solution.py:455
  1374.3 11.4 all-to-all-done.3
  (678 shorter events, 586.9 us)
Async XLA Ops:
  5.2 200.7 %all-to-all-start = ((bf16[32,10,2176]{2,1,0:T(8,128)(2,1)}), bf16[32,10,2176]{2,1,0:T(8,128)(2,1)S(1)}, u32[]{:S(2)}, u32[]{:S(2)}) async-start(bf16[32,10,2176]{2,1,0:T(8,128)(2,1)} %all_to_all.32), calls=%async_computation | async-start | bytes 4456448 | tf_op jit(solution)/shard_map/all_to_all | solution.py:583
  30.8 73.5 %collective-permute-start.33 = (bf16[128,1408]{0,1:T(8,128)(2,1)}, bf16[128,1408]{0,1:T(8,128)(2,1)}, u32[]{:S(2)}, u32[]{:S(2)}) collective-permute-start(bf16[128,1408]{0,1:T(8,128)(2,1)} %get-tuple-element.225), channel_id=1, source_target_pairs={{0,8},{2,10},{4,12},{6,14},{8,0},{10,2},{12,4},{14,6},{16,24},{18,... | collective-permute-start | bytes 1081352 | tf_op jit(solution)/shard_map/ppermute | solution.py:455
  35.4 146.6 %collective-permute-start.27 = (bf16[128,1408]{0,1:T(8,128)(2,1)}, bf16[128,1408]{0,1:T(8,128)(2,1)}, u32[]{:S(2)}, u32[]{:S(2)}) collective-permute-start(bf16[128,1408]{0,1:T(8,128)(2,1)} %copy.255), channel_id=1, source_target_pairs={{0,8},{2,10},{4,12},{6,14},{8,0},{10,2},{12,4},{14,6},{16,24},{18,... | collective-permute-start | bytes 1081352 | tf_op jit(solution)/shard_map/ppermute | solution.py:455
  69.3 115.3 %collective-permute-start.21 = (bf16[128,1408]{0,1:T(8,128)(2,1)}, bf16[128,1408]{0,1:T(8,128)(2,1)}, u32[]{:S(2)}, u32[]{:S(2)}) collective-permute-start(bf16[128,1408]{0,1:T(8,128)(2,1)} %copy.253), channel_id=1, source_target_pairs={{0,8},{2,10},{4,12},{6,14},{8,0},{10,2},{12,4},{14,6},{16,24},{18,... | collective-permute-start | bytes 1081352 | tf_op jit(solution)/shard_map/ppermute | solution.py:455
  75.0 101.7 %collective-permute-start.5 = (bf16[256,3200]{1,0:T(8,128)(2,1)}, bf16[256,3200]{1,0:T(8,128)(2,1)}, u32[]{:S(2)}, u32[]{:S(2)}) collective-permute-start(bf16[256,3200]{1,0:T(8,128)(2,1)} %get-tuple-element.177), channel_id=1, source_target_pairs={{0,16},{2,18},{4,20},{6,22},{8,24},{10,26},{12,28},{14,30},{16,0},... | collective-permute-start | bytes 4915208 | tf_op jit(solution)/shard_map/ppermute | solution.py:455
  84.6 118.8 %collective-permute-start.11 = (bf16[256,1024]{0,1:T(8,128)(2,1)S(1)}, bf16[256,1024]{0,1:T(8,128)(2,1)S(1)}, u32[]{:S(2)}, u32[]{:S(2)}) collective-permute-start(bf16[256,1024]{0,1:T(8,128)(2,1)S(1)} %get-tuple-element.173), channel_id=1, source_target_pairs={{0,16},{2,18},{4,20},{6,22},{8,24},{10,26},{12,28},{14,30},{16,0},... | collective-permute-start | bytes 1572872 | tf_op jit(solution)/shard_map/ppermute | solution.py:455
  106.8 116.4 %collective-permute-start.34 = (bf16[256,1408]{0,1:T(8,128)(2,1)}, bf16[256,1408]{0,1:T(8,128)(2,1)}, u32[]{:S(2)}, u32[]{:S(2)}) collective-permute-start(bf16[256,1408]{0,1:T(8,128)(2,1)} %get-tuple-element.165), channel_id=1, source_target_pairs={{0,16},{2,18},{4,20},{6,22},{8,24},{10,26},{12,28},{14,30},{16,0},... | collective-permute-start | bytes 2162696 | tf_op jit(solution)/shard_map/ppermute | solution.py:455
  180.6 148.0 %collective-permute-start.6 = (bf16[512,3200]{1,0:T(8,128)(2,1)}, bf16[512,3200]{1,0:T(8,128)(2,1)}, u32[]{:S(2)}, u32[]{:S(2)}) collective-permute-start(bf16[512,3200]{1,0:T(8,128)(2,1)} %pad_maximum_fusion.4), channel_id=1, source_target_pairs={{0,4},{2,0},{4,6},{6,2},{8,12},{10,8},{12,14},{14,10},{16,20},{18,... | collective-permute-start | bytes 9830408 | tf_op jit(solution)/shard_map/ppermute | solution.py:452
  184.5 72.5 %collective-permute-start.28 = (bf16[256,1408]{0,1:T(8,128)(2,1)}, bf16[256,1408]{0,1:T(8,128)(2,1)}, u32[]{:S(2)}, u32[]{:S(2)}) collective-permute-start(bf16[256,1408]{0,1:T(8,128)(2,1)} %get-tuple-element.171), channel_id=1, source_target_pairs={{0,16},{2,18},{4,20},{6,22},{8,24},{10,26},{12,28},{14,30},{16,0},... | collective-permute-start | bytes 2162696 | tf_op jit(solution)/shard_map/ppermute | solution.py:455
  184.5 148.6 %collective-permute-start.8 = (bf16[512,3200]{1,0:T(8,128)(2,1)}, bf16[512,3200]{1,0:T(8,128)(2,1)}, u32[]{:S(2)}, u32[]{:S(2)}) collective-permute-start(bf16[512,3200]{1,0:T(8,128)(2,1)} %pad_maximum_fusion.4), channel_id=1, source_target_pairs={{0,2},{2,6},{4,0},{6,4},{8,10},{10,14},{12,8},{14,12},{16,18},{18,... | collective-permute-start | bytes 9830408 | tf_op jit(solution)/shard_map/ppermute | solution.py:452
  204.5 88.0 %collective-permute-start.12 = (bf16[512,1024]{0,1:T(8,128)(2,1)}, bf16[512,1024]{0,1:T(8,128)(2,1)}, u32[]{:S(2)}, u32[]{:S(2)}) collective-permute-start(bf16[512,1024]{0,1:T(8,128)(2,1)} %pad_maximum_fusion.22), channel_id=1, source_target_pairs={{0,4},{2,0},{4,6},{6,2},{8,12},{10,8},{12,14},{14,10},{16,20},{18,... | collective-permute-start | bytes 3145736 | tf_op jit(solution)/shard_map/ppermute | solution.py:452
  205.9 301.6 %all-to-all-start.2 = ((bf16[32,10,2048]{2,1,0:T(8,128)(2,1)}), bf16[32,10,2048]{2,1,0:T(8,128)(2,1)}, u32[]{:S(2)}, u32[]{:S(2)}) async-start(bf16[32,10,2048]{2,1,0:T(8,128)(2,1)} %all_to_all.38), calls=%async_computation.2 | async-start | bytes 4194304 | tf_op jit(solution)/shard_map/all_to_all | solution.py:583
  223.3 75.0 %collective-permute-start.14 = (bf16[512,1024]{0,1:T(8,128)(2,1)}, bf16[512,1024]{0,1:T(8,128)(2,1)}, u32[]{:S(2)}, u32[]{:S(2)}) collective-permute-start(bf16[512,1024]{0,1:T(8,128)(2,1)} %pad_maximum_fusion.22), channel_id=1, source_target_pairs={{0,2},{2,6},{4,0},{6,4},{8,10},{10,14},{12,8},{14,12},{16,18},{18,... | collective-permute-start | bytes 3145736 | tf_op jit(solution)/shard_map/ppermute | solution.py:452
  328.5 134.6 %collective-permute-start.35 = (bf16[512,1408]{0,1:T(8,128)(2,1)}, bf16[512,1408]{0,1:T(8,128)(2,1)S(1)}, u32[]{:S(2)}, u32[]{:S(2)}) collective-permute-start(bf16[512,1408]{0,1:T(8,128)(2,1)} %pad_maximum_fusion.15), channel_id=1, source_target_pairs={{0,4},{2,0},{4,6},{6,2},{8,12},{10,8},{12,14},{14,10},{16,20},{18,... | collective-permute-start | bytes 4325384 | tf_op jit(solution)/shard_map/ppermute | solution.py:452
  339.2 128.9 %collective-permute-start.37 = (bf16[512,1408]{0,1:T(8,128)(2,1)}, bf16[512,1408]{0,1:T(8,128)(2,1)}, u32[]{:S(2)}, u32[]{:S(2)}) collective-permute-start(bf16[512,1408]{0,1:T(8,128)(2,1)} %pad_maximum_fusion.15), channel_id=1, source_target_pairs={{0,2},{2,6},{4,0},{6,4},{8,10},{10,14},{12,8},{14,12},{16,18},{18,... | collective-permute-start | bytes 4325384 | tf_op jit(solution)/shard_map/ppermute | solution.py:452
  342.2 135.2 %collective-permute-start.29 = (bf16[512,1408]{0,1:T(8,128)(2,1)}, bf16[512,1408]{0,1:T(8,128)(2,1)}, u32[]{:S(2)}, u32[]{:S(2)}) collective-permute-start(bf16[512,1408]{0,1:T(8,128)(2,1)} %pad_maximum_fusion.14), channel_id=1, source_target_pairs={{0,4},{2,0},{4,6},{6,2},{8,12},{10,8},{12,14},{14,10},{16,20},{18,... | collective-permute-start | bytes 4325384 | tf_op jit(solution)/shard_map/ppermute | solution.py:452
  398.3 81.3 %collective-permute-start.31 = (bf16[512,1408]{0,1:T(8,128)(2,1)}, bf16[512,1408]{0,1:T(8,128)(2,1)}, u32[]{:S(2)}, u32[]{:S(2)}) collective-permute-start(bf16[512,1408]{0,1:T(8,128)(2,1)} %pad_maximum_fusion.14), channel_id=1, source_target_pairs={{0,2},{2,6},{4,0},{6,4},{8,10},{10,14},{12,8},{14,12},{16,18},{18,... | collective-permute-start | bytes 4325384 | tf_op jit(solution)/shard_map/ppermute | solution.py:452
  400.3 83.2 %collective-permute-start.23 = (bf16[512,1408]{0,1:T(8,128)(2,1)}, bf16[512,1408]{0,1:T(8,128)(2,1)}, u32[]{:S(2)}, u32[]{:S(2)}) collective-permute-start(bf16[512,1408]{0,1:T(8,128)(2,1)} %pad_maximum_fusion.13), channel_id=1, source_target_pairs={{0,4},{2,0},{4,6},{6,2},{8,12},{10,8},{12,14},{14,10},{16,20},{18,... | collective-permute-start | bytes 4325384 | tf_op jit(solution)/shard_map/ppermute | solution.py:452
  639.1 120.7 %collective-permute-start.39 = (bf16[2,256,2048]{2,1,0:T(8,128)(2,1)}, bf16[2,256,2048]{2,1,0:T(8,128)(2,1)}, u32[]{:S(2)}, u32[]{:S(2)}) collective-permute-start(bf16[2,256,2048]{2,1,0:T(8,128)(2,1)} %fusion.26), channel_id=1, source_target_pairs={{0,1},{1,0},{2,3},{3,2},{4,5},{5,4},{6,7},{7,6},{8,9},{9,8},{10,11... | collective-permute-start | bytes 6291464 | tf_op jit(solution)/shard_map/ppermute | solution.py:461
  665.3 99.0 %collective-permute-start.44 = (bf16[2,256,2048]{2,1,0:T(8,128)(2,1)}, bf16[2,256,2048]{2,1,0:T(8,128)(2,1)}, u32[]{:S(2)}, u32[]{:S(2)}) collective-permute-start(bf16[2,256,2048]{2,1,0:T(8,128)(2,1)} %fusion.27), channel_id=1, source_target_pairs={{0,1},{1,0},{2,3},{3,2},{4,5},{5,4},{6,7},{7,6},{8,9},{9,8},{10,11... | collective-permute-start | bytes 6291464 | tf_op jit(solution)/shard_map/ppermute | solution.py:461
  764.3 82.8 %collective-permute-start.88 = (bf16[512,1408]{1,0:T(8,128)(2,1)}, bf16[512,1408]{1,0:T(8,128)(2,1)}, u32[]{:S(2)}, u32[]{:S(2)}) collective-permute-start(bf16[512,1408]{1,0:T(8,128)(2,1)} %pad_maximum_fusion.21), channel_id=1, source_target_pairs={{0,4},{2,0},{4,6},{6,2},{8,12},{10,8},{12,14},{14,10},{16,20},{18,... | collective-permute-start | bytes 4325384 | tf_op jit(solution)/shard_map/ppermute | solution.py:452
  788.5 137.9 %collective-permute-start.40 = (bf16[256,2048]{1,0:T(8,128)(2,1)S(1)}, bf16[256,2048]{1,0:T(8,128)(2,1)S(1)}, u32[]{:S(2)}, u32[]{:S(2)}) collective-permute-start(bf16[256,2048]{1,0:T(8,128)(2,1)S(1)} %fusion.62), channel_id=1, source_target_pairs={{0,8},{2,10},{4,12},{6,14},{8,0},{10,2},{12,4},{14,6},{16,24},{18,... | collective-permute-start | bytes 3145736 | tf_op jit(solution)/shard_map/ppermute | solution.py:455
  817.7 100.9 %collective-permute-start.45 = (bf16[256,2048]{1,0:T(8,128)(2,1)S(1)}, bf16[256,2048]{1,0:T(8,128)(2,1)S(1)}, u32[]{:S(2)}, u32[]{:S(2)}) collective-permute-start(bf16[256,2048]{1,0:T(8,128)(2,1)S(1)} %fusion.63), channel_id=1, source_target_pairs={{0,8},{2,10},{4,12},{6,14},{8,0},{10,2},{12,4},{14,6},{16,24},{18,... | collective-permute-start | bytes 3145736 | tf_op jit(solution)/shard_map/ppermute | solution.py:455
  857.6 116.3 %collective-permute-start.78 = (bf16[128,1408]{1,0:T(8,128)(2,1)S(1)}, bf16[128,1408]{1,0:T(8,128)(2,1)S(1)}, u32[]{:S(2)}, u32[]{:S(2)}) collective-permute-start(bf16[128,1408]{1,0:T(8,128)(2,1)S(1)} %dynamic-slice_convert_fusion.3), channel_id=1, source_target_pairs={{0,8},{2,10},{4,12},{6,14},{8,0},{10,2},{12,4},{14,6},{16,24},{18,... | collective-permute-start | bytes 1081352 | tf_op jit(solution)/shard_map/ppermute | solution.py:455
  903.9 70.1 %collective-permute-start.84 = (bf16[128,1408]{1,0:T(8,128)(2,1)}, bf16[128,1408]{1,0:T(8,128)(2,1)}, u32[]{:S(2)}, u32[]{:S(2)}) collective-permute-start(bf16[128,1408]{1,0:T(8,128)(2,1)} %dynamic-slice_convert_fusion.2), channel_id=1, source_target_pairs={{0,8},{2,10},{4,12},{6,14},{8,0},{10,2},{12,4},{14,6},{16,24},{18,... | collective-permute-start | bytes 1081352 | tf_op jit(solution)/shard_map/ppermute | solution.py:455
  938.4 221.5 %all-to-all-start.1 = ((bf16[32,10,2048]{2,1,0:T(8,128)(2,1)}), bf16[32,10,2048]{2,1,0:T(8,128)(2,1)}, u32[]{:S(2)}, u32[]{:S(2)}) async-start(bf16[32,10,2048]{2,1,0:T(8,128)(2,1)} %all_to_all.35), calls=%async_computation.1 | async-start | bytes 4194304 | tf_op jit(solution)/shard_map/all_to_all | solution.py:583
  1152.7 101.8 %collective-permute-start.64 = (bf16[512,3200]{1,0:T(8,128)(2,1)}, bf16[512,3200]{1,0:T(8,128)(2,1)}, u32[]{:S(2)}, u32[]{:S(2)}) collective-permute-start(bf16[512,3200]{1,0:T(8,128)(2,1)} %pad_maximum_fusion.6), channel_id=1, source_target_pairs={{0,4},{2,0},{4,6},{6,2},{8,12},{10,8},{12,14},{14,10},{16,20},{18,... | collective-permute-start | bytes 9830408 | tf_op jit(solution)/shard_map/ppermute | solution.py:452
  1156.4 98.1 %collective-permute-start.62 = (bf16[512,3200]{1,0:T(8,128)(2,1)}, bf16[512,3200]{1,0:T(8,128)(2,1)}, u32[]{:S(2)}, u32[]{:S(2)}) collective-permute-start(bf16[512,3200]{1,0:T(8,128)(2,1)} %pad_maximum_fusion.5), channel_id=1, source_target_pairs={{0,2},{2,6},{4,0},{6,4},{8,10},{10,14},{12,8},{14,12},{16,18},{18,... | collective-permute-start | bytes 9830408 | tf_op jit(solution)/shard_map/ppermute | solution.py:452
  1264.3 104.0 %collective-permute-start.65 = (bf16[256,3200]{1,0:T(8,128)(2,1)}, bf16[256,3200]{1,0:T(8,128)(2,1)}, u32[]{:S(2)}, u32[]{:S(2)}) collective-permute-start(bf16[256,3200]{1,0:T(8,128)(2,1)} %slice.757), channel_id=1, source_target_pairs={{0,16},{2,18},{4,20},{6,22},{8,24},{10,26},{12,28},{14,30},{16,0},... | collective-permute-start | bytes 4915208 | tf_op jit(solution)/shard_map/ppermute | solution.py:455
  1264.3 95.9 %collective-permute-start.54 = (f32[16,128]{1,0:T(8,128)S(1)}, f32[16,128]{1,0:T(8,128)S(1)}, u32[]{:S(2)}, u32[]{:S(2)}) collective-permute-start(f32[16,128]{1,0:T(8,128)S(1)} %add.634), channel_id=1, source_target_pairs={{0,16},{2,18},{4,20},{6,22},{8,24},{10,26},{12,28},{14,30},{16,0},... | collective-permute-start | bytes 24584 | tf_op jit(solution)/shard_map/ppermute | solution.py:455
  1267.3 95.9 %collective-permute-start.59 = (f32[280,128]{1,0:T(8,128)S(1)}, f32[280,128]{1,0:T(8,128)S(1)}, u32[]{:S(2)}, u32[]{:S(2)}) collective-permute-start(f32[280,128]{1,0:T(8,128)S(1)} %add.639), channel_id=1, source_target_pairs={{0,16},{2,18},{4,20},{6,22},{8,24},{10,26},{12,28},{14,30},{16,0},... | collective-permute-start | bytes 430088 | tf_op jit(solution)/shard_map/ppermute | solution.py:455
  1278.7 107.0 %all-to-all-start.3 = ((bf16[32,10,2048]{2,1,0:T(8,128)(2,1)}), bf16[32,10,2048]{2,1,0:T(8,128)(2,1)S(1)}, u32[]{:S(2)}, u32[]{:S(2)}) async-start(bf16[32,10,2048]{2,1,0:T(8,128)(2,1)} %all_to_all.41), calls=%async_computation.3 | async-start | bytes 4194304 | tf_op jit(solution)/shard_map/all_to_all | solution.py:583
  (179 other events, 5056.1 us)

commit v2 on v1

v2 whole, which is shorter than its diff:
```python
import functools

import jax
import jax.numpy as jnp
from jax import lax
from jax.experimental import pallas as pl
from jax.experimental.pallas import tpu as pltpu
from jax.sharding import PartitionSpec as P

bf = jnp.bfloat16
f32 = jnp.float32
DK = 128
DV = 256
CHUNK = 128
LANES = 128
GROUPS = 2
EPS_ROW = 1e-06
EPS_UNIT = 1e-06
EPS_HEAD = 1e-05
NEG = -1e30
VMEM_LIMIT = 56 * 2**20


def dot(left, right, left_dim, right_dim):
    return lax.dot_general(
        left.astype(bf), right.astype(bf), (((left_dim,), (right_dim,)), ((), ())), preferred_element_type=f32
    )


def nn(left, right):
    return dot(left, right, 1, 0)


def nt(left, right):
    return dot(left, right, 1, 1)


def tn(left, right):
    return dot(left, right, 0, 0)


def exact(left, right):
    return lax.dot_general(
        left, right, (((1,), (0,)), ((), ())), precision=lax.Precision.HIGHEST, preferred_element_type=f32
    )


def softplus(v):
    return jnp.maximum(v, 0.0) + jnp.log(1.0 + jnp.exp(-jnp.abs(v)))


def sigmoid(v):
    return 1.0 / (1.0 + jnp.exp(-v))


def unit_lower_inverses(systems, places, others):
    eye = (places == others).astype(f32)
    size = 16
    same = (places // size) == (others // size)
    power = [jnp.where(same, a, 0.0) for a in systems]
    inverse = [eye - a for a in power]
    span = 2
    while span < size:
        power = [nn(a, a) for a in power]
        inverse = [t + nn(t, a) for t, a in zip(inverse, power)]
        span *= 2
    while size < places.shape[0]:
        corner = ((places // (2 * size)) == (others // (2 * size))) & ((places // size) != (others // size))
        steps = [nn(jnp.where(corner, a, 0.0), t) for a, t in zip(systems, inverse)]
        inverse = [t - nn(t, s) for t, s in zip(inverse, steps)]
        size *= 2
    return inverse


def conv_channels(padded, group, taps, marks, columns):
    total = taps[0:1, columns] * padded[group, 8 : 8 + CHUNK, columns]
    for offset in range(1, 4):
        total = total + (taps[offset : offset + 1, columns] * marks[:, offset : offset + 1]) * (
            padded[group, 8 - offset : 8 - offset + CHUNK, columns]
        )
    return total


class Unit:
    def __init__(self, group, head, heads, first, lanes, shared):
        self.group = group
        self.head = head
        keys = heads * DK
        self.query_columns = slice(head * DK, head * DK + DK)
        self.key_columns = slice(keys + head * DK, keys + head * DK + DK)
        self.value_columns = slice(2 * keys + head * DV, 2 * keys + head * DV + DV)
        start = 2 * keys + heads * DV + head * DV
        self.gate_columns = slice(start, start + DV)
        self.out_columns = slice(head * DV, head * DV + DV)
        self.lane = first + head
        self.beta_lane = lanes + first + head
        cum, cum_rows, beta, causal, opening, closing = shared
        col = cum[:, self.lane : self.lane + 1]
        row = cum_rows[self.lane : self.lane + 1, :]
        self.decay = jnp.exp(jnp.where(causal, col - row, NEG))
        self.opened = jnp.exp(jnp.where(opening, col, NEG))
        last = cum[CHUNK - 1 : CHUNK, self.lane : self.lane + 1]
        self.closed = jnp.exp(jnp.where(closing, last - col, NEG))
        self.opened_last = self.opened[CHUNK - 1 : CHUNK, :]
        self.strength = beta[:, self.beta_lane : self.beta_lane + 1]


def chunk_units(heads, first, lanes, decays_ref, params, marks_ref, seg_ref, places, others):
    units, kept = [], []
    lower = (places >= others).astype(f32)
    for group in range(GROUPS):
        decays = decays_ref[0, group, 0]
        marks = marks_ref[group, 0]
        biased = decays + params[0:1, :]
        log_decay = -params[1:2, :] * softplus(biased)
        cum = exact(lower, log_decay)
        beta = sigmoid(decays)
        causal = (places >= others) & (marks[:, 0:1] == seg_ref[group, 0])
        shared = (cum, cum.T, beta, causal, marks[:, 4:5] > 0.0, marks[:, 5:6] > 0.0)
        kept.append((biased, log_decay, beta, marks))
        for head in range(heads):
            units.append(Unit(group, head, heads, first, lanes, shared))
    return units, kept


def forward_kernel(
    heads, first, lanes, core_ref, proj, decays, marks_ref, seg_ref, taps, params, gain, partner,
    out, kept_state, kept_inverse, state, padded,
):
    conv_width = heads * (2 * DK + DV)

    @pl.when(pl.program_id(0) == 0)
    def _():
        state[...] = jnp.zeros_like(state)
        padded[:, 0:8, :] = jnp.zeros((GROUPS, 8, conv_width), f32)

    for group in range(GROUPS):
        padded[group, 8:, :] = proj[0, group, 0, :, :conv_width].astype(f32)
    places = lax.broadcasted_iota(jnp.int32, (CHUNK, CHUNK), 0)
    others = lax.broadcasted_iota(jnp.int32, (CHUNK, CHUNK), 1)
    units, kept = chunk_units(heads, first, lanes, decays, params, marks_ref, seg_ref, places, others)
    strict = places > others
    queries, key_vecs, values = [], [], []
    for unit in units:
        marks = kept[unit.group][3]
        summed = conv_channels(padded, unit.group, taps, marks, unit.query_columns)
        act = summed * sigmoid(summed)
        scale = lax.rsqrt(jnp.sum(act * act, axis=1, keepdims=True) + EPS_UNIT)
        queries.append((act * (scale * DK**-0.5)).astype(bf))
        summed = conv_channels(padded, unit.group, taps, marks, unit.key_columns)
        act = summed * sigmoid(summed)
        scale = lax.rsqrt(jnp.sum(act * act, axis=1, keepdims=True) + EPS_UNIT)
        key_vecs.append((act * scale).astype(bf))
    pairs = [jnp.concatenate([q, k], axis=0) for q, k in zip(queries, key_vecs)]
    dots = [nt(pair, k) for pair, k in zip(pairs, key_vecs)]
    systems = [jnp.where(strict, unit.strength * unit.decay * d[CHUNK:], 0.0) for unit, d in zip(units, dots)]
    inverses = unit_lower_inverses(systems, places, others)
    for unit in units:
        summed = conv_channels(padded, unit.group, taps, kept[unit.group][3], unit.value_columns)
        values.append((summed * sigmoid(summed)).astype(bf).astype(f32))
    for group in range(GROUPS):
        padded[group, 0:8, :] = padded[group, CHUNK : CHUNK + 8, :]
    before = [state[number] for number in range(len(units))]
    for number in range(len(units)):
        kept_state[0, number] = before[number].astype(bf)
        kept_inverse[0, number] = inverses[number].astype(bf)
    reads = [nn(pair, s) for pair, s in zip(pairs, before)]
    rights = [unit.strength * (v - unit.opened * read[CHUNK:]) for unit, v, read in zip(units, values, reads)]
    news = [nn(t, r) for t, r in zip(inverses, rights)]
    mixed = [
        unit.opened * read[:CHUNK] + nn(d[:CHUNK] * unit.decay, new)
        for unit, read, d, new in zip(units, reads, dots, news)
    ]
    for number, unit in enumerate(units):
        state[number] = unit.opened_last * before[number] + tn(key_vecs[number], unit.closed * news[number])
    for unit, mix in zip(units, mixed):
        gate = proj[0, unit.group, 0, :, unit.gate_columns].astype(f32)
        scale = lax.rsqrt(jnp.mean(mix * mix, axis=1, keepdims=True) + EPS_HEAD)
        out[0, unit.group, 0, :, unit.out_columns] = (mix * scale * gain[...] * (gate * sigmoid(gate))).astype(bf)


def backward_kernel(
    heads, first, lanes, core_ref, proj, prev_rows, decays, grads, marks_ref, seg_ref, taps, params, gain,
    kept_state, kept_inverse, earlier, proj_grad, taps_grad, params_grad, gain_grad, state_grad, padded, summed_grad,
):
    conv_width = heads * (2 * DK + DV)
    width = conv_width + heads * DV

    @pl.when(pl.program_id(0) == 0)
    def _():
        taps_grad[...] = jnp.zeros_like(taps_grad)
        params_grad[...] = jnp.zeros_like(params_grad)
        gain_grad[...] = jnp.zeros_like(gain_grad)
        state_grad[...] = jnp.zeros_like(state_grad)
        summed_grad[:, CHUNK:, :] = jnp.zeros((GROUPS, 8, conv_width), f32)

    for group in range(GROUPS):
        padded[group, 0:8, :] = prev_rows[0, group, 0, :, :conv_width].astype(f32)[-8:]
        padded[group, 8:, :] = proj[0, group, 0, :, :conv_width].astype(f32)
    places = lax.broadcasted_iota(jnp.int32, (CHUNK, CHUNK), 0)
    others = lax.broadcasted_iota(jnp.int32, (CHUNK, CHUNK), 1)
    units, kept = chunk_units(heads, first, lanes, decays, params, marks_ref, seg_ref, places, others)
    strict = places > others
    q_sums, k_sums, v_sums, q_acts, k_acts, q_scale, k_scale = [], [], [], [], [], [], []
    queries, key_vecs, values = [], [], []
    for unit in units:
        marks = kept[unit.group][3]
        summed = conv_channels(padded, unit.group, taps, marks, unit.query_columns)
        act = summed * sigmoid(summed)
        scale = lax.rsqrt(jnp.sum(act * act, axis=1, keepdims=True) + EPS_UNIT)
        queries.append((act * (scale * DK**-0.5)).astype(bf))
        q_sums.append(summed)
        q_acts.append(act)
        q_scale.append(scale)
        summed = conv_channels(padded, unit.group, taps, marks, unit.key_columns)
        act = summed * sigmoid(summed)
        scale = lax.rsqrt(jnp.sum(act * act, axis=1, keepdims=True) + EPS_UNIT)
        key_vecs.append((act * scale).astype(bf))
        k_sums.append(summed)
        k_acts.append(act)
        k_scale.append(scale)
        summed = conv_channels(padded, unit.group, taps, marks, unit.value_columns)
        values.append((summed * sigmoid(summed)).astype(bf).astype(f32))
        v_sums.append(summed)
    count = len(units)
    pairs = [jnp.concatenate([q, k], axis=0) for q, k in zip(queries, key_vecs)]
    dots = [nt(pair, k) for pair, k in zip(pairs, key_vecs)]
    before = [kept_state[0, number] for number in range(count)]
    after_grad = [state_grad[number] for number in range(count)]
    inverses = [kept_inverse[0, number] for number in range(count)]
    reads = [nn(pair, s) for pair, s in zip(pairs, before)]
    gaps = [v - unit.opened * read[CHUNK:] for unit, v, read in zip(units, values, reads)]
    news = [nn(t, unit.strength * g) for t, unit, g in zip(inverses, units, gaps)]
    scores = [d[:CHUNK] * unit.decay for d, unit in zip(dots, units)]
    mixed = [unit.opened * read[:CHUNK] + nn(score, new) for unit, read, score, new in zip(units, reads, scores, news)]
    mix_grads = []
    gain_row = gain[...]
    gain_total = jnp.zeros((1, DV), f32)
    for unit, mix in zip(units, mixed):
        gate = proj[0, unit.group, 0, :, unit.gate_columns].astype(f32)
        grad = grads[0, unit.group, 0, :, unit.out_columns].astype(f32)
        scale = lax.rsqrt(jnp.mean(mix * mix, axis=1, keepdims=True) + EPS_HEAD)
        soft = sigmoid(gate)
        grad_normed = grad * (mix * scale)
        proj_grad[0, unit.group, 0, :, unit.gate_columns] = (
            grad_normed * gain_row * (soft * (1.0 + gate * (1.0 - soft)))
        ).astype(bf)
        silu = gate * soft
        gain_total = gain_total + jnp.sum(grad_normed * silu, axis=0, keepdims=True)
        inner = grad * silu * gain_row
        mix_grads.append(scale * inner - mix * (scale * scale * scale) * jnp.mean(inner * mix, axis=1, keepdims=True))
    gain_grad[0:1, :] += gain_total
    pushes = [nn(k, g) for k, g in zip(key_vecs, after_grad)]
    new_grads = [
        tn(score, grad) + unit.closed * push for score, grad, unit, push in zip(scores, mix_grads, units, pushes)
    ]
    score_grads = [nt(grad, new) for grad, new in zip(mix_grads, news)]
    right_grads = [tn(t, grad) for t, grad in zip(inverses, new_grads)]
    system_grads = [jnp.where(strict, -nt(grad, new), 0.0) for grad, new in zip(right_grads, news)]
    lane_ids = lax.broadcasted_iota(jnp.int32, (CHUNK, LANES), 1)
    rows_down = lax.broadcasted_iota(jnp.int32, (CHUNK, 1), 0)
    cum_grads = [jnp.zeros((CHUNK, LANES), f32) for _ in range(GROUPS)]
    beta_grads = [jnp.zeros((CHUNK, LANES), f32) for _ in range(GROUPS)]
    cross_rows = [[], []]
    raised = []
    for number, unit in enumerate(units):
        read_query = reads[number][:CHUNK]
        read_key = reads[number][CHUNK:]
        gram = dots[number][CHUNK:]
        decayed_score = score_grads[number] * unit.decay
        decayed_system = system_grads[number] * unit.decay
        system_gram = decayed_system * gram
        crossing = decayed_score * dots[number][:CHUNK] + unit.strength * system_gram
        value_grad = unit.strength * right_grads[number]
        beta_grad = jnp.sum(system_gram, axis=1, keepdims=True) + jnp.sum(
            right_grads[number] * gaps[number], axis=1, keepdims=True
        )
        open_grad = jnp.sum(mix_grads[number] * read_query - value_grad * read_key, axis=1, keepdims=True)
        close_grad = unit.closed * jnp.sum(news[number] * pushes[number], axis=1, keepdims=True)
        kept_dot = jnp.sum(
            jnp.sum(after_grad[number] * before[number].astype(f32), axis=1, keepdims=True), axis=0, keepdims=True
        )
        last_grad = jnp.sum(close_grad, axis=0, keepdims=True) + unit.opened_last * kept_dot
        col = jnp.sum(crossing, axis=1, keepdims=True) + unit.opened * open_grad - close_grad
        col = col + jnp.where(rows_down == CHUNK - 1, last_grad, 0.0)
        cross_rows[unit.group].append(jnp.sum(crossing, axis=0, keepdims=True))
        cum_grads[unit.group] = jnp.where(lane_ids == unit.lane, col, cum_grads[unit.group])
        beta_grads[unit.group] = jnp.where(lane_ids == unit.beta_lane, beta_grad, beta_grads[unit.group])
        raised.append((decayed_score.astype(bf), (unit.strength * decayed_system).astype(bf), value_grad))
    stacked = [
        jnp.concatenate([(unit.opened * grad).astype(bf), (-unit.opened * item[2]).astype(bf)], axis=0)
        for unit, item, grad in zip(units, raised, mix_grads)
    ]
    through = [nt(x, s) for x, s in zip(stacked, before)]
    grams = [jnp.concatenate([item[0], item[1]], axis=0) for item in raised]
    direct = [nn(g, k) for g, k in zip(grams, key_vecs)]
    turned = [tn(g, pair) for g, pair in zip(grams, pairs)]
    pushed = [nt(unit.closed * new, grad) for unit, new, grad in zip(units, news, after_grad)]
    for number, unit in enumerate(units):
        state_grad[number] = unit.opened_last * after_grad[number] + tn(pairs[number], stacked[number])
    for number, unit in enumerate(units):
        query_grad = (through[number][:CHUNK] + direct[number][:CHUNK]) * DK**-0.5
        key_grad = through[number][CHUNK:] + direct[number][CHUNK:] + turned[number] + pushed[number]
        for grad, act, scale, summed, columns in (
            (query_grad, q_acts[number], q_scale[number], q_sums[number], unit.query_columns),
            (key_grad, k_acts[number], k_scale[number], k_sums[number], unit.key_columns),
        ):
            inner = scale * (grad - act * (scale * scale) * jnp.sum(grad * act, axis=1, keepdims=True))
            soft = sigmoid(summed)
            summed_grad[unit.group, 0:CHUNK, columns] = inner * (soft * (1.0 + summed * (1.0 - soft)))
        summed = v_sums[number]
        soft = sigmoid(summed)
        summed_grad[unit.group, 0:CHUNK, unit.value_columns] = raised[number][2] * (
            soft * (1.0 + summed * (1.0 - soft))
        )
    for group in range(GROUPS):
        marks = kept[group][3]
        for start in range(0, conv_width, LANES):
            columns = slice(start, start + LANES)
            grad = summed_grad[group, 0:CHUNK, columns]
            total = taps[0:1, columns] * grad
            taps_grad[0:1, columns] += jnp.sum(grad * padded[group, 8 : 8 + CHUNK, columns], axis=0, keepdims=True)
            for offset in range(1, 4):
                later = summed_grad[group, offset : offset + CHUNK, columns]
                total = total + (taps[offset : offset + 1, columns] * marks[:, 5 + offset : 6 + offset]) * later
                taps_grad[offset : offset + 1, columns] += jnp.sum(
                    (grad * marks[:, offset : offset + 1]) * padded[group, 8 - offset : 8 - offset + CHUNK, columns],
                    axis=0, keepdims=True,
                )
            proj_grad[0, group, 0, :, columns] = total.astype(bf)
        summed_grad[group, CHUNK:, :] = summed_grad[group, 0:8, :]
    upper = (places <= others).astype(f32)
    for group in range(GROUPS):
        biased, log_decay, beta, _ = kept[group]
        blank = [jnp.zeros((first, CHUNK), f32)] if first else []
        rest = [jnp.zeros((CHUNK - heads - first, CHUNK), f32)]
        cross = jnp.concatenate(blank + cross_rows[group] + rest, axis=0).T
        log_grad = exact(upper, cum_grads[group] - cross)
        decay_grad = log_grad * (-params[1:2, :]) * sigmoid(biased)
        both = decay_grad + beta_grads[group] * beta * (1.0 - beta)
        if earlier is not None:
            both = both + earlier[0, group, 0].astype(f32)
        proj_grad[0, group, 0, :, width:] = both.astype(bf)
        params_grad[0:1, :] += jnp.sum(log_grad * log_decay, axis=0, keepdims=True)
        params_grad[1:2, :] += jnp.sum(decay_grad, axis=0, keepdims=True)


def folded(rows):
    return rows.reshape(2, GROUPS, -1, CHUNK, rows.shape[1])


def mixer_forward(first, lanes, core, proj, decays, marks, seg_rows, taps, params, gain, partner):
    conv_width = taps.shape[1]
    heads = conv_width // (2 * DK + DV)
    proj, decays = folded(proj), folded(decays)
    per_core = proj.shape[2]
    chunks = 2 * per_core
    units = GROUPS * heads

    def at(c, core_ref):
        return ((c // per_core) ^ core_ref[0], 0, c % per_core, 0, 0)

    fixed = lambda c, core_ref: (0, 0)
    here = lambda c, core_ref: (0, c, 0, 0)
    kept = lambda c, core_ref: (c, 0, 0, 0)
    full = proj.shape[:4] + (lanes * DV,)
    body = functools.partial(forward_kernel, heads, first, lanes)
    more_specs, more, aliases = [], [], {}
    if partner is None:
        inner = body

        def body(*refs):
            return inner(*refs[:8], None, *refs[8:])

    else:
        more_specs, more, aliases = [pl.BlockSpec(memory_space=pl.ANY)], [partner.reshape(full)], {8: 0}

    def out_at(c, core_ref):
        return at(c, core_ref)[:4] + (first // heads,)

    out, states, inverses = pl.pallas_call(
        body,
        grid_spec=pltpu.PrefetchScalarGridSpec(
            num_scalar_prefetch=1,
            grid=(chunks,),
            in_specs=[
                pl.BlockSpec((1, GROUPS, 1, CHUNK, proj.shape[4]), at),
                pl.BlockSpec((1, GROUPS, 1, CHUNK, LANES), at),
                pl.BlockSpec((GROUPS, 1, CHUNK, LANES), here),
                pl.BlockSpec((GROUPS, 1, 1, CHUNK), here),
                pl.BlockSpec((4, conv_width), fixed),
                pl.BlockSpec((8, LANES), fixed),
                pl.BlockSpec((1, DV), fixed),
            ]
            + more_specs,
            out_specs=[
                pl.BlockSpec((1, GROUPS, 1, CHUNK, heads * DV), out_at),
                pl.BlockSpec((1, units, DK, DV), kept),
                pl.BlockSpec((1, units, CHUNK, CHUNK), kept),
            ],
            scratch_shapes=[pltpu.VMEM((units, DK, DV), f32), pltpu.VMEM((GROUPS, CHUNK + 8, conv_width), f32)],
        ),
        out_shape=[
            jax.ShapeDtypeStruct(full, bf),
            jax.ShapeDtypeStruct((chunks, units, DK, DV), bf),
            jax.ShapeDtypeStruct((chunks, units, CHUNK, CHUNK), bf),
        ],
        compiler_params=pltpu.CompilerParams(vmem_limit_bytes=VMEM_LIMIT),
        cost_estimate=pl.CostEstimate(flops=16 * 10**9, bytes_accessed=16 * 2**20, transcendentals=0),
        input_output_aliases=aliases,
        name="mixer_forward",
    )(core, proj, decays, marks, seg_rows, taps, params, gain, *more)
    return out.reshape(-1, lanes * DV), states, inverses


def mixer_backward(first, lanes, core, proj, decays, grads, marks, seg_rows, taps, params, gain, states, inverses, earlier):
    conv_width = taps.shape[1]
    heads = conv_width // (2 * DK + DV)
    proj, decays, grads = folded(proj), folded(decays), folded(grads)
    per_core = proj.shape[2]
    chunks = 2 * per_core
    units = GROUPS * heads
    width = conv_width + heads * DV + LANES
    tail = 16

    def at(step, core_ref):
        c = chunks - 1 - step
        return ((c // per_core) ^ core_ref[0], 0, c % per_core, 0, 0)

    def prev(step, core_ref):
        c = jnp.maximum(chunks - 2 - step, 0)
        return ((c // per_core) ^ core_ref[0], 0, c % per_core, CHUNK // tail - 1, 0)

    def grad_at(step, core_ref):
        return at(step, core_ref)[:4] + (first // heads,)

    def last_lanes(step, core_ref):
        return at(step, core_ref)[:4] + ((conv_width + heads * DV) // LANES,)

    fixed = lambda step, core_ref: (0, 0)
    here = lambda step, core_ref: (0, chunks - 1 - step, 0, 0)
    kept = lambda step, core_ref: (chunks - 1 - step, 0, 0, 0)
    in_specs = [
        pl.BlockSpec((1, GROUPS, 1, CHUNK, proj.shape[4]), at),
        pl.BlockSpec((1, GROUPS, 1, tail, proj.shape[4]), prev),
        pl.BlockSpec((1, GROUPS, 1, CHUNK, LANES), at),
        pl.BlockSpec((1, GROUPS, 1, CHUNK, heads * DV), grad_at),
        pl.BlockSpec((GROUPS, 1, CHUNK, LANES), here),
        pl.BlockSpec((GROUPS, 1, 1, CHUNK), here),
        pl.BlockSpec((4, conv_width), fixed),
        pl.BlockSpec((8, LANES), fixed),
        pl.BlockSpec((1, DV), fixed),
        pl.BlockSpec((1, units, DK, DV), kept),
        pl.BlockSpec((1, units, CHUNK, CHUNK), kept),
    ]
    inputs = [core, proj, proj, decays, grads, marks, seg_rows, taps, params, gain, states, inverses]
    body = functools.partial(backward_kernel, heads, first, lanes)
    if earlier is not None:
        in_specs.append(pl.BlockSpec((1, GROUPS, 1, CHUNK, LANES), last_lanes))
        inputs.append(folded(earlier))
    else:
        whole = body

        def body(*refs):
            return whole(*refs[:12], None, *refs[12:])

    out, taps_grad, params_grad, gain_grad = pl.pallas_call(
        body,
        grid_spec=pltpu.PrefetchScalarGridSpec(
            num_scalar_prefetch=1,
            grid=(chunks,),
            in_specs=in_specs,
            out_specs=[
                pl.BlockSpec((1, GROUPS, 1, CHUNK, width), at),
                pl.BlockSpec((4, conv_width), fixed),
                pl.BlockSpec((8, LANES), fixed),
                pl.BlockSpec((8, DV), fixed),
            ],
            scratch_shapes=[
                pltpu.VMEM((units, DK, DV), f32),
                pltpu.VMEM((GROUPS, CHUNK + 8, conv_width), f32),
                pltpu.VMEM((GROUPS, CHUNK + 8, conv_width), f32),
            ],
        ),
        out_shape=[
            jax.ShapeDtypeStruct(proj.shape[:4] + (width,), bf),
            jax.ShapeDtypeStruct((4, conv_width), f32),
            jax.ShapeDtypeStruct((8, LANES), f32),
            jax.ShapeDtypeStruct((8, DV), f32),
        ],
        compiler_params=pltpu.CompilerParams(vmem_limit_bytes=VMEM_LIMIT),
        cost_estimate=pl.CostEstimate(flops=30 * 10**9, bytes_accessed=30 * 2**20, transcendentals=0),
        name="mixer_backward",
    )(*inputs)
    return out.reshape(-1, width), taps_grad, params_grad, gain_grad


def group_marks(lengths, group_rows):
    groups, count = lengths.shape
    position = jnp.arange(group_rows, dtype=jnp.int32)[None, :]
    segment = jnp.zeros((groups, group_rows), jnp.int32)
    end = jnp.zeros((groups, 1), jnp.int32)
    for number in range(count):
        segment = segment + (position >= end).astype(jnp.int32)
        end = end + lengths[:, number : number + 1]
    live = (position < end).astype(f32)
    padded = jnp.pad(segment, ((0, 0), (CHUNK, CHUNK)))
    later = lambda offset: padded[:, CHUNK + offset : CHUNK + offset + group_rows]
    chunked = segment.reshape(groups, group_rows // CHUNK, CHUNK)
    before = padded[:, CHUNK - 1 : CHUNK - 1 + group_rows].reshape(chunked.shape)[:, :, :1]
    columns = [segment]
    columns += [later(-offset) == segment for offset in (1, 2, 3)]
    columns += [(chunked == before).reshape(segment.shape), (chunked == chunked[:, :, -1:]).reshape(segment.shape)]
    columns += [later(offset) == segment for offset in (1, 2, 3)]
    lane = jnp.arange(LANES, dtype=jnp.int32)
    marks = jnp.zeros((groups, group_rows, LANES), f32)
    for number, column in enumerate(columns):
        marks = jnp.where(lane == number, column.astype(f32)[:, :, None], marks)
    marks = marks.reshape(groups, group_rows // CHUNK, CHUNK, LANES)
    seg_rows = segment.astype(f32).reshape(groups, group_rows // CHUNK, 1, CHUNK)
    return marks, seg_rows, live


def pick_kernel(pairs, turn_ref, *refs):
    count = len(refs) - len(pairs)
    for out, parts in zip(refs[count:], pairs):
        begin = 0
        for number, start, stop in parts:
            out[:, begin : begin + stop - start] = refs[number][:, start:stop]
            begin += stop - start


def picked(turn, weights, axes, joins):
    in_specs, inputs, shapes = [], [], []
    for weight, axis in zip(weights, axes):
        rows, columns = weight.shape
        if axis is None:
            in_specs += [pl.BlockSpec((rows, columns), lambda i, t: (0, 0))] * 2
            shapes.append((rows, columns))
        elif axis == 1:
            in_specs += [
                pl.BlockSpec((rows, columns // 2), lambda i, t: (0, t[0])),
                pl.BlockSpec((rows, columns // 2), lambda i, t: (0, 1 - t[0])),
            ]
            shapes.append((rows, columns // 2))
        else:
            in_specs += [
                pl.BlockSpec((rows // 2, columns), lambda i, t: (t[0], 0)),
                pl.BlockSpec((rows // 2, columns), lambda i, t: (1 - t[0], 0)),
            ]
            shapes.append((rows // 2, columns))
        inputs += [weight, weight]
    pairs, out_shapes = [], []
    for join in joins:
        width = sum(stop - start for _, start, stop in join)
        for given in (0, 1):
            pairs.append([(2 * number + given, start, stop) for number, start, stop in join])
            out_shapes.append((shapes[join[0][0]][0], width))
    outs = pl.pallas_call(
        functools.partial(pick_kernel, pairs),
        grid_spec=pltpu.PrefetchScalarGridSpec(
            num_scalar_prefetch=1,
            grid=(1,),
            in_specs=in_specs,
            out_specs=[pl.BlockSpec(shape, lambda i, t: (0, 0)) for shape in out_shapes],
        ),
        out_shape=[jax.ShapeDtypeStruct(shape, bf) for shape in out_shapes],
        compiler_params=pltpu.CompilerParams(vmem_limit_bytes=VMEM_LIMIT),
        cost_estimate=pl.CostEstimate(flops=0, bytes_accessed=8 * 2**20, transcendentals=0),
        name="picked",
    )(turn, *inputs)
    return [(outs[2 * number], outs[2 * number + 1]) for number in range(len(joins))]


TILE = 256
STRIP = 256


def call(body, grid, in_specs, out_specs, out_shape, flops, moved, name, inputs):
    return pl.pallas_call(
        body,
        grid=grid,
        in_specs=in_specs,
        out_specs=out_specs,
        out_shape=out_shape,
        compiler_params=pltpu.CompilerParams(vmem_limit_bytes=VMEM_LIMIT),
        cost_estimate=pl.CostEstimate(flops=flops, bytes_accessed=moved, transcendentals=0),
        name=name,
    )(*inputs)


def strip_sum(rows, pieces, start, product):
    total = None
    begin = 0
    depth = rows.shape[1] // len(pieces)
    for piece in pieces:
        part = product(rows[start : start + STRIP, begin : begin + depth], piece[...])
        total = part if total is None else total + part
        begin += depth
    return total


def whole(array):
    return pl.BlockSpec(array.shape, lambda i: (0,) * array.ndim)


def project(rows, pieces, width, extra):
    count = rows.shape[0]
    depth = pieces[0].shape[0]
    steps = width // TILE
    used = len(pieces)

    def body(rows_ref, *refs):
        weights = refs[:used]
        out = refs[2 * used if extra else used]
        for start in range(0, count, STRIP):
            out[start : start + STRIP, :] = strip_sum(rows_ref, weights, start, nn).astype(bf)
        if extra:

            @pl.when(pl.program_id(0) == 0)
            def _():
                for start in range(0, count, STRIP):
                    refs[-1][start : start + STRIP, :] = strip_sum(rows_ref, refs[used : 2 * used], start, nn)

    in_specs = [whole(rows)] + [pl.BlockSpec((depth, TILE), lambda i: (0, i))] * used
    out_specs = [pl.BlockSpec((count, TILE), lambda i: (0, i))]
    out_shape = [jax.ShapeDtypeStruct((count, width), bf)]
    inputs = [rows, *pieces]
    if extra:
        in_specs += [pl.BlockSpec((depth, LANES), lambda i: (0, width // LANES))] * used
        out_specs.append(pl.BlockSpec((count, LANES), lambda i: (0, 0)))
        out_shape.append(jax.ShapeDtypeStruct((count, LANES), f32))
        inputs += pieces
    flops = 2 * count * depth * used * width
    moved = 2 * (count * depth * used + depth * used * width + count * width)
    return call(body, (steps,), in_specs, out_specs, out_shape, flops, moved, "project", inputs)


def feed_forward(rows, gate_pieces, up_pieces):
    count = rows.shape[0]
    depth, width = gate_pieces[0].shape
    used = len(gate_pieces)

    def body(rows_ref, *refs):
        gate_out, up_out, hidden_out = refs[2 * used :]
        for start in range(0, count, STRIP):
            strip = slice(start, start + STRIP)
            gate = strip_sum(rows_ref, refs[:used], start, nn)
            up = strip_sum(rows_ref, refs[used : 2 * used], start, nn)
            gate_out[strip, :] = gate.astype(bf)
            up_out[strip, :] = up.astype(bf)
            hidden_out[strip, :] = (gate * sigmoid(gate) * up).astype(bf)

    out_spec = pl.BlockSpec((count, TILE), lambda i: (0, i))
    return call(
        body,
        (pl.cdiv(width, TILE),),
        [whole(rows)] + [pl.BlockSpec((depth, TILE), lambda i: (0, i))] * (2 * used),
        [out_spec] * 3,
        [jax.ShapeDtypeStruct((count, width), bf)] * 3,
        4 * count * depth * used * width,
        2 * (count * depth * used + 2 * depth * used * width + 3 * count * width),
        "feed_forward",
        [rows, *gate_pieces, *up_pieces],
    )


def feed_backward(rows, down_pieces, gate_pre, up_proj):
    count = rows.shape[0]
    width, depth = down_pieces[0].shape
    used = len(down_pieces)

    def body(rows_ref, *refs):
        gate_ref, up_ref, gate_out, up_out = refs[used:]
        for start in range(0, count, STRIP):
            strip = slice(start, start + STRIP)
            grad = strip_sum(rows_ref, refs[:used], start, nt)
            gate = gate_ref[strip, :].astype(f32)
            soft = sigmoid(gate)
            gate_out[strip, :] = (grad * up_ref[strip, :].astype(f32) * soft * (1.0 + gate * (1.0 - soft))).astype(bf)
            up_out[strip, :] = (grad * gate * soft).astype(bf)

    tile = pl.BlockSpec((count, TILE), lambda i: (0, i))
    return call(
        body,
        (pl.cdiv(width, TILE),),
        [whole(rows)] + [pl.BlockSpec((TILE, depth), lambda i: (i, 0))] * used + [tile] * 2,
        [tile] * 2,
        [jax.ShapeDtypeStruct((count, width), bf)] * 2,
        2 * count * depth * used * width,
        2 * (count * depth * used + depth * used * width + 4 * count * width),
        "feed_backward",
        [rows, *down_pieces, gate_pre, up_proj],
    )


def heads_backward(rows, out_pieces):
    count = rows.shape[0]
    width, depth = out_pieces[0].shape
    used = len(out_pieces)

    def body(rows_ref, *refs):
        for start in range(0, count, STRIP):
            refs[used][start : start + STRIP, :] = strip_sum(rows_ref, refs[:used], start, nt).astype(bf)

    return call(
        body,
        (width // TILE,),
        [whole(rows)] + [pl.BlockSpec((TILE, depth), lambda i: (i, 0))] * used,
        pl.BlockSpec((count, TILE), lambda i: (0, i)),
        jax.ShapeDtypeStruct((count, width), bf),
        2 * count * depth * used * width,
        2 * (count * depth * used + depth * used * width + count * width),
        "heads_backward",
        [rows, *out_pieces],
    )


def widen(terms, refs, product):
    outs = []
    for piece in range(4):
        total = None
        for number, begin, weight, first, columns in terms:
            left = refs[number][:, begin : begin + columns]
            right = refs[weight + piece]
            right = right[:, first : first + columns] if product is nt else right[...]
            part = product(left, right)
            total = part if total is None else total + part
        outs.append(total)
    return outs


def wide(terms, lefts, pieces, product, features, got):
    count = lefts[0].shape[0]
    per = count // 4
    given = got is None
    here = (lambda i: (i + 2, 0)) if given else (lambda i: (1 - i, 0))
    inputs = list(lefts) + [piece for group in pieces for piece in group]
    in_specs = [pl.BlockSpec((per, left.shape[1]), here) for left in lefts]
    in_specs += [whole(piece) for group in pieces for piece in group]
    flops = 2 * (count // 2) * features * sum(term[4] for term in terms)
    moved = 2 * sum(piece.size for group in pieces for piece in group) + 6 * count * features
    depth = features // 4
    if given:

        def body(*refs):
            for piece, total in enumerate(widen(terms, refs, product)):
                refs[-1][:, piece * depth : piece * depth + depth] = total.astype(bf)

        return call(
            body, (2,), in_specs, pl.BlockSpec((per, features), lambda i: (i, 0)),
            jax.ShapeDtypeStruct((count // 2, features), bf), flops, moved, "wide_given", inputs,
        )

    def body(*refs):
        got_ref, there, own = refs[-3:]
        totals = widen(terms, refs, product)
        for piece, total in enumerate(totals):
            columns = slice(piece * depth, piece * depth + depth)
            total = total + got_ref[:, columns].astype(f32)

            @pl.when(pl.program_id(0) == 0)
            def _():
                there[:, columns] = total.astype(bf)

            @pl.when(pl.program_id(0) == 1)
            def _():
                own[:, columns] = total

    return call(
        body, (2,), in_specs + [pl.BlockSpec((per, features), here)],
        [pl.BlockSpec((per, features), lambda i: (0, 0))] * 2,
        [jax.ShapeDtypeStruct((per, features), bf), jax.ShapeDtypeStruct((per, features), f32)],
        flops, moved, "wide_kept", inputs + [got],
    )


RING = (0, 1, 3, 2)


def matmul(left, right):
    return jnp.dot(left, right, preferred_element_type=f32)


def outer_sum(left, right):
    return lax.dot_general(left, right, (((0,), (0,)), ((), ())), preferred_element_type=f32)


def times_back(left, right):
    return lax.dot_general(left, right, (((1,), (1,)), ((), ())), preferred_element_type=f32)


def norm_back(inputs, scale, gain, grad_out):
    scaled = grad_out * gain
    grad_in = scale * scaled - inputs * scale**3 * jnp.mean(scaled * inputs, axis=1, keepdims=True)
    return (grad_in, jnp.sum(grad_out * inputs * scale, axis=0))


class Layout:
    def __init__(self):
        self.ways = lax.axis_size("dp")
        self.spans = self.ways // 8
        dp = lax.axis_index("dp")
        self.core = lax.axis_index("tensor")
        self.turn = (dp // 4) % 2
        self.far = dp // 8
        near = dp % 4
        self.spot = near ^ (near >> 1)
        self.queues = {}

    def queued(self, values, queue, depth):
        line = self.queues.setdefault(queue, [])
        if len(line) >= depth:
            values, _ = lax.optimization_barrier((values, line[-depth]))
        return values, line

    def ring(self, values, step):
        pairs = []
        for number in range(self.ways):
            near = number % 4
            pairs.append((number, number - near + RING[((near ^ (near >> 1)) + step) % 4]))
        values, line = self.queued(values, step, DEPTH)
        line.append(lax.ppermute(values, "dp", pairs))
        return line[-1]

    def flip(self, values, bit):
        return lax.ppermute(values, "dp", [(n, n ^ bit) for n in range(self.ways)])

    def turned(self, values):
        return self.flip(values, 4)

    def crossed(self, values):
        return lax.ppermute(values, "tensor", [(0, 1), (1, 0)])

    def far_bits(self):
        bit = 8
        while bit < self.ways:
            yield bit
            bit *= 2

    def sources(self):
        places = jnp.arange(self.ways, dtype=jnp.int32)
        step = places // (2 * self.spans)
        jump = (places // 2) % self.spans
        spot = (self.spot + step) % 4
        return ((self.far ^ jump) * 2 + places % 2) * 4 + (spot ^ (spot >> 1))

    def ordered(self, first, second, axis):
        return jnp.where(
            self.turn == 0, jnp.concatenate([first, second], axis=axis), jnp.concatenate([second, first], axis=axis)
        )

    def spread(self, blob, axis, upward):
        keep, give = blob
        give, line = self.queued(give, "turn", DEPTH)
        line.append(self.turned(give))
        chunk = self.ordered(keep, line[-1], axis)
        for bit in self.far_bits():
            sent, line = self.queued(chunk, "far", DEPTH)
            line.append(self.flip(sent, bit))
            chunk = jnp.concatenate([chunk, line[-1]], axis=axis)
        ahead = self.ring(chunk, -1)
        behind = self.ring(chunk, 1)
        across = self.ring(behind, 1) if upward else self.ring(ahead, -1)
        return [chunk, ahead, across, behind]

    def collect_ring(self, make, upward):
        if upward:
            up = self.ring(make(2).astype(bf), 1)
            down = self.ring(make(3).astype(bf), -1)
            up = self.ring((make(1) + up).astype(bf), 1)
        else:
            down = self.ring(make(2).astype(bf), -1)
            up = self.ring(make(1).astype(bf), 1)
            down = self.ring((make(3) + down).astype(bf), -1)
        return make(0) + up + down

    def collect_rest(self, own, axis):
        for bit in reversed(list(self.far_bits())):
            half = own.shape[axis] // 2
            sent = lax.slice_in_dim(own, half, 2 * half, axis=axis)
            own = lax.slice_in_dim(own, 0, half, axis=axis) + self.flip(sent.astype(bf), bit)
        half = own.shape[axis] // 2
        mine = lax.dynamic_slice_in_dim(own, self.turn * half, half, axis)
        other = lax.dynamic_slice_in_dim(own, (1 - self.turn) * half, half, axis)
        return mine, self.turned(other.astype(bf)).astype(f32)

    def joined(self, mine, theirs, axis):
        return self.ordered(jnp.concatenate(mine, axis=axis), jnp.concatenate(theirs, axis=axis), axis)

    def rows_of(self, own):
        across = self.crossed(own)
        there = self.turned(own)
        return jnp.concatenate([own, there, across, self.crossed(there)], axis=0)

    def own_of(self, terms, lefts, pieces, product, features):
        given = wide(terms, lefts, pieces, product, features, None)
        there, own = wide(terms, lefts, pieces, product, features, self.crossed(given))
        return own + self.turned(there)

    def everywhere(self, values):
        bit = 1
        while bit < self.ways:
            values = values + self.flip(values, bit)
            bit *= 2
        return values + self.crossed(values)


DEPTH = 1


def flat(parts):
    joined = jnp.concatenate([part.reshape(-1) for part in parts])
    return jnp.pad(joined, (0, -joined.shape[0] % (8 * LANES))).reshape(-1, LANES)


def shards(
    tokens, cotangent, lengths, slot_of, norm_gains, w_query, w_key, w_value, w_gate, w_decay, w_beta,
    conv_weights, a_log, dt_bias, out_gain, w_out, w_mlp_gate, w_mlp_up, w_mlp_down,
):
    lay = Layout()
    row_count, features = tokens.shape
    tensor_ways = lax.axis_size("tensor")
    device_count = lay.ways * tensor_ways
    group_rows = row_count * tensor_ways
    capacity = row_count // device_count + 2
    bulk_rows = device_count * capacity
    all_heads = a_log.shape[0]
    heads = all_heads // (2 * tensor_ways)
    pair = heads // 2
    all_keys = all_heads * DK
    keys, vals = pair * DK, pair * DV
    width = 2 * keys + 2 * vals
    share = lay.core * 2 + lay.turn
    turn = lay.turn.reshape(1)
    core = lay.core.reshape(1)

    target = slot_of // row_count
    within = slot_of % row_count
    hits = target[:, None] == jnp.arange(device_count, dtype=jnp.int32)[None, :]
    places = jnp.arange(row_count, dtype=jnp.int32)
    earlier = (places[:, None] >= places[None, :]).astype(bf)
    rank = jnp.sum(matmul(earlier, hits.astype(bf)) * hits.astype(f32), axis=1).astype(jnp.int32) - 1
    outgoing = target * capacity + rank
    sending = (jnp.arange(bulk_rows, dtype=jnp.int32)[:, None] == outgoing[None, :]).astype(bf)
    slot_mark = jnp.broadcast_to((within + 1).astype(bf)[:, None], (row_count, LANES))
    send_tokens = matmul(sending, jnp.concatenate([tokens, slot_mark], axis=1)).astype(bf)
    send_cot = matmul(sending, cotangent).astype(bf)

    def exchange(values):
        return lax.all_to_all(values, ("dp", "tensor"), split_axis=0, concat_axis=0, tiled=True)


    def half_heads(weight):
        kept = jnp.where(lay.turn == 0, weight[:, :heads], weight[:, heads:])
        given = jnp.where(lay.turn == 0, weight[:, heads:], weight[:, :heads])
        return kept, given

    decay_halves, beta_halves = half_heads(w_decay), half_heads(w_beta)
    lanes_of = [
        jnp.pad(jnp.concatenate([d, b], axis=1), ((0, 0), (0, LANES - 2 * heads)))
        for d, b in zip(decay_halves, beta_halves)
    ]
    first_join = [(0, 0, keys), (1, 0, keys), (2, 0, vals), (3, 0, vals)]
    second_join = [(0, keys, 2 * keys), (1, keys, 2 * keys), (2, vals, 2 * vals), (3, vals, 2 * vals)]
    blob_first, blob_second = picked(
        turn, [w_query, w_key, w_value, w_gate], [1] * 4, [first_join, second_join]
    )
    blob_first = tuple(jnp.concatenate([blob, extra], axis=1) for blob, extra in zip(blob_first, lanes_of))
    out_rows, hidden_here = w_out.shape[0] // 2, w_mlp_gate.shape[1] // 2
    block = features // lay.ways
    blob_out, blob_gate, blob_up, blob_down = picked(
        turn, [w_out, w_mlp_gate, w_mlp_up, w_mlp_down], [0, 1, 1, 0],
        [[(0, 0, block)], [(1, 0, hidden_here)], [(2, 0, hidden_here)], [(3, 0, block)]],
    )
    got_tokens = exchange(send_tokens)
    in_first = lay.spread(blob_first, 0, True)
    in_second = lay.spread(blob_second, 0, False)
    out_pieces = lay.spread(blob_out, 1, True)
    gate_pieces = lay.spread(blob_gate, 0, False)
    up_pieces = lay.spread(blob_up, 0, True)
    down_pieces = lay.spread(blob_down, 1, False)

    got_slot = got_tokens[:, features].astype(jnp.int32)
    landing = (places[:, None] + 1 == got_slot[None, :]).astype(bf)
    sources = lay.sources()
    feature = jnp.arange(features, dtype=jnp.int32)
    origin = (sources[:, None] * block + jnp.arange(block, dtype=jnp.int32)[None, :]).reshape(1, -1)
    turning = (feature[:, None] == origin).astype(bf)
    numbers = jnp.arange(lay.ways, dtype=jnp.int32)
    picking = (sources[:, None] == numbers[None, :]).astype(f32)

    def reordered_gain(gain):
        return jnp.sum(picking[:, :, None] * gain.reshape(1, lay.ways, block), axis=1).reshape(features)

    def straight_gain(grad):
        return jnp.sum(picking[:, :, None] * grad.reshape(lay.ways, 1, block), axis=0).reshape(features)

    gains = (reordered_gain(norm_gains[0]), reordered_gain(norm_gains[1]))
    x_own = matmul(matmul(landing, got_tokens[:, :features]).astype(bf), turning)

    pair_lengths = jnp.concatenate([lengths, lay.turned(lengths)], axis=0)
    marks, seg_rows, live = group_marks(pair_lengths, group_rows)
    live_own = lax.dynamic_slice_in_dim(live[0], lay.core * row_count, row_count)[:, None]
    starts = [(share * heads + first) * DK for first in (0, pair)]
    cuts = [
        [(start, keys), (all_keys + start, keys), (2 * all_keys + 2 * start, vals)] for start in starts
    ]
    taps = [
        jnp.concatenate([lax.dynamic_slice_in_dim(conv_weights, start, size, 1) for start, size in cut], axis=1)
        for cut in cuts
    ]
    log_here = lax.dynamic_slice_in_dim(a_log, share * heads, heads)
    bias_here = lax.dynamic_slice_in_dim(dt_bias, share * heads, heads)
    params = jnp.pad(jnp.stack([bias_here, jnp.exp(log_here)]), ((0, 6), (0, LANES - heads)))
    gain_row = out_gain[None, :]

    scale_one = lax.rsqrt(jnp.mean(x_own * x_own, axis=1, keepdims=True) + EPS_ROW)
    first_rows = lay.rows_of((x_own * scale_one * gains[0]).astype(bf))
    proj_first, decays = project(first_rows, in_first, width, True)
    heads_out, states_first, inverses_first = mixer_forward(
        0, heads, core, proj_first, decays, marks, seg_rows, taps[0], params, gain_row, None
    )
    proj_second = project(first_rows, in_second, width, False)[0]
    heads_out, states_second, inverses_second = mixer_forward(
        pair, heads, core, proj_second, decays, marks, seg_rows, taps[1], params, gain_row, heads_out
    )
    mixed_own = lay.own_of([(0, 0, 1, 0, out_rows)], [heads_out], [out_pieces], nn, features)
    middle = x_own + live_own * mixed_own

    got_cot = exchange(send_cot)
    dy_own = matmul(matmul(landing, got_cot).astype(bf), turning)
    branch_rows = lay.rows_of((live_own * dy_own).astype(bf))
    scale_two = lax.rsqrt(jnp.mean(middle * middle, axis=1, keepdims=True) + EPS_ROW)
    second_rows = lay.rows_of((middle * scale_two * gains[1]).astype(bf))
    gate_pre, up_proj, hidden = feed_forward(second_rows, gate_pieces, up_pieces)
    depth = features // 4

    def columns_of(rows, piece):
        return rows[:, piece * depth : piece * depth + depth]

    down_own = lay.collect_ring(lambda r: outer_sum(hidden, columns_of(branch_rows, r)), True)
    grad_gate, grad_up = feed_backward(branch_rows, down_pieces, gate_pre, up_proj)
    gate_own = lay.collect_ring(lambda r: outer_sum(columns_of(second_rows, r), grad_gate), False)
    up_own = lay.collect_ring(lambda r: outer_sum(columns_of(second_rows, r), grad_up), True)
    grad_second = lay.own_of(
        [(0, 0, 2, 0, hidden_here), (1, 0, 6, 0, hidden_here)],
        [grad_gate, grad_up], [gate_pieces, up_pieces], nt, features,
    )
    grad_mid_norm, gain_two_grad = norm_back(middle, scale_two, gains[1], grad_second)
    grad_middle = dy_own + grad_mid_norm
    mix_rows = lay.rows_of((live_own * grad_middle).astype(bf))

    grad_heads = heads_backward(mix_rows, out_pieces)
    out_own = lay.collect_ring(lambda r: outer_sum(heads_out, columns_of(mix_rows, r)), False)
    grad_proj_first, taps_first, params_first, gain_first = mixer_backward(
        0, heads, core, proj_first, decays, grad_heads, marks, seg_rows, taps[0], params, gain_row,
        states_first, inverses_first, None,
    )
    first_own = lay.collect_ring(
        lambda r: outer_sum(columns_of(first_rows, r), grad_proj_first[:, :width]), True
    )
    grad_proj_second, taps_second, params_second, gain_second = mixer_backward(
        pair, heads, core, proj_second, decays, grad_heads, marks, seg_rows, taps[1], params, gain_row,
        states_second, inverses_second, grad_proj_first,
    )
    second_own = lay.collect_ring(lambda r: outer_sum(columns_of(first_rows, r), grad_proj_second), False)
    grad_first = lay.own_of(
        [(0, 0, 2, 0, width), (1, 0, 6, 0, width), (1, width, 2, width, LANES)],
        [grad_proj_first, grad_proj_second], [in_first, in_second], nt, features,
    )
    grad_x_norm, gain_one_grad = norm_back(x_own, scale_one, gains[0], grad_first)
    grad_tokens = (grad_middle + grad_x_norm).astype(bf)

    def sent_back(own):
        straight = times_back(own, turning).astype(bf)
        back = exchange(outer_sum(landing, straight).astype(bf))
        return outer_sum(sending, back).astype(bf)

    branch_own = lay.own_of([(0, 0, 1, 0, hidden_here)], [hidden], [down_pieces], nn, features)
    output = sent_back((middle + live_own * branch_own).astype(bf))
    tokens_grad = sent_back(grad_tokens)

    conv_full = jnp.zeros(conv_weights.shape, f32)
    for cut, grad in zip(cuts, (taps_first, taps_second)):
        begin = 0
        for start, size in cut:
            conv_full = lax.dynamic_update_slice_in_dim(conv_full, grad[:, begin : begin + size], start, 1)
            begin += size
    params_grad = params_first + params_second
    log_full = lax.dynamic_update_slice_in_dim(jnp.zeros_like(a_log), params_grad[0, :heads], share * heads, 0)
    bias_full = lax.dynamic_update_slice_in_dim(jnp.zeros_like(dt_bias), params_grad[1, :heads], share * heads, 0)
    gain_grad = gain_first[0] + gain_second[0]
    sums = flat([conv_full, straight_gain(gain_two_grad), gain_grad, log_full, bias_full])
    sums = lay.everywhere(sums).reshape(-1)
    late = lay.everywhere(flat([straight_gain(gain_one_grad)])).reshape(-1)[:features]
    ends = [conv_full.size]
    for size in (features, DV, all_heads, all_heads):
        ends.append(ends[-1] + size)
    norm_grad = jnp.stack([late, sums[ends[0] : ends[1]]])

    gate_grad, up_grad = lay.collect_rest(gate_own, 0), lay.collect_rest(up_own, 0)
    down_grad, out_grad = lay.collect_rest(down_own, 1), lay.collect_rest(out_own, 1)
    first_grad, second_grad = lay.collect_rest(first_own, 0), lay.collect_rest(second_own, 0)
    in_grads = []
    begin = 0
    for size in (keys, keys, vals, vals):
        part = slice(begin, begin + size)
        in_grads.append(
            lay.joined(*[[grads[0][:, part], grads[1][:, part]] for grads in zip(first_grad, second_grad)], 1)
        )
        begin += size
    for size in (heads, heads):
        in_grads.append(lay.joined(*[[grad[:, begin : begin + size]] for grad in second_grad], 1))
        begin += size
    return (
        output,
        tokens_grad,
        norm_grad,
        *in_grads,
        sums[: ends[0]].reshape(conv_full.shape),
        sums[ends[2] : ends[3]],
        sums[ends[3] : ends[4]],
        sums[ends[1] : ends[2]],
        lay.ordered(*out_grad, 0),
        lay.ordered(*gate_grad, 1),
        lay.ordered(*up_grad, 1),
        lay.ordered(*down_grad, 0),
    )


def solution(mesh):
    return jax.shard_map(
        shards,
        mesh=mesh,
        in_specs=(
            P(("dp", "tensor"), None),
            P(("dp", "tensor"), None),
            P("dp", None),
            P(("dp", "tensor")),
            P(),
            P("dp", "tensor"),
            P("dp", "tensor"),
            P("dp", "tensor"),
            P("dp", "tensor"),
            P("dp", "tensor"),
            P("dp", "tensor"),
            P(),
            P(),
            P(),
            P(),
            P("tensor", "dp"),
            P("dp", "tensor"),
            P("dp", "tensor"),
            P("tensor", "dp"),
        ),
        out_specs=(
            P(("dp", "tensor"), None),
            P(("dp", "tensor"), None),
            P(),
            P("dp", "tensor"),
            P("dp", "tensor"),
            P("dp", "tensor"),
            P("dp", "tensor"),
            P("dp", "tensor"),
            P("dp", "tensor"),
            P(),
            P(),
            P(),
            P(),
            P("tensor", "dp"),
            P("dp", "tensor"),
            P("dp", "tensor"),
            P("tensor", "dp"),
        ),
        check_vma=False,
    )
```

time: 1420 us -> 1140 us (0.80)
  Pallas kernels: 76.8 us -> 250 us
  waiting for transfers between devices: 681 us -> 525 us
  local copies, waits for them, and re-layouts: 184 us -> 38.4 us
  matrix products: 219 us -> 127 us
  other arithmetic: 142 us -> 75.8 us
    ppermute x40 -> x36, waiting for transfers between devices: 237 us -> 59.9 us  [ring(): line.append(lax.ppermute(values, 'dp', pairs))]
    pallas_call x2 -> x19, Pallas kernels: 76.8 us -> 250 us  [the longest x13 154 us: call(): pl.pallas_call(body, grid=grid, in_specs=in_specs, out_specs=out_specs, o...]
    dot_general x10 -> x5, matrix products: 83.5 us -> 14.4 us  [matmul(): return jnp.dot(left, right, preferred_element_type=f32)]
    unnamed x270 -> x175, local copies, waits for them, and re-layouts: 70.6 us -> 5.09 us
    dot_general x5 -> x0, matrix products: 55.6 us -> none  [times_back(): lax.dot_general(left, right, (((1,), (1,)), ((), ())), preferred_element_...]
    another operation x11 -> x1, other arithmetic: 34.9 us -> 0.62 us  [shards(): norm_grad = jnp.stack([late, sums[ends[0]:ends[1]]])]
    dot_general x9 -> x28, matrix products: 79.9 us -> 113 us  [outer_sum(): lax.dot_general(left, right, (((0,), (0,)), ((), ())), preferred_element_...]
    ppermute x37 -> x41, waiting for transfers between devices: 433 us -> 465 us  [flip(): return lax.ppermute(values, 'dp', [(n, n ^ bit) for n in range(self.ways)])]
  transfers between devices with their start and end apart: 95 -> 95, of which waited for: 35 -> 34; matrix products, arithmetic and copies ran while one was open for 32% -> 18% of each run, Pallas kernels for 5% -> 22%
where the time goes in v2:
time: 1140 us; the launch traced here: 1130 us
  waiting for transfers between devices  525 us (46%)
  Pallas kernels  250 us (22%)
  matrix products  127 us (11%)
  starting transfers between devices  114 us (10%)
  other arithmetic  75.8 us (7%)
  local copies, waits for them, and re-layouts  38.4 us (3%)
    ppermute x41, waiting for transfers between devices, flip(): return lax.ppermute(values, 'dp', [(n, n ^ bit) for n in range(self.ways)])  465 us
    pallas_call x13, Pallas kernels, call(): pl.pallas_call(body, grid=grid, in_specs=in_specs, out_specs=out_specs, o...  154 us
    dot_general x28, matrix products, outer_sum(): lax.dot_general(left, right, (((0,), (0,)), ((), ())), preferred_element_...  113 us
    ppermute x36, waiting for transfers between devices, ring(): line.append(lax.ppermute(values, 'dp', pairs))  59.9 us
    pallas_call x2, Pallas kernels, mixer_backward(): pl.pallas_call(body, grid_spec=pltpu.PrefetchScalarGridSpec(num_scalar_pr...  58.1 us
    ppermute x41, starting transfers between devices, flip(): return lax.ppermute(values, 'dp', [(n, n ^ bit) for n in range(self.ways)])  51.3 us
    ppermute x36, starting transfers between devices, ring(): line.append(lax.ppermute(values, 'dp', pairs))  42.5 us
    pallas_call x2, Pallas kernels, mixer_forward(): pl.pallas_call(body, grid_spec=pltpu.PrefetchScalarGridSpec(num_scalar_pr...  31.9 us
  transfers between devices with their start and end apart: 95, of which 34 were waited for; matrix products, arithmetic and copies ran while one was open for 18% of the time, Pallas kernels for 22%

profile of v2, /device:TPU:0, one launch (start us, length us, event | category | flops | bytes accessed | tf_op | source)
XLA Modules:
  0.0 1133.0 jit_solution(11632660554233881998)
XLA Ops:
  24.4 34.4 %collective-permute-done.4 = bf16[128,1664]{1,0:T(8,128)(2,1)} collective-permute-done((bf16[128,1664]{1,0:T(8,128)(2,1)}, bf16[128,1664]{1,0:T(8,128)(2,1)}, u32[]{:S(2)}, u32[]{:S(2)}) %collective-permute-start.4) | collective-permute-done | bytes 426016 | tf_op jit(solution)/shard_map/ppermute | solution.py:827
  64.9 36.8 %collective-permute-done.6 = bf16[256,1664]{1,0:T(8,128)(2,1)S(1)} collective-permute-done((bf16[256,1664]{1,0:T(8,128)(2,1)S(1)}, bf16[256,1664]{1,0:T(8,128)(2,1)S(1)}, u32[]{:S(2)}, u32[]{:S(2)}) %collective-permute-start.6) | collective-permute-done | bytes 852000 | tf_op jit(solution)/shard_map/ppermute | solution.py:827
  125.9 16.6 %collective-permute-done.11.refs_3_.refs_7_.refs_5_ = bf16[512,1664]{1,0:T(8,128)(2,1)} collective-permute-done((bf16[512,1664]{1,0:T(8,128)(2,1)}, bf16[512,1664]{1,0:T(8,128)(2,1)}, u32[]{:S(2)}, u32[]{:S(2)}) %collective-permute-start.11) | collective-permute-done | bytes 1703968 | tf_op jit(solution)/shard_map/ppermute | solution.py:823
  159.1 16.9 %collective-permute-done.1 = bf16[256,2048]{1,0:T(8,128)(2,1)} collective-permute-done((bf16[256,2048]{1,0:T(8,128)(2,1)}, bf16[256,2048]{1,0:T(8,128)(2,1)}, u32[]{:S(2)}, u32[]{:S(2)}) %collective-permute-start.1) | collective-permute-done | bytes 1048608 | tf_op jit(solution)/shard_map/ppermute | solution.py:827
  215.0 12.8 %project.3 = (bf16[1024,1536]{1,0:T(8,128)(2,1)}, f32[1024,128]{1,0:T(8,128)}) custom-call(bf16[1024,2048]{1,0:T(8,128)(2,1)} %pad_maximum_fusion.rows_ref, bf16[512,1664]{1,0:T(8,128)(2,1)} %pad_maximum_fusion.4.refs_0_.refs_4_.refs_2_, bf16[512,1664]{1,0:T(8,128)(2,1)} %collective-permute-done.8.refs_1_.refs_5_.refs_3_, ...), custom_call_target="tpu_custom_call" | custom-call | flops 6442450944 | bytes 13631488 | tf_op jit(solution)/shard_map/project/pallas_call | solution.py:580
  233.5 16.1 %mixer_forward.2 = (bf16[2,2,2,128,1024]{4,3,2,1,0:T(8,128)(2,1)}, bf16[4,4,128,256]{3,2,1,0:T(8,128)(2,1)}, bf16[4,4,128,128]{3,2,1,0:T(8,128)(2,1)}) custom-call(s32[1]{0:T(128)} %bitcast.2.refs_0_.core_ref, bf16[2,2,2,128,1536]{4,3,2,1,0:T(8,128)(2,1)} %bitcast.112, f32[2,2,2,128,128]{4,3,2,1,0:T(8,128)} %bitcast.120, ...), custom_call_target="tpu_custom_call" | custom-call | flops 16000000000 | bytes 16777216 | tf_op jit(solution)/shard_map/mixer_forward/pallas_call | solution.py:381
  250.6 11.3 %project.2 = bf16[1024,1536]{1,0:T(8,128)(2,1)} custom-call(bf16[1024,2048]{1,0:T(8,128)(2,1)} %pad_maximum_fusion.rows_ref, bf16[512,1536]{1,0:T(8,128)(2,1)} %pad_maximum_fusion.5.refs_0_.refs_6_, bf16[512,1536]{1,0:T(8,128)(2,1)} %collective-permute-done.9.refs_1_.refs_7_, bf16[512,1536]{1,0:T(8,128)(2,1)} %collective-permute-done.10.refs_2_.refs_8_, ...), custom_call_target="tpu_custom_call" | custom-call | flops 6442450944 | bytes 13631488 | tf_op jit(solution)/shard_map/project/pallas_call | solution.py:580
  263.0 15.8 %mixer_forward.3 = (bf16[2,2,2,128,1024]{4,3,2,1,0:T(8,128)(2,1)}, bf16[4,4,128,256]{3,2,1,0:T(8,128)(2,1)}, bf16[4,4,128,128]{3,2,1,0:T(8,128)(2,1)}) custom-call(s32[1]{0:T(128)} %bitcast.2.refs_0_.core_ref, bf16[2,2,2,128,1536]{4,3,2,1,0:T(8,128)(2,1)} %bitcast.115, f32[2,2,2,128,128]{4,3,2,1,0:T(8,128)} %bitcast.121, ...), custom_call_target="tpu_custom_call", output_to_operand_aliasing={{0}: (8, {})} | custom-call | flops 16000000000 | bytes 16777216 | tf_op jit(solution)/shard_map/mixer_forward/pallas_call | solution.py:381
  304.2 36.9 %collective-permute-done.29 = bf16[128,1408]{1,0:T(8,128)(2,1)S(1)} collective-permute-done((bf16[128,1408]{1,0:T(8,128)(2,1)S(1)}, bf16[128,1408]{1,0:T(8,128)(2,1)S(1)}, u32[]{:S(2)}, u32[]{:S(2)}) %collective-permute-start.29) | collective-permute-done | bytes 360480 | tf_op jit(solution)/shard_map/ppermute | solution.py:827
  344.7 9.9 collective-permute-done.26.refs_1_.refs_3_
  378.0 12.6 %collective-permute-done.30 = bf16[256,1408]{1,0:T(8,128)(2,1)} collective-permute-done((bf16[256,1408]{1,0:T(8,128)(2,1)S(1)}, bf16[256,1408]{1,0:T(8,128)(2,1)}, u32[]{:S(2)}, u32[]{:S(2)}) %collective-permute-start.30) | collective-permute-done | bytes 720928 | tf_op jit(solution)/shard_map/ppermute | solution.py:827
  393.9 17.7 %collective-permute-done.20 = bf16[256,2048]{1,0:T(8,128)(2,1)} collective-permute-done((bf16[256,2048]{1,0:T(8,128)(2,1)}, bf16[256,2048]{1,0:T(8,128)(2,1)}, u32[]{:S(2)}, u32[]{:S(2)}) %collective-permute-start.20) | collective-permute-done | bytes 1048608 | tf_op jit(solution)/shard_map/ppermute | solution.py:827
  431.1 15.8 %collective-permute-done.21 = bf16[256,2048]{1,0:T(8,128)(2,1)} collective-permute-done((bf16[256,2048]{1,0:T(8,128)(2,1)S(1)}, bf16[256,2048]{1,0:T(8,128)(2,1)}, u32[]{:S(2)}, u32[]{:S(2)}) %collective-permute-start.21) | collective-permute-done | bytes 1048608 | tf_op jit(solution)/shard_map/ppermute | solution.py:827
  446.9 22.4 %collective-permute-done.41 = bf16[256,2048]{1,0:T(8,128)(2,1)} collective-permute-done((bf16[256,2048]{1,0:T(8,128)(2,1)}, bf16[256,2048]{1,0:T(8,128)(2,1)}, u32[]{:S(2)}, u32[]{:S(2)}) %collective-permute-start.41) | collective-permute-done | bytes 1048608 | tf_op jit(solution)/shard_map/ppermute | solution.py:827
  475.4 18.5 %feed_forward.1 = (bf16[1024,1408]{1,0:T(8,128)(2,1)}, bf16[1024,1408]{1,0:T(8,128)(2,1)}, bf16[1024,1408]{1,0:T(8,128)(2,1)}) custom-call(bf16[1024,2048]{1,0:T(8,128)(2,1)} %pad_maximum_fusion.1.rows_ref, bf16[512,1408]{1,0:T(8,128)(2,1)} %pad_maximum_fusion.6.refs_0_.refs_2_, bf16[512,1408]{1,0:T(8,128)(2,1)} %collective-permute-done.26.refs_1_.refs_3_, ...), custom_call_target="tpu_custom_call" | custom-call | flops 11811160064 | bytes 24379392 | tf_op jit(solution)/shard_map/feed_forward/pallas_call | solution.py:580
  513.4 14.1 %feed_backward.1 = (bf16[1024,1408]{1,0:T(8,128)(2,1)}, bf16[1024,1408]{1,0:T(8,128)(2,1)}) custom-call(bf16[1024,2048]{1,0:T(8,128)(2,1)} %copy-done.27, bf16[1408,512]{1,0:T(8,128)(2,1)} %pad_maximum_fusion.8.refs_1_.refs_0_, bf16[1408,512]{1,0:T(8,128)(2,1)} %collective-permute-done.36.refs_2_.refs_1_, ...), custom_call_target="tpu_custom_call" | custom-call | flops 5905580032 | bytes 21495808 | tf_op jit(solution)/shard_map/feed_backward/pallas_call | solution.py:580
  527.5 12.8 %wide_given.6 = bf16[512,2048]{1,0:T(8,128)(2,1)} custom-call(bf16[1024,1408]{1,0:T(8,128)(2,1)} %get-tuple-element.151.refs_0_, bf16[1024,1408]{1,0:T(8,128)(2,1)} %get-tuple-element.152.refs_1_, bf16[512,1408]{1,0:T(8,128)(2,1)} %pad_maximum_fusion.6.refs_0_.refs_2_, bf16[512,1408]{1,0:T(8,128)(2,1)} %collective-permute-done.26.refs_1_.refs_3_, ...), custom_call_target="tpu_custom_call" | custom-call | flops 5905580032 | bytes 24117248 | tf_op jit(solution)/shard_map/wide_given/pallas_call | solution.py:580
  561.6 10.3 wide_kept.5
  571.9 14.4 %wide_kept.6 = (bf16[256,2048]{1,0:T(8,128)(2,1)}, f32[256,2048]{1,0:T(8,128)}) custom-call(bf16[1024,1408]{1,0:T(8,128)(2,1)} %get-tuple-element.151.refs_0_, bf16[1024,1408]{1,0:T(8,128)(2,1)} %get-tuple-element.152.refs_1_, bf16[512,1408]{1,0:T(8,128)(2,1)} %pad_maximum_fusion.6.refs_0_.refs_2_, ...), custom_call_target="tpu_custom_call" | custom-call | flops 5905580032 | bytes 24117248 | tf_op jit(solution)/shard_map/wide_kept/pallas_call | solution.py:580
  602.1 32.7 %collective-permute-done.45 = bf16[256,2048]{1,0:T(8,128)(2,1)S(1)} collective-permute-done((bf16[256,2048]{1,0:T(8,128)(2,1)}, bf16[256,2048]{1,0:T(8,128)(2,1)S(1)}, u32[]{:S(2)}, u32[]{:S(2)}) %collective-permute-start.45) | collective-permute-done | bytes 1048608 | tf_op jit(solution)/shard_map/ppermute | solution.py:827
  665.0 29.7 %collective-permute-done.90 = bf16[1408,128]{1,0:T(8,128)(2,1)S(1)} collective-permute-done((bf16[1408,128]{1,0:T(8,128)(2,1)S(1)}, bf16[1408,128]{1,0:T(8,128)(2,1)S(1)}, u32[]{:S(2)}, u32[]{:S(2)}) %collective-permute-start.90) | collective-permute-done | bytes 360480 | tf_op jit(solution)/shard_map/ppermute | solution.py:827
  715.0 28.6 %mixer_backward.2 = (bf16[2,2,2,128,1664]{4,3,2,1,0:T(8,128)(2,1)}, f32[4,1024]{1,0:T(4,128)}, f32[8,128]{1,0:T(8,128)}, f32[8,256]{1,0:T(8,128)}) custom-call(s32[1]{0:T(128)} %bitcast.2.refs_0_.core_ref, bf16[2,2,2,128,1536]{4,3,2,1,0:T(8,128)(2,1)} %bitcast.113, bf16[2,2,2,128,1536]{4,3,2,1,0:T(8,128)(2,1)} %bitcast.114, ...), custom_call_target="tpu_custom_call" | custom-call | flops 30000001024 | bytes 31457280 | tf_op jit(solution)/shard_map/mixer_backward/pallas_call | solution.py:467
  743.6 29.4 %mixer_backward.3 = (bf16[2,2,2,128,1664]{4,3,2,1,0:T(8,128)(2,1)}, f32[4,1024]{1,0:T(4,128)}, f32[8,128]{1,0:T(8,128)}, f32[8,256]{1,0:T(8,128)}) custom-call(s32[1]{0:T(128)} %bitcast.2.refs_0_.core_ref, bf16[2,2,2,128,1536]{4,3,2,1,0:T(8,128)(2,1)} %bitcast.116, bf16[2,2,2,128,1536]{4,3,2,1,0:T(8,128)(2,1)} %bitcast.117, ...), custom_call_target="tpu_custom_call" | custom-call | flops 30000001024 | bytes 31457280 | tf_op jit(solution)/shard_map/mixer_backward/pallas_call | solution.py:467
  781.6 13.9 %wide_given.7 = bf16[512,2048]{1,0:T(8,128)(2,1)} custom-call(bf16[1024,1664]{1,0:T(8,128)(2,1)} %bitcast.106, bf16[1024,1664]{1,0:T(8,128)(2,1)} %bitcast.69, bf16[512,1664]{1,0:T(8,128)(2,1)} %pad_maximum_fusion.4.refs_0_.refs_4_.refs_2_, bf16[512,1664]{1,0:T(8,128)(2,1)} %collective-permute-done.8.refs_1_.refs_5_.refs_3_, ...), custom_call_target="tpu_custom_call" | custom-call | flops 6710886400 | bytes 25690112 | tf_op jit(solution)/shard_map/wide_given/pallas_call | solution.py:580
  821.7 22.3 %collective-permute-done.65 = bf16[512,1408]{1,0:T(8,128)(2,1)} collective-permute-done((bf16[512,1408]{1,0:T(8,128)(2,1)}, bf16[512,1408]{1,0:T(8,128)(2,1)}, u32[]{:S(2)}, u32[]{:S(2)}) %collective-permute-start.65) | collective-permute-done | bytes 1441824 | tf_op jit(solution)/shard_map/ppermute | solution.py:823
  861.9 15.5 %wide_kept.7 = (bf16[256,2048]{1,0:T(8,128)(2,1)}, f32[256,2048]{1,0:T(8,128)}) custom-call(bf16[1024,1664]{1,0:T(8,128)(2,1)} %bitcast.108, bf16[1024,1664]{1,0:T(8,128)(2,1)} %bitcast.70, bf16[512,1664]{1,0:T(8,128)(2,1)} %pad_maximum_fusion.4.refs_0_.refs_4_.refs_2_, bf16[512,1664]{1,0:T(8,128)(2,1)} %collective-permute-done.8.refs_1_.refs_5_.refs_3_, ...), custom_call_target="tpu_custom_call" | custom-call | flops 6710886400 | bytes 25690112 | tf_op jit(solution)/shard_map/wide_kept/pallas_call | solution.py:580
  891.2 18.1 %collective-permute-done.50 = bf16[256,2048]{1,0:T(8,128)(2,1)S(1)} collective-permute-done((bf16[256,2048]{1,0:T(8,128)(2,1)}, bf16[256,2048]{1,0:T(8,128)(2,1)S(1)}, u32[]{:S(2)}, u32[]{:S(2)}) %collective-permute-start.50) | collective-permute-done | bytes 1048608 | tf_op jit(solution)/shard_map/ppermute | solution.py:827
  967.5 34.4 %collective-permute-done.58 = f32[280,128]{1,0:T(8,128)S(1)} collective-permute-done((f32[280,128]{1,0:T(8,128)S(1)}, f32[280,128]{1,0:T(8,128)S(1)}, u32[]{:S(2)}, u32[]{:S(2)}) %collective-permute-start.58) | collective-permute-done | bytes 143392 | tf_op jit(solution)/shard_map/ppermute | solution.py:827
  1007.5 10.8 collective-permute-done.59
  1035.8 31.4 %collective-permute-done.76 = bf16[256,1536]{1,0:T(8,128)(2,1)} collective-permute-done((bf16[256,1536]{1,0:T(8,128)(2,1)}, bf16[256,1536]{1,0:T(8,128)(2,1)}, u32[]{:S(2)}, u32[]{:S(2)}) %collective-permute-start.76) | collective-permute-done | bytes 786464 | tf_op jit(solution)/shard_map/ppermute | solution.py:827
  1079.0 22.0 %collective-permute-done.81 = bf16[128,1536]{1,0:T(8,128)(2,1)S(1)} collective-permute-done((bf16[128,1536]{1,0:T(8,128)(2,1)S(1)}, bf16[128,1536]{1,0:T(8,128)(2,1)S(1)}, u32[]{:S(2)}, u32[]{:S(2)}) %collective-permute-start.81) | collective-permute-done | bytes 393248 | tf_op jit(solution)/shard_map/ppermute | solution.py:827
  1101.8 11.4 %collective-permute-done.80 = bf16[256,1664]{1,0:T(8,128)(2,1)S(1)} collective-permute-done((bf16[256,1664]{1,0:T(8,128)(2,1)S(1)}, bf16[256,1664]{1,0:T(8,128)(2,1)S(1)}, u32[]{:S(2)}, u32[]{:S(2)}) %collective-permute-start.80) | collective-permute-done | bytes 852000 | tf_op jit(solution)/shard_map/ppermute | solution.py:827
  (549 shorter events, 484.3 us)
Async XLA Ops:
  5.2 112.2 %all-to-all-start = ((bf16[32,10,2176]{2,1,0:T(8,128)(2,1)}), bf16[32,10,2176]{2,1,0:T(8,128)(2,1)S(1)}, u32[]{:S(2)}, u32[]{:S(2)}) async-start(bf16[32,10,2176]{2,1,0:T(8,128)(2,1)} %all_to_all.32), calls=%async_computation | async-start | bytes 4456448 | tf_op jit(solution)/shard_map/all_to_all | solution.py:951
  18.9 90.1 %collective-permute-start = (s32[1,4]{1,0:T(1,128)S(1)}, s32[1,4]{1,0:T(1,128)S(1)}, u32[]{:S(2)}, u32[]{:S(2)}) collective-permute-start(s32[1,4]{1,0:T(1,128)S(1)} %copy-done.76), channel_id=1, source_target_pairs={{0,8},{2,10},{4,12},{6,14},{8,0},{10,2},{12,4},{14,6},{16,24},{18,... | collective-permute-start | bytes 56 | tf_op jit(solution)/shard_map/ppermute | solution.py:827
  156.2 52.9 %collective-permute-start.9 = (bf16[512,1536]{1,0:T(8,128)(2,1)}, bf16[512,1536]{1,0:T(8,128)(2,1)}, u32[]{:S(2)}, u32[]{:S(2)}) collective-permute-start(bf16[512,1536]{1,0:T(8,128)(2,1)} %pad_maximum_fusion.5.refs_0_.refs_6_), channel_id=1, source_target_pairs={{0,4},{2,0},{4,6},{6,2},{8,12},{10,8},{12,14},{14,10},{16,20},{18,... | collective-permute-start | bytes 4718600 | tf_op jit(solution)/shard_map/ppermute | solution.py:823
  159.0 52.5 %collective-permute-start.2 = (bf16[256,2048]{1,0:T(8,128)(2,1)}, bf16[256,2048]{1,0:T(8,128)(2,1)S(1)}, u32[]{:S(2)}, u32[]{:S(2)}) collective-permute-start(bf16[256,2048]{1,0:T(8,128)(2,1)} %multiply_convert_fusion.3), channel_id=1, source_target_pairs={{0,1},{1,0},{2,3},{3,2},{4,5},{5,4},{6,7},{7,6},{8,9},{9,8},{10,11... | collective-permute-start | bytes 3145736 | tf_op jit(solution)/shard_map/ppermute | solution.py:833
  209.0 89.3 %collective-permute-start.25 = (bf16[256,1408]{1,0:T(8,128)(2,1)}, bf16[256,1408]{1,0:T(8,128)(2,1)}, u32[]{:S(2)}, u32[]{:S(2)}) collective-permute-start(bf16[256,1408]{1,0:T(8,128)(2,1)} %maximum_select_fusion.8), channel_id=1, source_target_pairs={{0,16},{2,18},{4,20},{6,22},{8,24},{10,26},{12,28},{14,30},{16,0},... | collective-permute-start | bytes 2162696 | tf_op jit(solution)/shard_map/ppermute | solution.py:827
  292.0 67.1 %collective-permute-start.19 = (bf16[512,2048]{1,0:T(8,128)(2,1)}, bf16[512,2048]{1,0:T(8,128)(2,1)}, u32[]{:S(2)}, u32[]{:S(2)}) collective-permute-start(bf16[512,2048]{1,0:T(8,128)(2,1)} %wide_given.4), channel_id=1, source_target_pairs={{0,1},{1,0},{2,3},{3,2},{4,5},{5,4},{6,7},{7,6},{8,9},{9,8},{10,11... | collective-permute-start | bytes 6291464 | tf_op jit(solution)/shard_map/ppermute | solution.py:833
  294.1 76.1 %all-to-all-start.2 = ((bf16[32,10,2048]{2,1,0:T(8,128)(2,1)}), bf16[32,10,2048]{2,1,0:T(8,128)(2,1)S(1)}, u32[]{:S(2)}, u32[]{:S(2)}) async-start(bf16[32,10,2048]{2,1,0:T(8,128)(2,1)} %all_to_all.38), calls=%async_computation.2 | async-start | bytes 4194304 | tf_op jit(solution)/shard_map/all_to_all | solution.py:951
  300.9 53.7 %collective-permute-start.26 = (bf16[512,1408]{1,0:T(8,128)(2,1)}, bf16[512,1408]{1,0:T(8,128)(2,1)}, u32[]{:S(2)}, u32[]{:S(2)}) collective-permute-start(bf16[512,1408]{1,0:T(8,128)(2,1)} %pad_maximum_fusion.6.refs_0_.refs_2_), channel_id=1, source_target_pairs={{0,4},{2,0},{4,6},{6,2},{8,12},{10,8},{12,14},{14,10},{16,20},{18,... | collective-permute-start | bytes 4325384 | tf_op jit(solution)/shard_map/ppermute | solution.py:823
  343.6 48.3 %collective-permute-start.28 = (bf16[512,1408]{1,0:T(8,128)(2,1)}, bf16[512,1408]{1,0:T(8,128)(2,1)}, u32[]{:S(2)}, u32[]{:S(2)}) collective-permute-start(bf16[512,1408]{1,0:T(8,128)(2,1)} %pad_maximum_fusion.6.refs_0_.refs_2_), channel_id=1, source_target_pairs={{0,2},{2,6},{4,0},{6,4},{8,10},{10,14},{12,8},{14,12},{16,18},{18,... | collective-permute-start | bytes 4325384 | tf_op jit(solution)/shard_map/ppermute | solution.py:823
  503.7 44.9 %collective-permute-start.61 = (bf16[1408,512]{1,0:T(8,128)(2,1)}, bf16[1408,512]{1,0:T(8,128)(2,1)}, u32[]{:S(2)}, u32[]{:S(2)}) collective-permute-start(bf16[1408,512]{1,0:T(8,128)(2,1)} %convolution_convert_fusion.7), channel_id=1, source_target_pairs={{0,2},{2,6},{4,0},{6,4},{8,10},{10,14},{12,8},{14,12},{16,18},{18,... | collective-permute-start | bytes 4325384 | tf_op jit(solution)/shard_map/ppermute | solution.py:823
  512.8 48.8 %collective-permute-start.39 = (bf16[512,2048]{1,0:T(8,128)(2,1)}, bf16[512,2048]{1,0:T(8,128)(2,1)}, u32[]{:S(2)}, u32[]{:S(2)}) collective-permute-start(bf16[512,2048]{1,0:T(8,128)(2,1)} %wide_given.5), channel_id=1, source_target_pairs={{0,1},{1,0},{2,3},{3,2},{4,5},{5,4},{6,7},{7,6},{8,9},{9,8},{10,11... | collective-permute-start | bytes 6291464 | tf_op jit(solution)/shard_map/ppermute | solution.py:833
  512.8 45.1 %collective-permute-start.69 = (bf16[1408,512]{1,0:T(8,128)(2,1)}, bf16[1408,512]{1,0:T(8,128)(2,1)}, u32[]{:S(2)}, u32[]{:S(2)}) collective-permute-start(bf16[1408,512]{1,0:T(8,128)(2,1)} %convolution_convert_fusion.3), channel_id=1, source_target_pairs={{0,4},{2,0},{4,6},{6,2},{8,12},{10,8},{12,14},{14,10},{16,20},{18,... | collective-permute-start | bytes 4325384 | tf_op jit(solution)/shard_map/ppermute | solution.py:823
  571.9 77.9 %collective-permute-start.40 = (bf16[256,2048]{1,0:T(8,128)(2,1)}, bf16[256,2048]{1,0:T(8,128)(2,1)}, u32[]{:S(2)}, u32[]{:S(2)}) collective-permute-start(bf16[256,2048]{1,0:T(8,128)(2,1)} %get-tuple-element.148), channel_id=1, source_target_pairs={{0,8},{2,10},{4,12},{6,14},{8,0},{10,2},{12,4},{14,6},{16,24},{18,... | collective-permute-start | bytes 3145736 | tf_op jit(solution)/shard_map/ppermute | solution.py:827
  586.4 48.5 %collective-permute-start.45 = (bf16[256,2048]{1,0:T(8,128)(2,1)}, bf16[256,2048]{1,0:T(8,128)(2,1)S(1)}, u32[]{:S(2)}, u32[]{:S(2)}) collective-permute-start(bf16[256,2048]{1,0:T(8,128)(2,1)} %get-tuple-element.154), channel_id=1, source_target_pairs={{0,8},{2,10},{4,12},{6,14},{8,0},{10,2},{12,4},{14,6},{16,24},{18,... | collective-permute-start | bytes 3145736 | tf_op jit(solution)/shard_map/ppermute | solution.py:827
  588.4 50.9 %collective-permute-start.63 = (bf16[512,1408]{1,0:T(8,128)(2,1)}, bf16[512,1408]{1,0:T(8,128)(2,1)S(1)}, u32[]{:S(2)}, u32[]{:S(2)}) collective-permute-start(bf16[512,1408]{1,0:T(8,128)(2,1)} %convolution_convert_fusion.8), channel_id=1, source_target_pairs={{0,2},{2,6},{4,0},{6,4},{8,10},{10,14},{12,8},{14,12},{16,18},{18,... | collective-permute-start | bytes 4325384 | tf_op jit(solution)/shard_map/ppermute | solution.py:823
  638.9 57.9 %collective-permute-start.46 = (bf16[256,2048]{1,0:T(8,128)(2,1)}, bf16[256,2048]{1,0:T(8,128)(2,1)}, u32[]{:S(2)}, u32[]{:S(2)}) collective-permute-start(bf16[256,2048]{1,0:T(8,128)(2,1)} %get-tuple-element.250), channel_id=1, source_target_pairs={{0,8},{2,10},{4,12},{6,14},{8,0},{10,2},{12,4},{14,6},{16,24},{18,... | collective-permute-start | bytes 3145736 | tf_op jit(solution)/shard_map/ppermute | solution.py:827
  638.9 62.4 %collective-permute-start.47 = (bf16[256,2048]{1,0:T(8,128)(2,1)}, bf16[256,2048]{1,0:T(8,128)(2,1)}, u32[]{:S(2)}, u32[]{:S(2)}) collective-permute-start(bf16[256,2048]{1,0:T(8,128)(2,1)} %get-tuple-element.250), channel_id=1, source_target_pairs={{0,1},{1,0},{2,3},{3,2},{4,5},{5,4},{6,7},{7,6},{8,9},{9,8},{10,11... | collective-permute-start | bytes 3145736 | tf_op jit(solution)/shard_map/ppermute | solution.py:833
  639.3 55.5 %collective-permute-start.90 = (bf16[1408,128]{1,0:T(8,128)(2,1)S(1)}, bf16[1408,128]{1,0:T(8,128)(2,1)S(1)}, u32[]{:S(2)}, u32[]{:S(2)}) collective-permute-start(bf16[1408,128]{1,0:T(8,128)(2,1)S(1)} %dynamic-slice_convert_fusion.2), channel_id=1, source_target_pairs={{0,8},{2,10},{4,12},{6,14},{8,0},{10,2},{12,4},{14,6},{16,24},{18,... | collective-permute-start | bytes 1081352 | tf_op jit(solution)/shard_map/ppermute | solution.py:827
  646.0 52.3 %collective-permute-start.85 = (bf16[256,1408]{1,0:T(8,128)(2,1)}, bf16[256,1408]{1,0:T(8,128)(2,1)}, u32[]{:S(2)}, u32[]{:S(2)}) collective-permute-start(bf16[256,1408]{1,0:T(8,128)(2,1)} %slice.549), channel_id=1, source_target_pairs={{0,16},{2,18},{4,20},{6,22},{8,24},{10,26},{12,28},{14,30},{16,0},... | collective-permute-start | bytes 2162696 | tf_op jit(solution)/shard_map/ppermute | solution.py:827
  660.2 156.9 %all-to-all-start.1 = ((bf16[32,10,2048]{2,1,0:T(8,128)(2,1)}), bf16[32,10,2048]{2,1,0:T(8,128)(2,1)S(1)}, u32[]{:S(2)}, u32[]{:S(2)}) async-start(bf16[32,10,2048]{2,1,0:T(8,128)(2,1)} %all_to_all.35), calls=%async_computation.1 | async-start | bytes 4194304 | tf_op jit(solution)/shard_map/all_to_all | solution.py:951
  696.1 109.0 %collective-permute-start.64 = (bf16[512,1408]{1,0:T(8,128)(2,1)}, bf16[512,1408]{1,0:T(8,128)(2,1)}, u32[]{:S(2)}, u32[]{:S(2)}) collective-permute-start(bf16[512,1408]{1,0:T(8,128)(2,1)} %convolution_convert_fusion.9), channel_id=1, source_target_pairs={{0,2},{2,6},{4,0},{6,4},{8,10},{10,14},{12,8},{14,12},{16,18},{18,... | collective-permute-start | bytes 4325384 | tf_op jit(solution)/shard_map/ppermute | solution.py:823
  696.9 117.6 %collective-permute-start.72 = (bf16[512,1408]{1,0:T(8,128)(2,1)}, bf16[512,1408]{1,0:T(8,128)(2,1)}, u32[]{:S(2)}, u32[]{:S(2)}) collective-permute-start(bf16[512,1408]{1,0:T(8,128)(2,1)} %convolution_convert_fusion.5), channel_id=1, source_target_pairs={{0,4},{2,0},{4,6},{6,2},{8,12},{10,8},{12,14},{14,10},{16,20},{18,... | collective-permute-start | bytes 4325384 | tf_op jit(solution)/shard_map/ppermute | solution.py:823
  700.4 114.1 %collective-permute-start.86 = (bf16[128,1408]{1,0:T(8,128)(2,1)}, bf16[128,1408]{1,0:T(8,128)(2,1)S(1)}, u32[]{:S(2)}, u32[]{:S(2)}) collective-permute-start(bf16[128,1408]{1,0:T(8,128)(2,1)} %dynamic-slice_convert_fusion.4), channel_id=1, source_target_pairs={{0,8},{2,10},{4,12},{6,14},{8,0},{10,2},{12,4},{14,6},{16,24},{18,... | collective-permute-start | bytes 1081352 | tf_op jit(solution)/shard_map/ppermute | solution.py:827
  795.5 66.4 %collective-permute-start.49 = (bf16[512,2048]{1,0:T(8,128)(2,1)}, bf16[512,2048]{1,0:T(8,128)(2,1)}, u32[]{:S(2)}, u32[]{:S(2)}) collective-permute-start(bf16[512,2048]{1,0:T(8,128)(2,1)} %wide_given.7), channel_id=1, source_target_pairs={{0,1},{1,0},{2,3},{3,2},{4,5},{5,4},{6,7},{7,6},{8,9},{9,8},{10,11... | collective-permute-start | bytes 6291464 | tf_op jit(solution)/shard_map/ppermute | solution.py:833
  889.1 51.1 %collective-permute-start.75 = (bf16[512,1536]{1,0:T(8,128)(2,1)}, bf16[512,1536]{1,0:T(8,128)(2,1)}, u32[]{:S(2)}, u32[]{:S(2)}) collective-permute-start(bf16[512,1536]{1,0:T(8,128)(2,1)} %convolution_convert_fusion.6), channel_id=1, source_target_pairs={{0,4},{2,0},{4,6},{6,2},{8,12},{10,8},{12,14},{14,10},{16,20},{18,... | collective-permute-start | bytes 4718600 | tf_op jit(solution)/shard_map/ppermute | solution.py:823
  890.9 50.2 %collective-permute-start.67 = (bf16[512,1536]{1,0:T(8,128)(2,1)}, bf16[512,1536]{1,0:T(8,128)(2,1)}, u32[]{:S(2)}, u32[]{:S(2)}) collective-permute-start(bf16[512,1536]{1,0:T(8,128)(2,1)} %convolution_convert_fusion.10), channel_id=1, source_target_pairs={{0,2},{2,6},{4,0},{6,4},{8,10},{10,14},{12,8},{14,12},{16,18},{18,... | collective-permute-start | bytes 4718600 | tf_op jit(solution)/shard_map/ppermute | solution.py:823
  914.7 50.7 %collective-permute-start.83 = (bf16[1024,256]{1,0:T(8,128)(2,1)S(1)}, bf16[1024,256]{1,0:T(8,128)(2,1)}, u32[]{:S(2)}, u32[]{:S(2)}) collective-permute-start(bf16[1024,256]{1,0:T(8,128)(2,1)S(1)} %slice.550), channel_id=1, source_target_pairs={{0,16},{2,18},{4,20},{6,22},{8,24},{10,26},{12,28},{14,30},{16,0},... | collective-permute-start | bytes 1572872 | tf_op jit(solution)/shard_map/ppermute | solution.py:827
  940.2 79.6 %collective-permute-start.78 = (bf16[512,1664]{1,0:T(8,128)(2,1)}, bf16[512,1664]{1,0:T(8,128)(2,1)}, u32[]{:S(2)}, u32[]{:S(2)}) collective-permute-start(bf16[512,1664]{1,0:T(8,128)(2,1)} %convolution_convert_fusion.1), channel_id=1, source_target_pairs={{0,4},{2,0},{4,6},{6,2},{8,12},{10,8},{12,14},{14,10},{16,20},{18,... | collective-permute-start | bytes 5111816 | tf_op jit(solution)/shard_map/ppermute | solution.py:823
  946.9 71.6 %collective-permute-start.68 = (bf16[512,1536]{1,0:T(8,128)(2,1)}, bf16[512,1536]{1,0:T(8,128)(2,1)}, u32[]{:S(2)}, u32[]{:S(2)}) collective-permute-start(bf16[512,1536]{1,0:T(8,128)(2,1)} %fusion.12), channel_id=1, source_target_pairs={{0,2},{2,6},{4,0},{6,4},{8,10},{10,14},{12,8},{14,12},{16,18},{18,... | collective-permute-start | bytes 4718600 | tf_op jit(solution)/shard_map/ppermute | solution.py:823
  959.5 74.9 %all-to-all-start.3 = ((bf16[32,10,2048]{2,1,0:T(8,128)(2,1)}), bf16[32,10,2048]{2,1,0:T(8,128)(2,1)S(1)}, u32[]{:S(2)}, u32[]{:S(2)}) async-start(bf16[32,10,2048]{2,1,0:T(8,128)(2,1)} %all_to_all.41), calls=%async_computation.3 | async-start | bytes 4194304 | tf_op jit(solution)/shard_map/all_to_all | solution.py:951
  1018.5 50.5 %collective-permute-start.77 = (bf16[512,1664]{1,0:T(8,128)(2,1)}, bf16[512,1664]{1,0:T(8,128)(2,1)}, u32[]{:S(2)}, u32[]{:S(2)}) collective-permute-start(bf16[512,1664]{1,0:T(8,128)(2,1)} %convolution_convert_fusion.2), channel_id=1, source_target_pairs={{0,2},{2,6},{4,0},{6,4},{8,10},{10,14},{12,8},{14,12},{16,18},{18,... | collective-permute-start | bytes 5111816 | tf_op jit(solution)/shard_map/ppermute | solution.py:823
  1024.6 44.4 %collective-permute-start.79 = (bf16[512,1664]{1,0:T(8,128)(2,1)}, bf16[512,1664]{1,0:T(8,128)(2,1)}, u32[]{:S(2)}, u32[]{:S(2)}) collective-permute-start(bf16[512,1664]{1,0:T(8,128)(2,1)} %add_convert_fusion), channel_id=1, source_target_pairs={{0,4},{2,0},{4,6},{6,2},{8,12},{10,8},{12,14},{14,10},{16,20},{18,... | collective-permute-start | bytes 5111816 | tf_op jit(solution)/shard_map/ppermute | solution.py:823
  (150 other events, 4032.6 us)

commit v3 on v2

--- a/solution.py
+++ b/solution.py
@@ -19,6 +19,7 @@
 EPS_HEAD = 1e-05
 NEG = -1e30
 VMEM_LIMIT = 56 * 2**20
+COST = 1.0
 
 
 def dot(left, right, left_dim, right_dim):
@@ -406,7 +407,7 @@
             jax.ShapeDtypeStruct((chunks, units, CHUNK, CHUNK), bf),
         ],
         compiler_params=pltpu.CompilerParams(vmem_limit_bytes=VMEM_LIMIT),
-        cost_estimate=pl.CostEstimate(flops=16 * 10**9, bytes_accessed=16 * 2**20, transcendentals=0),
+        cost_estimate=pl.CostEstimate(flops=int(COST * 16 * 10**9), bytes_accessed=int(COST * 16 * 2**20), transcendentals=0),
         input_output_aliases=aliases,
         name="mixer_forward",
     )(core, proj, decays, marks, seg_rows, taps, params, gain, *more)
@@ -489,7 +490,7 @@
             jax.ShapeDtypeStruct((8, DV), f32),
         ],
         compiler_params=pltpu.CompilerParams(vmem_limit_bytes=VMEM_LIMIT),
-        cost_estimate=pl.CostEstimate(flops=30 * 10**9, bytes_accessed=30 * 2**20, transcendentals=0),
+        cost_estimate=pl.CostEstimate(flops=int(COST * 30 * 10**9), bytes_accessed=int(COST * 30 * 2**20), transcendentals=0),
         name="mixer_backward",
     )(*inputs)
     return out.reshape(-1, width), taps_grad, params_grad, gain_grad
@@ -576,15 +577,16 @@
 STRIP = 256
 
 
-def call(body, grid, in_specs, out_specs, out_shape, flops, moved, name, inputs):
+def call(body, grid, in_specs, out_specs, out_shape, flops, moved, name, inputs, scratch=()):
     return pl.pallas_call(
         body,
         grid=grid,
+        scratch_shapes=scratch,
         in_specs=in_specs,
         out_specs=out_specs,
         out_shape=out_shape,
         compiler_params=pltpu.CompilerParams(vmem_limit_bytes=VMEM_LIMIT),
-        cost_estimate=pl.CostEstimate(flops=flops, bytes_accessed=moved, transcendentals=0),
+        cost_estimate=pl.CostEstimate(flops=int(flops * COST), bytes_accessed=int(moved * COST), transcendentals=0),
         name=name,
     )(*inputs)
 
@@ -636,61 +638,66 @@
     return call(body, (steps,), in_specs, out_specs, out_shape, flops, moved, "project", inputs)
 
 
-def feed_forward(rows, gate_pieces, up_pieces):
+def feed_forward(rows, pieces):
     count = rows.shape[0]
-    depth, width = gate_pieces[0].shape
-    used = len(gate_pieces)
+    depth, width = pieces[0].shape
+    used = len(pieces)
 
     def body(rows_ref, *refs):
-        gate_out, up_out, hidden_out = refs[2 * used :]
+        pre_out, hidden_out = refs[used:]
         for start in range(0, count, STRIP):
             strip = slice(start, start + STRIP)
-            gate = strip_sum(rows_ref, refs[:used], start, nn)
-            up = strip_sum(rows_ref, refs[used : 2 * used], start, nn)
-            gate_out[strip, :] = gate.astype(bf)
-            up_out[strip, :] = up.astype(bf)
-            hidden_out[strip, :] = (gate * sigmoid(gate) * up).astype(bf)
-
-    out_spec = pl.BlockSpec((count, TILE), lambda i: (0, i))
+            both = strip_sum(rows_ref, refs[:used], start, nn)
+            gate = both[:, :LANES]
+            pre_out[strip, :] = both.astype(bf)
+            hidden_out[strip, :] = (gate * sigmoid(gate) * both[:, LANES:]).astype(bf)
+
     return call(
         body,
-        (pl.cdiv(width, TILE),),
-        [whole(rows)] + [pl.BlockSpec((depth, TILE), lambda i: (0, i))] * (2 * used),
-        [out_spec] * 3,
-        [jax.ShapeDtypeStruct((count, width), bf)] * 3,
-        4 * count * depth * used * width,
-        2 * (count * depth * used + 2 * depth * used * width + 3 * count * width),
+        (width // (2 * LANES),),
+        [whole(rows)] + [pl.BlockSpec((depth, 2 * LANES), lambda i: (0, i))] * used,
+        [pl.BlockSpec((count, 2 * LANES), lambda i: (0, i)), pl.BlockSpec((count, LANES), lambda i: (0, i))],
+        [jax.ShapeDtypeStruct((count, width), bf), jax.ShapeDtypeStruct((count, width // 2), bf)],
+        2 * count * depth * used * width,
+        2 * (count * depth * used + depth * used * width + 2 * count * width),
         "feed_forward",
-        [rows, *gate_pieces, *up_pieces],
-    )
-
-
-def feed_backward(rows, down_pieces, gate_pre, up_proj):
+        [rows, *pieces],
+    )
+
+
+def feed_backward(rows, down_pieces, pre):
     count = rows.shape[0]
     width, depth = down_pieces[0].shape
     used = len(down_pieces)
 
     def body(rows_ref, *refs):
-        gate_ref, up_ref, gate_out, up_out = refs[used:]
-        for start in range(0, count, STRIP):
-            strip = slice(start, start + STRIP)
-            grad = strip_sum(rows_ref, refs[:used], start, nt)
-            gate = gate_ref[strip, :].astype(f32)
-            soft = sigmoid(gate)
-            gate_out[strip, :] = (grad * up_ref[strip, :].astype(f32) * soft * (1.0 + gate * (1.0 - soft))).astype(bf)
-            up_out[strip, :] = (grad * gate * soft).astype(bf)
-
-    tile = pl.BlockSpec((count, TILE), lambda i: (0, i))
+        pre_ref, out = refs[used:]
+        for begin in range(0, width, TILE):
+            size = min(TILE, width - begin)
+            total = None
+            for number in range(used):
+                part = nt(rows_ref[:, number * depth : number * depth + depth], refs[number][begin : begin + size, :])
+                total = part if total is None else total + part
+            for shift in range(0, size, LANES):
+                grad = total[:, shift : shift + LANES]
+                at = 2 * (begin + shift)
+                gate = pre_ref[:, at : at + LANES].astype(f32)
+                up = pre_ref[:, at + LANES : at + 2 * LANES].astype(f32)
+                soft = sigmoid(gate)
+                out[:, at : at + LANES] = (grad * up * soft * (1.0 + gate * (1.0 - soft))).astype(bf)
+                out[:, at + LANES : at + 2 * LANES] = (grad * gate * soft).astype(bf)
+
+    strip = pl.BlockSpec((STRIP, 2 * width), lambda i: (i, 0))
     return call(
         body,
-        (pl.cdiv(width, TILE),),
-        [whole(rows)] + [pl.BlockSpec((TILE, depth), lambda i: (i, 0))] * used + [tile] * 2,
-        [tile] * 2,
-        [jax.ShapeDtypeStruct((count, width), bf)] * 2,
+        (count // STRIP,),
+        [pl.BlockSpec((STRIP, depth * used), lambda i: (i, 0))] + [whole(piece) for piece in down_pieces] + [strip],
+        strip,
+        jax.ShapeDtypeStruct((count, 2 * width), bf),
         2 * count * depth * used * width,
         2 * (count * depth * used + depth * used * width + 4 * count * width),
         "feed_backward",
-        [rows, *down_pieces, gate_pre, up_proj],
+        [rows, *down_pieces, pre],
     )
 
 
@@ -716,62 +723,62 @@
     )
 
 
-def widen(terms, refs, product):
-    outs = []
-    for piece in range(4):
-        total = None
-        for number, begin, weight, first, columns in terms:
-            left = refs[number][:, begin : begin + columns]
-            right = refs[weight + piece]
-            right = right[:, first : first + columns] if product is nt else right[...]
-            part = product(left, right)
-            total = part if total is None else total + part
-        outs.append(total)
-    return outs
-
-
 def wide(terms, lefts, pieces, product, features, got):
     count = lefts[0].shape[0]
-    per = count // 4
+    half, per = count // 2, count // 4
+    depth = features // 4
     given = got is None
-    here = (lambda i: (i + 2, 0)) if given else (lambda i: (1 - i, 0))
+    used = len(pieces)
     inputs = list(lefts) + [piece for group in pieces for piece in group]
-    in_specs = [pl.BlockSpec((per, left.shape[1]), here) for left in lefts]
-    in_specs += [whole(piece) for group in pieces for piece in group]
-    flops = 2 * (count // 2) * features * sum(term[4] for term in terms)
+    in_specs = [pl.BlockSpec((half, left.shape[1]), (lambda i: (1, 0)) if given else (lambda i: (0, 0))) for left in lefts]
+    in_specs += [pl.BlockSpec(memory_space=pl.ANY)] * (4 * used)
+    flops = 2 * half * features * sum(term[4] for term in terms)
     moved = 2 * sum(piece.size for group in pieces for piece in group) + 6 * count * features
-    depth = features // 4
+    skip = len(lefts) + 4 * used
+
+    def body(*refs):
+        held, sems = refs[-1 - used : -1], refs[-1]
+
+        def copy(number, piece):
+            source = refs[len(lefts) + 4 * number + piece]
+            return pltpu.make_async_copy(source, held[number].at[piece], sems.at[number, piece])
+
+        for piece in range(4):
+            for number in range(used):
+                copy(number, piece).start()
+        for piece in range(4):
+            columns = slice(piece * depth, piece * depth + depth)
+            for number in range(used):
+                copy(number, piece).wait()
+            for strip in range(2):
+                rows = slice(strip * per, strip * per + per)
+                total = None
+                for number, begin, weight, first, size in terms:
+                    left = refs[number][rows, begin : begin + size]
+                    right = held[weight][piece]
+                    right = right[:, first : first + size] if product is nt else right
+                    part = product(left, right)
+                    total = part if total is None else total + part
+                if given:
+                    refs[skip][rows, columns] = total.astype(bf)
+                else:
+                    total = total + refs[skip][rows, columns].astype(f32)
+                    if strip == 0:
+                        refs[skip + 2][:, columns] = total
+                    else:
+                        refs[skip + 1][:, columns] = total.astype(bf)
+
+    scratch = [pltpu.VMEM((4,) + group[0].shape, bf) for group in pieces] + [pltpu.SemaphoreType.DMA((used, 4))]
     if given:
-
-        def body(*refs):
-            for piece, total in enumerate(widen(terms, refs, product)):
-                refs[-1][:, piece * depth : piece * depth + depth] = total.astype(bf)
-
-        return call(
-            body, (2,), in_specs, pl.BlockSpec((per, features), lambda i: (i, 0)),
-            jax.ShapeDtypeStruct((count // 2, features), bf), flops, moved, "wide_given", inputs,
-        )
-
-    def body(*refs):
-        got_ref, there, own = refs[-3:]
-        totals = widen(terms, refs, product)
-        for piece, total in enumerate(totals):
-            columns = slice(piece * depth, piece * depth + depth)
-            total = total + got_ref[:, columns].astype(f32)
-
-            @pl.when(pl.program_id(0) == 0)
-            def _():
-                there[:, columns] = total.astype(bf)
-
-            @pl.when(pl.program_id(0) == 1)
-            def _():
-                own[:, columns] = total
-
+        out_specs = pl.BlockSpec((half, features), lambda i: (0, 0))
+        out_shape = jax.ShapeDtypeStruct((half, features), bf)
+    else:
+        in_specs.append(pl.BlockSpec((half, features), lambda i: (0, 0)))
+        inputs.append(got)
+        out_specs = [pl.BlockSpec((per, features), lambda i: (0, 0))] * 2
+        out_shape = [jax.ShapeDtypeStruct((per, features), bf), jax.ShapeDtypeStruct((per, features), f32)]
     return call(
-        body, (2,), in_specs + [pl.BlockSpec((per, features), here)],
-        [pl.BlockSpec((per, features), lambda i: (0, 0))] * 2,
-        [jax.ShapeDtypeStruct((per, features), bf), jax.ShapeDtypeStruct((per, features), f32)],
-        flops, moved, "wide_kept", inputs + [got],
+        body, (1,), in_specs, out_specs, out_shape, flops, moved, "wide_given" if given else "wide_kept", inputs, scratch
     )
 
 
@@ -850,40 +857,53 @@
             self.turn == 0, jnp.concatenate([first, second], axis=axis), jnp.concatenate([second, first], axis=axis)
         )
 
-    def spread(self, blob, axis, upward):
-        keep, give = blob
-        give, line = self.queued(give, "turn", DEPTH)
-        line.append(self.turned(give))
-        chunk = self.ordered(keep, line[-1], axis)
+    def tie(self, values, *others):
+        return lax.optimization_barrier((values, *others))[0]
+
+    def spread_far(self, chunk, axis, *others):
         for bit in self.far_bits():
             sent, line = self.queued(chunk, "far", DEPTH)
             line.append(self.flip(sent, bit))
+            line[-1] = self.tie(line[-1], *others)
             chunk = jnp.concatenate([chunk, line[-1]], axis=axis)
+        return chunk
+
+    def spread_ring(self, chunk, upward):
         ahead = self.ring(chunk, -1)
         behind = self.ring(chunk, 1)
         across = self.ring(behind, 1) if upward else self.ring(ahead, -1)
         return [chunk, ahead, across, behind]
 
     def collect_ring(self, make, upward):
+        across = make(2).astype(bf)
         if upward:
-            up = self.ring(make(2).astype(bf), 1)
-            down = self.ring(make(3).astype(bf), -1)
-            up = self.ring((make(1) + up).astype(bf), 1)
-        else:
-            down = self.ring(make(2).astype(bf), -1)
-            up = self.ring(make(1).astype(bf), 1)
-            down = self.ring((make(3) + down).astype(bf), -1)
-        return make(0) + up + down
-
-    def collect_rest(self, own, axis):
+            behind = make(3).astype(bf)
+            up = self.ring(across, 1)
+            down = self.ring(behind, -1)
+            last = self.ring((make(1) + up).astype(bf), 1)
+            return make(0) + last + down, (across, behind), (up, down, last)
+        ahead = make(1).astype(bf)
+        down = self.ring(across, -1)
+        up = self.ring(ahead, 1)
+        last = self.ring((make(3) + down).astype(bf), -1)
+        return make(0) + up + last, (across, ahead), (down, up, last)
+
+    def collect_far(self, own, axis):
         for bit in reversed(list(self.far_bits())):
             half = own.shape[axis] // 2
             sent = lax.slice_in_dim(own, half, 2 * half, axis=axis)
-            own = lax.slice_in_dim(own, 0, half, axis=axis) + self.flip(sent.astype(bf), bit)
+            own = lax.slice_in_dim(own, 0, half, axis=axis), self.flip(sent.astype(bf), bit)
+            if bit > 8:
+                own = own[0] + own[1]
+        return own
+
+    def collect_last(self, own, axis, *others):
+        if isinstance(own, tuple):
+            own = own[0] + self.tie(own[1], *others)
         half = own.shape[axis] // 2
         mine = lax.dynamic_slice_in_dim(own, self.turn * half, half, axis)
         other = lax.dynamic_slice_in_dim(own, (1 - self.turn) * half, half, axis)
-        return mine, self.turned(other.astype(bf)).astype(f32)
+        return mine, self.turned(other.astype(bf))
 
     def joined(self, mine, theirs, axis):
         return self.ordered(jnp.concatenate(mine, axis=axis), jnp.concatenate(theirs, axis=axis), axis)
@@ -898,11 +918,14 @@
         there, own = wide(terms, lefts, pieces, product, features, self.crossed(given))
         return own + self.turned(there)
 
-    def everywhere(self, values):
+    def everywhere(self, values, marks):
+        bits = []
         bit = 1
         while bit < self.ways:
-            values = values + self.flip(values, bit)
+            bits.append(bit)
             bit *= 2
+        for bit in reversed(bits):
+            values = values + self.tie(self.flip(values, bit), *marks)
         return values + self.crossed(values)
 
 
@@ -963,23 +986,37 @@
     ]
     first_join = [(0, 0, keys), (1, 0, keys), (2, 0, vals), (3, 0, vals)]
     second_join = [(0, keys, 2 * keys), (1, keys, 2 * keys), (2, vals, 2 * vals), (3, vals, 2 * vals)]
-    blob_first, blob_second = picked(
-        turn, [w_query, w_key, w_value, w_gate], [1] * 4, [first_join, second_join]
-    )
-    blob_first = tuple(jnp.concatenate([blob, extra], axis=1) for blob, extra in zip(blob_first, lanes_of))
     out_rows, hidden_here = w_out.shape[0] // 2, w_mlp_gate.shape[1] // 2
     block = features // lay.ways
-    blob_out, blob_gate, blob_up, blob_down = picked(
-        turn, [w_out, w_mlp_gate, w_mlp_up, w_mlp_down], [0, 1, 1, 0],
-        [[(0, 0, block)], [(1, 0, hidden_here)], [(2, 0, hidden_here)], [(3, 0, block)]],
-    )
-    got_tokens = exchange(send_tokens)
-    in_first = lay.spread(blob_first, 0, True)
-    in_second = lay.spread(blob_second, 0, False)
-    out_pieces = lay.spread(blob_out, 1, True)
-    gate_pieces = lay.spread(blob_gate, 0, False)
-    up_pieces = lay.spread(blob_up, 0, True)
-    down_pieces = lay.spread(blob_down, 1, False)
+    mixed_join = []
+    for start in range(0, hidden_here, LANES):
+        mixed_join += [(0, start, start + LANES), (1, start, start + LANES)]
+    blob_first, (second_keep, second_give) = picked(
+        turn, [w_query, w_key, w_value, w_gate], [1] * 4, [first_join, second_join]
+    )
+    first_keep, first_give = [
+        jnp.concatenate([blob, extra], axis=1) for blob, extra in zip(blob_first, lanes_of)
+    ]
+    first_got = lay.turned(first_give)
+    got_tokens = exchange(lay.tie(send_tokens, first_got))
+    first_chunk = lay.spread_far(lay.ordered(first_keep, first_got, 0), 0)
+    second_got = lay.turned(lay.tie(second_give, first_chunk))
+    [(feed_keep, feed_give)] = picked(turn, [w_mlp_gate, w_mlp_up], [1, 1], [mixed_join])
+
+    def half_rows(weight):
+        half = weight.shape[0] // 2
+        return [lax.dynamic_slice_in_dim(weight, place * half, half, 0) for place in (lay.turn, 1 - lay.turn)]
+
+    out_keep, out_give = half_rows(w_out)
+    down_keep, down_give = half_rows(w_mlp_down)
+    tall_got = lay.turned(lay.tie(jnp.concatenate([out_give, down_give], axis=0), second_got))
+    feed_got = lay.turned(lay.tie(feed_give, second_got))
+    second_chunk = lay.spread_far(lay.ordered(second_keep, second_got, 0), 0)
+    in_first = lay.spread_ring(first_chunk, True)
+    tall_got = lay.tie(tall_got, in_first[1], in_first[3])
+    out_chunk = lay.spread_far(lay.ordered(out_keep, tall_got[:out_rows], 1), 1)
+    in_second = lay.spread_ring(second_chunk, False)
+    out_pieces = lay.spread_ring(out_chunk, True)
 
     got_slot = got_tokens[:, features].astype(jnp.int32)
     landing = (places[:, None] + 1 == got_slot[None, :]).astype(bf)
@@ -1018,6 +1055,7 @@
     scale_one = lax.rsqrt(jnp.mean(x_own * x_own, axis=1, keepdims=True) + EPS_ROW)
     first_rows = lay.rows_of((x_own * scale_one * gains[0]).astype(bf))
     proj_first, decays = project(first_rows, in_first, width, True)
+    feed_chunk = lay.spread_far(lay.ordered(feed_keep, lay.tie(feed_got, first_rows), 0), 0, proj_first)
     heads_out, states_first, inverses_first = mixer_forward(
         0, heads, core, proj_first, decays, marks, seg_rows, taps[0], params, gain_row, None
     )
@@ -1025,61 +1063,71 @@
     heads_out, states_second, inverses_second = mixer_forward(
         pair, heads, core, proj_second, decays, marks, seg_rows, taps[1], params, gain_row, heads_out
     )
-    mixed_own = lay.own_of([(0, 0, 1, 0, out_rows)], [heads_out], [out_pieces], nn, features)
+    mixed_own = lay.own_of([(0, 0, 0, 0, out_rows)], [lay.tie(heads_out, feed_chunk)], [out_pieces], nn, features)
     middle = x_own + live_own * mixed_own
 
-    got_cot = exchange(send_cot)
-    dy_own = matmul(matmul(landing, got_cot).astype(bf), turning)
+    got_cot = exchange(lay.tie(send_cot, in_second[2]))
+    scale_two = lax.rsqrt(jnp.mean(middle * middle, axis=1, keepdims=True) + EPS_ROW)
+    second_own_rows = (middle * scale_two * gains[1]).astype(bf)
+    second_rows = lay.rows_of(second_own_rows)
+    feed_behind = lay.ring(feed_chunk, 1)
+    feed_ahead = lay.ring(feed_chunk, -1)
+    feed_across = lay.ring(lay.tie(feed_ahead, second_own_rows), -1)
+    feed_pieces = [feed_chunk, feed_ahead, feed_across, feed_behind]
+    down_chunk = lay.spread_far(lay.ordered(down_keep, tall_got[out_rows:], 1), 1, second_own_rows)
+    down_pieces = lay.spread_ring(down_chunk, True)
+    dy_own = matmul(matmul(landing, lay.tie(got_cot, mixed_own)).astype(bf), turning)
     branch_rows = lay.rows_of((live_own * dy_own).astype(bf))
-    scale_two = lax.rsqrt(jnp.mean(middle * middle, axis=1, keepdims=True) + EPS_ROW)
-    second_rows = lay.rows_of((middle * scale_two * gains[1]).astype(bf))
-    gate_pre, up_proj, hidden = feed_forward(second_rows, gate_pieces, up_pieces)
+    pre, hidden = feed_forward(second_rows, feed_pieces)
     depth = features // 4
 
     def columns_of(rows, piece):
         return rows[:, piece * depth : piece * depth + depth]
 
-    down_own = lay.collect_ring(lambda r: outer_sum(hidden, columns_of(branch_rows, r)), True)
-    grad_gate, grad_up = feed_backward(branch_rows, down_pieces, gate_pre, up_proj)
-    gate_own = lay.collect_ring(lambda r: outer_sum(columns_of(second_rows, r), grad_gate), False)
-    up_own = lay.collect_ring(lambda r: outer_sum(columns_of(second_rows, r), grad_up), True)
-    grad_second = lay.own_of(
-        [(0, 0, 2, 0, hidden_here), (1, 0, 6, 0, hidden_here)],
-        [grad_gate, grad_up], [gate_pieces, up_pieces], nt, features,
-    )
+    down_own, down_terms, down_sent = lay.collect_ring(lambda r: outer_sum(hidden, columns_of(branch_rows, r)), True)
+    grad_pre = feed_backward(lay.tie(branch_rows, *down_terms), down_pieces, pre)
+    feed_own, feed_terms, feed_sent = lay.collect_ring(
+        lambda r: outer_sum(columns_of(second_rows, r), grad_pre), False
+    )
+    grad_second = lay.own_of([(0, 0, 0, 0, 2 * hidden_here)], [grad_pre], [feed_pieces], nt, features)
     grad_mid_norm, gain_two_grad = norm_back(middle, scale_two, gains[1], grad_second)
     grad_middle = dy_own + grad_mid_norm
     mix_rows = lay.rows_of((live_own * grad_middle).astype(bf))
 
-    grad_heads = heads_backward(mix_rows, out_pieces)
-    out_own = lay.collect_ring(lambda r: outer_sum(heads_out, columns_of(mix_rows, r)), False)
+    grad_heads = heads_backward(lay.tie(mix_rows, feed_sent[0]), out_pieces)
+    out_own, out_terms, out_sent = lay.collect_ring(lambda r: outer_sum(heads_out, columns_of(mix_rows, r)), True)
     grad_proj_first, taps_first, params_first, gain_first = mixer_backward(
-        0, heads, core, proj_first, decays, grad_heads, marks, seg_rows, taps[0], params, gain_row,
-        states_first, inverses_first, None,
-    )
-    first_own = lay.collect_ring(
+        0, heads, core, proj_first, decays, lay.tie(grad_heads, *out_terms), marks, seg_rows, taps[0], params,
+        gain_row, states_first, inverses_first, None,
+    )
+    first_own, first_terms, first_sent = lay.collect_ring(
         lambda r: outer_sum(columns_of(first_rows, r), grad_proj_first[:, :width]), True
     )
     grad_proj_second, taps_second, params_second, gain_second = mixer_backward(
-        pair, heads, core, proj_second, decays, grad_heads, marks, seg_rows, taps[1], params, gain_row,
-        states_second, inverses_second, grad_proj_first,
-    )
-    second_own = lay.collect_ring(lambda r: outer_sum(columns_of(first_rows, r), grad_proj_second), False)
+        pair, heads, core, proj_second, decays, lay.tie(grad_heads, feed_sent[1], *first_terms), marks, seg_rows,
+        taps[1], params, gain_row, states_second, inverses_second, grad_proj_first,
+    )
+    second_own, second_terms, second_sent = lay.collect_ring(
+        lambda r: outer_sum(columns_of(first_rows, r), grad_proj_second), False
+    )
     grad_first = lay.own_of(
-        [(0, 0, 2, 0, width), (1, 0, 6, 0, width), (1, width, 2, width, LANES)],
-        [grad_proj_first, grad_proj_second], [in_first, in_second], nt, features,
+        [(0, 0, 0, 0, width), (1, 0, 1, 0, width), (1, width, 0, width, LANES)],
+        [grad_proj_first, lay.tie(grad_proj_second, feed_sent[2], out_sent[0], *second_terms)],
+        [in_first, in_second], nt, features,
     )
     grad_x_norm, gain_one_grad = norm_back(x_own, scale_one, gains[0], grad_first)
     grad_tokens = (grad_middle + grad_x_norm).astype(bf)
 
-    def sent_back(own):
+    def sent_out(own, *others):
         straight = times_back(own, turning).astype(bf)
-        back = exchange(outer_sum(landing, straight).astype(bf))
-        return outer_sum(sending, back).astype(bf)
-
-    branch_own = lay.own_of([(0, 0, 1, 0, hidden_here)], [hidden], [down_pieces], nn, features)
-    output = sent_back((middle + live_own * branch_own).astype(bf))
-    tokens_grad = sent_back(grad_tokens)
+        return exchange(lay.tie(outer_sum(landing, straight).astype(bf), *others))
+
+    def sent_home(back, *others):
+        return outer_sum(sending, lay.tie(back, *others)).astype(bf)
+
+    branch_own = lay.own_of([(0, 0, 0, 0, hidden_here)], [lay.tie(hidden, feed_terms[0], grad_second)], [down_pieces], nn, features)
+    output = sent_home(sent_out((middle + live_own * branch_own).astype(bf), out_sent[0]), first_sent[2])
+    tokens_grad = sent_home(sent_out(grad_tokens), *second_sent[1:])
 
     conv_full = jnp.zeros(conv_weights.shape, f32)
     for cut, grad in zip(cuts, (taps_first, taps_second)):
@@ -1091,17 +1139,24 @@
     log_full = lax.dynamic_update_slice_in_dim(jnp.zeros_like(a_log), params_grad[0, :heads], share * heads, 0)
     bias_full = lax.dynamic_update_slice_in_dim(jnp.zeros_like(dt_bias), params_grad[1, :heads], share * heads, 0)
     gain_grad = gain_first[0] + gain_second[0]
-    sums = flat([conv_full, straight_gain(gain_two_grad), gain_grad, log_full, bias_full])
-    sums = lay.everywhere(sums).reshape(-1)
-    late = lay.everywhere(flat([straight_gain(gain_one_grad)])).reshape(-1)[:features]
+    norm_grads = jnp.stack([straight_gain(gain_one_grad), straight_gain(gain_two_grad)])
+    sums = flat([conv_full, norm_grads, gain_grad, log_full, bias_full])
+    sums = lay.everywhere(sums, second_sent[1:]).reshape(-1)
     ends = [conv_full.size]
-    for size in (features, DV, all_heads, all_heads):
+    for size in (2 * features, DV, all_heads, all_heads):
         ends.append(ends[-1] + size)
-    norm_grad = jnp.stack([late, sums[ends[0] : ends[1]]])
-
-    gate_grad, up_grad = lay.collect_rest(gate_own, 0), lay.collect_rest(up_own, 0)
-    down_grad, out_grad = lay.collect_rest(down_own, 1), lay.collect_rest(out_own, 1)
-    first_grad, second_grad = lay.collect_rest(first_own, 0), lay.collect_rest(second_own, 0)
+    norm_grad = sums[ends[0] : ends[1]].reshape(2, features)
+
+    end = second_sent[1:]
+    down_grad = lay.collect_last(lay.collect_far(down_own, 1), 1, feed_sent[2])
+    first_grad = lay.collect_last(lay.collect_far(first_own, 0), 0, *end)
+    second_grad = lay.collect_last(lay.collect_far(second_own, 0), 0)
+    feed_grad = lay.collect_last(lay.collect_far(feed_own, 0), 0, *end)
+    out_grad = lay.collect_last(lay.collect_far(out_own, 1), 1, *end)
+    down_grad, feed_grad, out_grad = [
+        (mine, lay.tie(theirs, *end).astype(f32)) for mine, theirs in (down_grad, feed_grad, out_grad)
+    ]
+    first_grad, second_grad = [(mine, theirs.astype(f32)) for mine, theirs in (first_grad, second_grad)]
     in_grads = []
     begin = 0
     for size in (keys, keys, vals, vals):
@@ -1113,6 +1168,10 @@
     for size in (heads, heads):
         in_grads.append(lay.joined(*[[grad[:, begin : begin + size]] for grad in second_grad], 1))
         begin += size
+
+    def alternate(grad, part):
+        return grad.reshape(grad.shape[0], -1, 2, LANES)[:, :, part].reshape(grad.shape[0], -1)
+
     return (
         output,
         tokens_grad,
@@ -1123,8 +1182,7 @@
         sums[ends[3] : ends[4]],
         sums[ends[1] : ends[2]],
         lay.ordered(*out_grad, 0),
-        lay.ordered(*gate_grad, 1),
-        lay.ordered(*up_grad, 1),
+        *[lay.ordered(*[alternate(grad, part) for grad in feed_grad], 1) for part in (0, 1)],
         lay.ordered(*down_grad, 0),
     )
 

time: 1140 us -> 1100 us (0.965)
  waiting for transfers between devices: 525 us -> 475 us
  local copies, waits for them, and re-layouts: 38.4 us -> 73 us
  starting transfers between devices: 114 us -> 92.7 us
    ppermute x41 -> x32, waiting for transfers between devices: 465 us -> 260 us  [flip(): return lax.ppermute(values, 'dp', [(n, n ^ bit) for n in range(self.ways)])]
    ppermute x36 -> x30, waiting for transfers between devices: 59.9 us -> 154 us  [ring(): line.append(lax.ppermute(values, 'dp', pairs))]
    all_to_all x4, waiting for transfers between devices: 0.01 us -> 59.6 us  [exchange(): lax.all_to_all(values, ('dp', 'tensor'), split_axis=0, concat_axis=0, til...]
    slice x7 -> x12, local copies, waits for them, and re-layouts: 2.37 us -> 14.7 us  [the longest x4 6.6 us: alternate(): grad.reshape(grad.shape[0], -1, 2, LANES)[:, :, part]]
    ppermute x41 -> x32, starting transfers between devices: 51.3 us -> 40.7 us  [flip(): return lax.ppermute(values, 'dp', [(n, n ^ bit) for n in range(self.ways)])]
    ppermute x36 -> x30, starting transfers between devices: 42.5 us -> 37.8 us  [ring(): line.append(lax.ppermute(values, 'dp', pairs))]
    dot_general x28 -> x24, matrix products: 113 us -> 115 us  [outer_sum(): lax.dot_general(left, right, (((0,), (0,)), ((), ())), preferred_element_...]
  transfers between devices with their start and end apart: 95 -> 79, of which waited for: 34 -> 36; matrix products, arithmetic and copies ran while one was open for 18% -> 22% of each run, Pallas kernels for 22% -> 19%
where the time goes in v3:
time: 1100 us; the launch traced here: 1090 us
  waiting for transfers between devices  475 us (43%)
  Pallas kernels  242 us (22%)
  matrix products  129 us (12%)
  starting transfers between devices  92.7 us (8%)
  local copies, waits for them, and re-layouts  73 us (7%)
  other arithmetic  71.5 us (6%)
    ppermute x32, waiting for transfers between devices, flip(): return lax.ppermute(values, 'dp', [(n, n ^ bit) for n in range(self.ways)])  260 us
    ppermute x30, waiting for transfers between devices, ring(): line.append(lax.ppermute(values, 'dp', pairs))  154 us
    pallas_call x13, Pallas kernels, call(): pl.pallas_call(body, grid=grid, scratch_shapes=scratch, in_specs=in_specs...  147 us
    dot_general x24, matrix products, outer_sum(): lax.dot_general(left, right, (((0,), (0,)), ((), ())), preferred_element_...  115 us
    all_to_all x4, waiting for transfers between devices, exchange(): lax.all_to_all(values, ('dp', 'tensor'), split_axis=0, concat_axis=0, til...  59.6 us
    pallas_call x2, Pallas kernels, mixer_backward(): pl.pallas_call(body, grid_spec=pltpu.PrefetchScalarGridSpec(num_scalar_pr...  58.4 us
    ppermute x32, starting transfers between devices, flip(): return lax.ppermute(values, 'dp', [(n, n ^ bit) for n in range(self.ways)])  40.7 us
    ppermute x30, starting transfers between devices, ring(): line.append(lax.ppermute(values, 'dp', pairs))  37.8 us
  transfers between devices with their start and end apart: 79, of which 36 were waited for; matrix products, arithmetic and copies ran while one was open for 22% of the time, Pallas kernels for 19%

profile of v3, /device:TPU:0, one launch (start us, length us, event | category | flops | bytes accessed | tf_op | source)
XLA Modules:
  0.0 1085.3 jit_solution(4293612832762670462)
XLA Ops:
  35.0 51.2 %collective-permute-done.5 = bf16[256,1664]{1,0:T(8,128)(2,1)} collective-permute-done((bf16[256,1664]{1,0:T(8,128)(2,1)}, bf16[256,1664]{1,0:T(8,128)(2,1)}, u32[]{:S(2)}, u32[]{:S(2)}) %collective-permute-start.5) | collective-permute-done | bytes 852000 | tf_op jit(solution)/shard_map/ppermute | solution.py:834
  97.5 13.3 %collective-permute-done.6 = bf16[128,1536]{1,0:T(8,128)(2,1)S(1)} collective-permute-done((bf16[128,1536]{1,0:T(8,128)(2,1)S(1)}, bf16[128,1536]{1,0:T(8,128)(2,1)S(1)}, u32[]{:S(2)}, u32[]{:S(2)}) %collective-permute-start.6) | collective-permute-done | bytes 393248 | tf_op jit(solution)/shard_map/ppermute | solution.py:834
  112.2 20.4 %collective-permute-done.11.refs_3_.refs_7_.refs_5_ = bf16[512,1664]{1,0:T(8,128)(2,1)} collective-permute-done((bf16[512,1664]{1,0:T(8,128)(2,1)}, bf16[512,1664]{1,0:T(8,128)(2,1)}, u32[]{:S(2)}, u32[]{:S(2)}) %collective-permute-start.11) | collective-permute-done | bytes 1703968 | tf_op jit(solution)/shard_map/ppermute | solution.py:830
  151.4 32.7 %collective-permute-done.15 = bf16[2432,128]{1,0:T(8,128)(2,1)} collective-permute-done((bf16[2432,128]{1,0:T(8,128)(2,1)}, bf16[2432,128]{1,0:T(8,128)(2,1)}, u32[]{:S(2)}, u32[]{:S(2)}) %collective-permute-start.15) | collective-permute-done | bytes 622624 | tf_op jit(solution)/shard_map/ppermute | solution.py:834
  189.6 21.4 %collective-permute-done.16 = bf16[1024,256]{1,0:T(8,128)(2,1)S(1)} collective-permute-done((bf16[1024,256]{1,0:T(8,128)(2,1)S(1)}, bf16[1024,256]{1,0:T(8,128)(2,1)S(1)}, u32[]{:S(2)}, u32[]{:S(2)}) %collective-permute-start.16) | collective-permute-done | bytes 524320 | tf_op jit(solution)/shard_map/ppermute | solution.py:834
  218.6 12.8 %project.3 = (bf16[1024,1536]{1,0:T(8,128)(2,1)}, f32[1024,128]{1,0:T(8,128)}) custom-call(bf16[1024,2048]{1,0:T(8,128)(2,1)} %pad_maximum_fusion.rows_ref, bf16[512,1664]{1,0:T(8,128)(2,1)} %pad_maximum_fusion.5.refs_0_.refs_4_.refs_2_, bf16[512,1664]{1,0:T(8,128)(2,1)} %collective-permute-done.8.refs_1_.refs_5_.refs_3_, ...), custom_call_target="tpu_custom_call" | custom-call | flops 6442450944 | bytes 13631488 | tf_op jit(solution)/shard_map/project/pallas_call | solution.py:581
  231.4 16.2 %collective-permute-done.13.refs_3_.refs_9_ = bf16[512,1536]{1,0:T(8,128)(2,1)} collective-permute-done((bf16[512,1536]{1,0:T(8,128)(2,1)}, bf16[512,1536]{1,0:T(8,128)(2,1)}, u32[]{:S(2)}, u32[]{:S(2)}) %collective-permute-start.13) | collective-permute-done | bytes 1572896 | tf_op jit(solution)/shard_map/ppermute | solution.py:830
  248.5 16.1 %mixer_forward.2 = (bf16[2,2,2,128,1024]{4,3,2,1,0:T(8,128)(2,1)}, bf16[4,4,128,256]{3,2,1,0:T(8,128)(2,1)}, bf16[4,4,128,128]{3,2,1,0:T(8,128)(2,1)}) custom-call(s32[1]{0:T(128)} %bitcast.3.refs_0_.core_ref, bf16[2,2,2,128,1536]{4,3,2,1,0:T(8,128)(2,1)} %bitcast.129, f32[2,2,2,128,128]{4,3,2,1,0:T(8,128)} %bitcast.134, ...), custom_call_target="tpu_custom_call" | custom-call | flops 16000000000 | bytes 16777216 | tf_op jit(solution)/shard_map/mixer_forward/pallas_call | solution.py:382
  265.7 11.4 %project.2 = bf16[1024,1536]{1,0:T(8,128)(2,1)} custom-call(bf16[1024,2048]{1,0:T(8,128)(2,1)} %pad_maximum_fusion.rows_ref, bf16[512,1536]{1,0:T(8,128)(2,1)} %pad_maximum_fusion.6.refs_0_.refs_6_, bf16[512,1536]{1,0:T(8,128)(2,1)} %collective-permute-done.9.refs_1_.refs_7_, bf16[512,1536]{1,0:T(8,128)(2,1)} %collective-permute-done.10.refs_2_.refs_8_, ...), custom_call_target="tpu_custom_call" | custom-call | flops 6442450944 | bytes 13631488 | tf_op jit(solution)/shard_map/project/pallas_call | solution.py:581
  278.3 15.8 %mixer_forward.3 = (bf16[2,2,2,128,1024]{4,3,2,1,0:T(8,128)(2,1)}, bf16[4,4,128,256]{3,2,1,0:T(8,128)(2,1)}, bf16[4,4,128,128]{3,2,1,0:T(8,128)(2,1)}) custom-call(s32[1]{0:T(128)} %bitcast.3.refs_0_.core_ref, bf16[2,2,2,128,1536]{4,3,2,1,0:T(8,128)(2,1)} %bitcast.126, f32[2,2,2,128,128]{4,3,2,1,0:T(8,128)} %bitcast.135, ...), custom_call_target="tpu_custom_call", output_to_operand_aliasing={{0}: (8, {})} | custom-call | flops 16000000000 | bytes 16777216 | tf_op jit(solution)/shard_map/mixer_forward/pallas_call | solution.py:382
  329.5 33.8 %all-to-all-done.1 = bf16[32,10,2048]{2,1,0:T(8,128)(2,1)S(1)} async-done(((bf16[32,10,2048]{2,1,0:T(8,128)(2,1)}), bf16[32,10,2048]{2,1,0:T(8,128)(2,1)S(1)}, u32[]{:S(2)}, u32[]{:S(2)}) %all-to-all-start.1) | async-done | bytes 1310752 | tf_op jit(solution)/shard_map/all_to_all | solution.py:974
  364.6 20.1 %collective-permute-done.22 = bf16[256,2048]{1,0:T(8,128)(2,1)} collective-permute-done((bf16[256,2048]{1,0:T(8,128)(2,1)}, bf16[256,2048]{1,0:T(8,128)(2,1)}, u32[]{:S(2)}, u32[]{:S(2)}) %collective-permute-start.22) | collective-permute-done | bytes 1048608 | tf_op jit(solution)/shard_map/ppermute | solution.py:834
  416.3 22.3 %collective-permute-done.29 = bf16[256,2048]{1,0:T(8,128)(2,1)S(1)} collective-permute-done((bf16[256,2048]{1,0:T(8,128)(2,1)}, bf16[256,2048]{1,0:T(8,128)(2,1)S(1)}, u32[]{:S(2)}, u32[]{:S(2)}) %collective-permute-start.29) | collective-permute-done | bytes 1048608 | tf_op jit(solution)/shard_map/ppermute | solution.py:834
  444.2 22.6 %collective-permute-done.27.refs_2_.refs_3_ = bf16[512,2816]{1,0:T(8,128)(2,1)} collective-permute-done((bf16[512,2816]{1,0:T(8,128)(2,1)}, bf16[512,2816]{1,0:T(8,128)(2,1)}, u32[]{:S(2)}, u32[]{:S(2)}) %collective-permute-start.27) | collective-permute-done | bytes 2883616 | tf_op jit(solution)/shard_map/ppermute | solution.py:830
  467.1 18.7 %feed_forward.1 = (bf16[1024,2816]{1,0:T(8,128)(2,1)}, bf16[1024,1408]{1,0:T(8,128)(2,1)}) custom-call(bf16[1024,2048]{1,0:T(8,128)(2,1)} %pad_maximum_fusion.1.rows_ref, bf16[512,2816]{1,0:T(8,128)(2,1)} %pad_maximum_fusion.4.refs_0_.refs_1_, bf16[512,2816]{1,0:T(8,128)(2,1)} %collective-permute-done.26.refs_1_.refs_2_, ...), custom_call_target="tpu_custom_call" | custom-call | flops 11811160064 | bytes 27262976 | tf_op jit(solution)/shard_map/feed_forward/pallas_call | solution.py:581
  499.5 13.8 %feed_backward.1.refs_0_ = bf16[1024,2816]{1,0:T(8,128)(2,1)} custom-call(bf16[1024,2048]{1,0:T(8,128)(2,1)} %copy-done.20, bf16[1408,512]{1,0:T(8,128)(2,1)} %pad_maximum_fusion.7.refs_0_.refs_1_, bf16[1408,512]{1,0:T(8,128)(2,1)} %collective-permute-done.33.refs_1_.refs_2_, bf16[1408,512]{1,0:T(8,128)(2,1)} %collective-permute-done.35.refs_2_.refs_3_, ...), custom_call_target="tpu_custom_call" | custom-call | flops 5905580032 | bytes 21495808 | tf_op jit(solution)/shard_map/feed_backward/pallas_call | solution.py:581
  513.4 11.8 %wide_given.5 = bf16[512,2048]{1,0:T(8,128)(2,1)} custom-call(bf16[1024,2816]{1,0:T(8,128)(2,1)} %feed_backward.1.refs_0_, bf16[512,2816]{1,0:T(8,128)(2,1)} %pad_maximum_fusion.4.refs_0_.refs_1_, bf16[512,2816]{1,0:T(8,128)(2,1)} %collective-permute-done.26.refs_1_.refs_2_, bf16[512,2816]{1,0:T(8,128)(2,1)} %collective-permute-done.27.refs_2_.refs_3_, ...), custom_call_target="tpu_custom_call" | custom-call | flops 5905580032 | bytes 24117248 | tf_op jit(solution)/shard_map/wide_given/pallas_call | solution.py:581
  529.7 12.1 %wide_kept.5 = (bf16[256,2048]{1,0:T(8,128)(2,1)}, f32[256,2048]{1,0:T(8,128)}) custom-call(bf16[1024,2816]{1,0:T(8,128)(2,1)} %feed_backward.1.refs_0_, bf16[512,2816]{1,0:T(8,128)(2,1)} %pad_maximum_fusion.4.refs_0_.refs_1_, bf16[512,2816]{1,0:T(8,128)(2,1)} %collective-permute-done.26.refs_1_.refs_2_, ...), custom_call_target="tpu_custom_call" | custom-call | flops 5905580032 | bytes 24117248 | tf_op jit(solution)/shard_map/wide_kept/pallas_call | solution.py:581
  550.6 8.9 collective-permute-done.43
  587.9 9.5 collective-permute-done.44
  605.4 23.3 %collective-permute-done.48 = bf16[512,2816]{1,0:T(8,128)(2,1)} collective-permute-done((bf16[512,2816]{1,0:T(8,128)(2,1)}, bf16[512,2816]{1,0:T(8,128)(2,1)}, u32[]{:S(2)}, u32[]{:S(2)}) %collective-permute-start.48) | collective-permute-done | bytes 2883616 | tf_op jit(solution)/shard_map/ppermute | solution.py:830
  661.6 29.0 %mixer_backward.2 = (bf16[2,2,2,128,1664]{4,3,2,1,0:T(8,128)(2,1)}, f32[4,1024]{1,0:T(4,128)}, f32[8,128]{1,0:T(8,128)}, f32[8,256]{1,0:T(8,128)}) custom-call(s32[1]{0:T(128)} %bitcast.3.refs_0_.core_ref, bf16[2,2,2,128,1536]{4,3,2,1,0:T(8,128)(2,1)} %bitcast.130, bf16[2,2,2,128,1536]{4,3,2,1,0:T(8,128)(2,1)} %bitcast.131, ...), custom_call_target="tpu_custom_call" | custom-call | flops 30000001024 | bytes 31457280 | tf_op jit(solution)/shard_map/mixer_backward/pallas_call | solution.py:468
  700.7 29.4 %mixer_backward.3 = (bf16[2,2,2,128,1664]{4,3,2,1,0:T(8,128)(2,1)}, f32[4,1024]{1,0:T(4,128)}, f32[8,128]{1,0:T(8,128)}, f32[8,256]{1,0:T(8,128)}) custom-call(s32[1]{0:T(128)} %bitcast.3.refs_0_.core_ref, bf16[2,2,2,128,1536]{4,3,2,1,0:T(8,128)(2,1)} %bitcast.127, bf16[2,2,2,128,1536]{4,3,2,1,0:T(8,128)(2,1)} %bitcast.128, ...), custom_call_target="tpu_custom_call" | custom-call | flops 30000001024 | bytes 31457280 | tf_op jit(solution)/shard_map/mixer_backward/pallas_call | solution.py:468
  744.2 13.3 %wide_given.7 = bf16[512,2048]{1,0:T(8,128)(2,1)} custom-call(bf16[1024,1664]{1,0:T(8,128)(2,1)} %bitcast.121, bf16[1024,1664]{1,0:T(8,128)(2,1)} %bitcast.77, bf16[512,1664]{1,0:T(8,128)(2,1)} %pad_maximum_fusion.5.refs_0_.refs_4_.refs_2_, bf16[512,1664]{1,0:T(8,128)(2,1)} %collective-permute-done.8.refs_1_.refs_5_.refs_3_, ...), custom_call_target="tpu_custom_call" | custom-call | flops 6710886400 | bytes 25690112 | tf_op jit(solution)/shard_map/wide_given/pallas_call | solution.py:581
  783.2 9.4 collective-permute-done.49
  801.5 13.4 %wide_kept.7 = (bf16[256,2048]{1,0:T(8,128)(2,1)}, f32[256,2048]{1,0:T(8,128)}) custom-call(bf16[1024,1664]{1,0:T(8,128)(2,1)} %bitcast.122, bf16[1024,1664]{1,0:T(8,128)(2,1)} %bitcast.78, bf16[512,1664]{1,0:T(8,128)(2,1)} %pad_maximum_fusion.5.refs_0_.refs_4_.refs_2_, bf16[512,1664]{1,0:T(8,128)(2,1)} %collective-permute-done.8.refs_1_.refs_5_.refs_3_, ...), custom_call_target="tpu_custom_call" | custom-call | flops 6710886400 | bytes 25690112 | tf_op jit(solution)/shard_map/wide_kept/pallas_call | solution.py:581
  823.7 20.1 %collective-permute-done.57 = bf16[512,1536]{1,0:T(8,128)(2,1)} collective-permute-done((bf16[512,1536]{1,0:T(8,128)(2,1)}, bf16[512,1536]{1,0:T(8,128)(2,1)}, u32[]{:S(2)}, u32[]{:S(2)}) %collective-permute-start.57) | collective-permute-done | bytes 1572896 | tf_op jit(solution)/shard_map/ppermute | solution.py:830
  851.0 13.3 %collective-permute-done.54 = bf16[256,2048]{1,0:T(8,128)(2,1)S(1)} collective-permute-done((bf16[256,2048]{1,0:T(8,128)(2,1)}, bf16[256,2048]{1,0:T(8,128)(2,1)S(1)}, u32[]{:S(2)}, u32[]{:S(2)}) %collective-permute-start.54) | collective-permute-done | bytes 1048608 | tf_op jit(solution)/shard_map/ppermute | solution.py:834
  920.4 25.8 %all-to-all-done.3 = bf16[32,10,2048]{2,1,0:T(8,128)(2,1)S(1)} async-done(((bf16[32,10,2048]{2,1,0:T(8,128)(2,1)}), bf16[32,10,2048]{2,1,0:T(8,128)(2,1)S(1)}, u32[]{:S(2)}, u32[]{:S(2)}) %all-to-all-start.3) | async-done | bytes 1310752 | tf_op jit(solution)/shard_map/all_to_all | solution.py:974
  950.5 27.2 %collective-permute-done.69 = bf16[1024,256]{1,0:T(8,128)(2,1)} collective-permute-done((bf16[1024,256]{1,0:T(8,128)(2,1)S(1)}, bf16[1024,256]{1,0:T(8,128)(2,1)}, u32[]{:S(2)}, u32[]{:S(2)}) %collective-permute-start.69) | collective-permute-done | bytes 524320 | tf_op jit(solution)/shard_map/ppermute | solution.py:834
  981.8 14.7 %collective-permute-done.65 = bf16[256,1536]{1,0:T(8,128)(2,1)S(1)} collective-permute-done((bf16[256,1536]{1,0:T(8,128)(2,1)}, bf16[256,1536]{1,0:T(8,128)(2,1)S(1)}, u32[]{:S(2)}, u32[]{:S(2)}) %collective-permute-start.65) | collective-permute-done | bytes 786464 | tf_op jit(solution)/shard_map/ppermute | solution.py:834
  1024.9 12.9 %collective-permute-done.61 = f32[296,128]{1,0:T(8,128)S(1)} collective-permute-done((f32[296,128]{1,0:T(8,128)S(1)}, f32[296,128]{1,0:T(8,128)S(1)}, u32[]{:S(2)}, u32[]{:S(2)}) %collective-permute-start.61) | collective-permute-done | bytes 151584 | tf_op jit(solution)/shard_map/ppermute | solution.py:834
  (541 shorter events, 466.2 us)
Async XLA Ops:
  0.7 94.8 %collective-permute-start.1 = (s32[1,4]{1,0:T(1,128)}, s32[1,4]{1,0:T(1,128)}, u32[]{:S(2)}, u32[]{:S(2)}) collective-permute-start(s32[1,4]{1,0:T(1,128)} %param.21), channel_id=1, source_target_pairs={{0,8},{2,10},{4,12},{6,14},{8,0},{10,2},{12,4},{14,6},{16,24},{18,... | collective-permute-start | bytes 56 | tf_op jit(solution)/shard_map/ppermute | solution.py:834
  23.2 63.0 %collective-permute-start.5 = (bf16[256,1664]{1,0:T(8,128)(2,1)}, bf16[256,1664]{1,0:T(8,128)(2,1)}, u32[]{:S(2)}, u32[]{:S(2)}) collective-permute-start(bf16[256,1664]{1,0:T(8,128)(2,1)} %maximum_select_fusion.7), channel_id=1, source_target_pairs={{0,16},{2,18},{4,20},{6,22},{8,24},{10,26},{12,28},{14,30},{16,0},... | collective-permute-start | bytes 2555912 | tf_op jit(solution)/shard_map/ppermute | solution.py:834
  28.6 106.3 %all-to-all-start = ((bf16[32,10,2176]{2,1,0:T(8,128)(2,1)}), bf16[32,10,2176]{2,1,0:T(8,128)(2,1)S(1)}, u32[]{:S(2)}, u32[]{:S(2)}) async-start(bf16[32,10,2176]{2,1,0:T(8,128)(2,1)} %all_to_all.32), calls=%async_computation | async-start | bytes 4456448 | tf_op jit(solution)/shard_map/all_to_all | solution.py:974
  96.9 54.0 %collective-permute-start.8 = (bf16[512,1664]{1,0:T(8,128)(2,1)}, bf16[512,1664]{1,0:T(8,128)(2,1)}, u32[]{:S(2)}, u32[]{:S(2)}) collective-permute-start(bf16[512,1664]{1,0:T(8,128)(2,1)} %pad_maximum_fusion.5.refs_0_.refs_4_.refs_2_), channel_id=1, source_target_pairs={{0,4},{2,0},{4,6},{6,2},{8,12},{10,8},{12,14},{14,10},{16,20},{18,... | collective-permute-start | bytes 5111816 | tf_op jit(solution)/shard_map/ppermute | solution.py:830
  132.6 56.1 %collective-permute-start.12 = (bf16[512,1664]{1,0:T(8,128)(2,1)}, bf16[512,1664]{1,0:T(8,128)(2,1)}, u32[]{:S(2)}, u32[]{:S(2)}) collective-permute-start(bf16[512,1664]{1,0:T(8,128)(2,1)} %collective-permute-done.11.refs_3_.refs_7_.refs_5_), channel_id=1, source_target_pairs={{0,2},{2,6},{4,0},{6,4},{8,10},{10,14},{12,8},{14,12},{16,18},{18,... | collective-permute-start | bytes 5111816 | tf_op jit(solution)/shard_map/ppermute | solution.py:830
  151.0 61.7 %collective-permute-start.9 = (bf16[512,1536]{1,0:T(8,128)(2,1)}, bf16[512,1536]{1,0:T(8,128)(2,1)}, u32[]{:S(2)}, u32[]{:S(2)}) collective-permute-start(bf16[512,1536]{1,0:T(8,128)(2,1)} %pad_maximum_fusion.6.refs_0_.refs_6_), channel_id=1, source_target_pairs={{0,4},{2,0},{4,6},{6,2},{8,12},{10,8},{12,14},{14,10},{16,20},{18,... | collective-permute-start | bytes 4718600 | tf_op jit(solution)/shard_map/ppermute | solution.py:830
  212.7 51.9 %collective-permute-start.10 = (bf16[512,1536]{1,0:T(8,128)(2,1)}, bf16[512,1536]{1,0:T(8,128)(2,1)}, u32[]{:S(2)}, u32[]{:S(2)}) collective-permute-start(bf16[512,1536]{1,0:T(8,128)(2,1)} %collective-permute-done.9.refs_1_.refs_7_), channel_id=1, source_target_pairs={{0,4},{2,0},{4,6},{6,2},{8,12},{10,8},{12,14},{14,10},{16,20},{18,... | collective-permute-start | bytes 4718600 | tf_op jit(solution)/shard_map/ppermute | solution.py:830
  218.5 75.5 %collective-permute-start.17 = (bf16[256,2816]{1,0:T(8,128)(2,1)S(1)}, bf16[256,2816]{1,0:T(8,128)(2,1)S(1)}, u32[]{:S(2)}, u32[]{:S(2)}) collective-permute-start(bf16[256,2816]{1,0:T(8,128)(2,1)S(1)} %maximum_select_fusion), channel_id=1, source_target_pairs={{0,16},{2,18},{4,20},{6,22},{8,24},{10,26},{12,28},{14,30},{16,0},... | collective-permute-start | bytes 4325384 | tf_op jit(solution)/shard_map/ppermute | solution.py:834
  310.8 52.5 %all-to-all-start.1 = ((bf16[32,10,2048]{2,1,0:T(8,128)(2,1)}), bf16[32,10,2048]{2,1,0:T(8,128)(2,1)S(1)}, u32[]{:S(2)}, u32[]{:S(2)}) async-start(bf16[32,10,2048]{2,1,0:T(8,128)(2,1)} %all_to_all.35), calls=%async_computation.1 | async-start | bytes 4194304 | tf_op jit(solution)/shard_map/all_to_all | solution.py:974
  313.6 87.1 %collective-permute-start.28 = (bf16[512,2816]{1,0:T(8,128)(2,1)}, bf16[512,2816]{1,0:T(8,128)(2,1)}, u32[]{:S(2)}, u32[]{:S(2)}) collective-permute-start(bf16[512,2816]{1,0:T(8,128)(2,1)} %pad_maximum_fusion.4.refs_0_.refs_1_), channel_id=1, source_target_pairs={{0,2},{2,6},{4,0},{6,4},{8,10},{10,14},{12,8},{14,12},{16,18},{18,... | collective-permute-start | bytes 8650760 | tf_op jit(solution)/shard_map/ppermute | solution.py:830
  315.3 85.4 %collective-permute-start.26 = (bf16[512,2816]{1,0:T(8,128)(2,1)}, bf16[512,2816]{1,0:T(8,128)(2,1)}, u32[]{:S(2)}, u32[]{:S(2)}) collective-permute-start(bf16[512,2816]{1,0:T(8,128)(2,1)} %pad_maximum_fusion.4.refs_0_.refs_1_), channel_id=1, source_target_pairs={{0,4},{2,0},{4,6},{6,2},{8,12},{10,8},{12,14},{14,10},{16,20},{18,... | collective-permute-start | bytes 8650760 | tf_op jit(solution)/shard_map/ppermute | solution.py:830
  323.1 61.6 %collective-permute-start.22 = (bf16[256,2048]{1,0:T(8,128)(2,1)}, bf16[256,2048]{1,0:T(8,128)(2,1)}, u32[]{:S(2)}, u32[]{:S(2)}) collective-permute-start(bf16[256,2048]{1,0:T(8,128)(2,1)} %get-tuple-element.142), channel_id=1, source_target_pairs={{0,8},{2,10},{4,12},{6,14},{8,0},{10,2},{12,4},{14,6},{16,24},{18,... | collective-permute-start | bytes 3145736 | tf_op jit(solution)/shard_map/ppermute | solution.py:834
  327.0 66.9 %collective-permute-start.32 = (bf16[1408,256]{1,0:T(8,128)(2,1)}, bf16[1408,256]{1,0:T(8,128)(2,1)}, u32[]{:S(2)}, u32[]{:S(2)}) collective-permute-start(bf16[1408,256]{1,0:T(8,128)(2,1)} %maximum_select_fusion.9), channel_id=1, source_target_pairs={{0,16},{2,18},{4,20},{6,22},{8,24},{10,26},{12,28},{14,30},{16,0},... | collective-permute-start | bytes 2162696 | tf_op jit(solution)/shard_map/ppermute | solution.py:834
  402.1 64.7 %collective-permute-start.27 = (bf16[512,2816]{1,0:T(8,128)(2,1)}, bf16[512,2816]{1,0:T(8,128)(2,1)}, u32[]{:S(2)}, u32[]{:S(2)}) collective-permute-start(bf16[512,2816]{1,0:T(8,128)(2,1)} %collective-permute-done.26.refs_1_.refs_2_), channel_id=1, source_target_pairs={{0,4},{2,0},{4,6},{6,2},{8,12},{10,8},{12,14},{14,10},{16,20},{18,... | collective-permute-start | bytes 8650760 | tf_op jit(solution)/shard_map/ppermute | solution.py:830
  439.1 54.3 %collective-permute-start.35 = (bf16[1408,512]{1,0:T(8,128)(2,1)}, bf16[1408,512]{1,0:T(8,128)(2,1)}, u32[]{:S(2)}, u32[]{:S(2)}) collective-permute-start(bf16[1408,512]{1,0:T(8,128)(2,1)} %collective-permute-done.34.refs_3_.refs_4_), channel_id=1, source_target_pairs={{0,2},{2,6},{4,0},{6,4},{8,10},{10,14},{12,8},{14,12},{16,18},{18,... | collective-permute-start | bytes 4325384 | tf_op jit(solution)/shard_map/ppermute | solution.py:830
  564.3 64.4 %collective-permute-start.48 = (bf16[512,2816]{1,0:T(8,128)(2,1)}, bf16[512,2816]{1,0:T(8,128)(2,1)}, u32[]{:S(2)}, u32[]{:S(2)}) collective-permute-start(bf16[512,2816]{1,0:T(8,128)(2,1)} %convolution_convert_fusion.1), channel_id=1, source_target_pairs={{0,4},{2,0},{4,6},{6,2},{8,12},{10,8},{12,14},{14,10},{16,20},{18,... | collective-permute-start | bytes 8650760 | tf_op jit(solution)/shard_map/ppermute | solution.py:830
  580.5 54.9 %collective-permute-start.38 = (bf16[512,2048]{1,0:T(8,128)(2,1)}, bf16[512,2048]{1,0:T(8,128)(2,1)}, u32[]{:S(2)}, u32[]{:S(2)}) collective-permute-start(bf16[512,2048]{1,0:T(8,128)(2,1)} %wide_given.6), channel_id=1, source_target_pairs={{0,1},{1,0},{2,3},{3,2},{4,5},{5,4},{6,7},{7,6},{8,9},{9,8},{10,11... | collective-permute-start | bytes 6291464 | tf_op jit(solution)/shard_map/ppermute | solution.py:840
  602.5 175.4 %collective-permute-start.73 = (bf16[1408,256]{1,0:T(8,128)(2,1)}, bf16[1408,256]{1,0:T(8,128)(2,1)}, u32[]{:S(2)}, u32[]{:S(2)}) collective-permute-start(bf16[1408,256]{1,0:T(8,128)(2,1)} %slice.551), channel_id=1, source_target_pairs={{0,16},{2,18},{4,20},{6,22},{8,24},{10,26},{12,28},{14,30},{16,0},... | collective-permute-start | bytes 2162696 | tf_op jit(solution)/shard_map/ppermute | solution.py:834
  604.9 95.3 %collective-permute-start.45 = (bf16[512,2816]{1,0:T(8,128)(2,1)}, bf16[512,2816]{1,0:T(8,128)(2,1)S(1)}, u32[]{:S(2)}, u32[]{:S(2)}) collective-permute-start(bf16[512,2816]{1,0:T(8,128)(2,1)} %convolution_convert_fusion), channel_id=1, source_target_pairs={{0,2},{2,6},{4,0},{6,4},{8,10},{10,14},{12,8},{14,12},{16,18},{18,... | collective-permute-start | bytes 8650760 | tf_op jit(solution)/shard_map/ppermute | solution.py:830
  635.3 108.8 %collective-permute-start.52 = (bf16[512,2816]{1,0:T(8,128)(2,1)}, bf16[512,2816]{1,0:T(8,128)(2,1)}, u32[]{:S(2)}, u32[]{:S(2)}) collective-permute-start(bf16[512,2816]{1,0:T(8,128)(2,1)} %add_convert_fusion), channel_id=1, source_target_pairs={{0,4},{2,0},{4,6},{6,2},{8,12},{10,8},{12,14},{14,10},{16,20},{18,... | collective-permute-start | bytes 8650760 | tf_op jit(solution)/shard_map/ppermute | solution.py:830
  645.7 118.0 %collective-permute-start.39 = (bf16[256,2048]{1,0:T(8,128)(2,1)}, bf16[256,2048]{1,0:T(8,128)(2,1)}, u32[]{:S(2)}, u32[]{:S(2)}) collective-permute-start(bf16[256,2048]{1,0:T(8,128)(2,1)} %get-tuple-element.161), channel_id=1, source_target_pairs={{0,8},{2,10},{4,12},{6,14},{8,0},{10,2},{12,4},{14,6},{16,24},{18,... | collective-permute-start | bytes 3145736 | tf_op jit(solution)/shard_map/ppermute | solution.py:834
  774.1 102.1 %all-to-all-start.2 = ((bf16[32,10,2048]{2,1,0:T(8,128)(2,1)}), bf16[32,10,2048]{2,1,0:T(8,128)(2,1)}, u32[]{:S(2)}, u32[]{:S(2)}) async-start(bf16[32,10,2048]{2,1,0:T(8,128)(2,1)} %all_to_all.38), calls=%async_computation.2 | async-start | bytes 4194304 | tf_op jit(solution)/shard_map/all_to_all | solution.py:974
  781.5 227.3 %collective-permute-start.74 = (bf16[1408,128]{1,0:T(8,128)(2,1)}, bf16[1408,128]{1,0:T(8,128)(2,1)}, u32[]{:S(2)}, u32[]{:S(2)}) collective-permute-start(bf16[1408,128]{1,0:T(8,128)(2,1)} %dynamic-slice_convert_fusion.3), channel_id=1, source_target_pairs={{0,8},{2,10},{4,12},{6,14},{8,0},{10,2},{12,4},{14,6},{16,24},{18,... | collective-permute-start | bytes 1081352 | tf_op jit(solution)/shard_map/ppermute | solution.py:834
  792.6 52.9 %collective-permute-start.50 = (bf16[512,1536]{1,0:T(8,128)(2,1)}, bf16[512,1536]{1,0:T(8,128)(2,1)}, u32[]{:S(2)}, u32[]{:S(2)}) collective-permute-start(bf16[512,1536]{1,0:T(8,128)(2,1)} %convolution_convert_fusion.6), channel_id=1, source_target_pairs={{0,2},{2,6},{4,0},{6,4},{8,10},{10,14},{12,8},{14,12},{16,18},{18,... | collective-permute-start | bytes 4718600 | tf_op jit(solution)/shard_map/ppermute | solution.py:830
  814.9 49.4 %collective-permute-start.54 = (bf16[256,2048]{1,0:T(8,128)(2,1)}, bf16[256,2048]{1,0:T(8,128)(2,1)S(1)}, u32[]{:S(2)}, u32[]{:S(2)}) collective-permute-start(bf16[256,2048]{1,0:T(8,128)(2,1)} %get-tuple-element.185), channel_id=1, source_target_pairs={{0,8},{2,10},{4,12},{6,14},{8,0},{10,2},{12,4},{14,6},{16,24},{18,... | collective-permute-start | bytes 3145736 | tf_op jit(solution)/shard_map/ppermute | solution.py:834
  823.3 124.2 %collective-permute-start.71 = (bf16[256,2816]{1,0:T(8,128)(2,1)}, bf16[256,2816]{1,0:T(8,128)(2,1)}, u32[]{:S(2)}, u32[]{:S(2)}) collective-permute-start(bf16[256,2816]{1,0:T(8,128)(2,1)} %slice.548), channel_id=1, source_target_pairs={{0,16},{2,18},{4,20},{6,22},{8,24},{10,26},{12,28},{14,30},{16,0},... | collective-permute-start | bytes 4325384 | tf_op jit(solution)/shard_map/ppermute | solution.py:834
  876.2 70.0 %all-to-all-start.3 = ((bf16[32,10,2048]{2,1,0:T(8,128)(2,1)}), bf16[32,10,2048]{2,1,0:T(8,128)(2,1)S(1)}, u32[]{:S(2)}, u32[]{:S(2)}) async-start(bf16[32,10,2048]{2,1,0:T(8,128)(2,1)} %all_to_all.41), calls=%async_computation.3 | async-start | bytes 4194304 | tf_op jit(solution)/shard_map/all_to_all | solution.py:974
  888.4 59.2 %collective-permute-start.55 = (bf16[512,1664]{1,0:T(8,128)(2,1)}, bf16[512,1664]{1,0:T(8,128)(2,1)}, u32[]{:S(2)}, u32[]{:S(2)}) collective-permute-start(bf16[512,1664]{1,0:T(8,128)(2,1)} %convolution_convert_fusion.3), channel_id=1, source_target_pairs={{0,2},{2,6},{4,0},{6,4},{8,10},{10,14},{12,8},{14,12},{16,18},{18,... | collective-permute-start | bytes 5111816 | tf_op jit(solution)/shard_map/ppermute | solution.py:830
  895.6 54.9 %collective-permute-start.59 = (bf16[512,1664]{1,0:T(8,128)(2,1)}, bf16[512,1664]{1,0:T(8,128)(2,1)}, u32[]{:S(2)}, u32[]{:S(2)}) collective-permute-start(bf16[512,1664]{1,0:T(8,128)(2,1)} %add_convert_fusion.1), channel_id=1, source_target_pairs={{0,4},{2,0},{4,6},{6,2},{8,12},{10,8},{12,14},{14,10},{16,20},{18,... | collective-permute-start | bytes 5111816 | tf_op jit(solution)/shard_map/ppermute | solution.py:830
  900.8 76.9 %collective-permute-start.69 = (bf16[1024,256]{1,0:T(8,128)(2,1)S(1)}, bf16[1024,256]{1,0:T(8,128)(2,1)}, u32[]{:S(2)}, u32[]{:S(2)}) collective-permute-start(bf16[1024,256]{1,0:T(8,128)(2,1)S(1)} %slice.552), channel_id=1, source_target_pairs={{0,16},{2,18},{4,20},{6,22},{8,24},{10,26},{12,28},{14,30},{16,0},... | collective-permute-start | bytes 1572872 | tf_op jit(solution)/shard_map/ppermute | solution.py:834
  947.6 69.0 %collective-permute-start.60 = (f32[296,128]{1,0:T(8,128)}, f32[296,128]{1,0:T(8,128)S(1)}, u32[]{:S(2)}, u32[]{:S(2)}) collective-permute-start(f32[296,128]{1,0:T(8,128)} %pad_bitcast_fusion), channel_id=1, source_target_pairs={{0,16},{2,18},{4,20},{6,22},{8,24},{10,26},{12,28},{14,30},{16,0},... | collective-permute-start | bytes 454664 | tf_op jit(solution)/shard_map/ppermute | solution.py:834
  1014.3 52.3 %collective-permute-start.66 = (bf16[256,1664]{1,0:T(8,128)(2,1)}, bf16[256,1664]{1,0:T(8,128)(2,1)}, u32[]{:S(2)}, u32[]{:S(2)}) collective-permute-start(bf16[256,1664]{1,0:T(8,128)(2,1)} %slice.549), channel_id=1, source_target_pairs={{0,16},{2,18},{4,20},{6,22},{8,24},{10,26},{12,28},{14,30},{16,0},... | collective-permute-start | bytes 2555912 | tf_op jit(solution)/shard_map/ppermute | solution.py:834
  (146 other events, 3327.0 us)

commit v4 on v3

--- a/solution.py
+++ b/solution.py
@@ -56,7 +56,7 @@
 
 def unit_lower_inverses(systems, places, others):
     eye = (places == others).astype(f32)
-    size = 16
+    size = 2
     same = (places // size) == (others // size)
     power = [jnp.where(same, a, 0.0) for a in systems]
     inverse = [eye - a for a in power]
@@ -1094,10 +1094,10 @@
     grad_middle = dy_own + grad_mid_norm
     mix_rows = lay.rows_of((live_own * grad_middle).astype(bf))
 
-    grad_heads = heads_backward(lay.tie(mix_rows, feed_sent[0]), out_pieces)
+    grad_heads = heads_backward(mix_rows, out_pieces)
     out_own, out_terms, out_sent = lay.collect_ring(lambda r: outer_sum(heads_out, columns_of(mix_rows, r)), True)
     grad_proj_first, taps_first, params_first, gain_first = mixer_backward(
-        0, heads, core, proj_first, decays, lay.tie(grad_heads, *out_terms), marks, seg_rows, taps[0], params,
+        0, heads, core, proj_first, decays, lay.tie(grad_heads, feed_sent[0], *out_terms), marks, seg_rows, taps[0], params,
         gain_row, states_first, inverses_first, None,
     )
     first_own, first_terms, first_sent = lay.collect_ring(

time: 1100 us -> 1100 us (level)
  transfers between devices with their start and end apart: 79 -> 79, of which waited for: 36 -> 36; matrix products, arithmetic and copies ran while one was open for 22% -> 22% of each run, Pallas kernels for 19% -> 20%
where the time goes in v4:
time: 1100 us; the launch traced here: 1090 us
  waiting for transfers between devices  474 us (43%)
  Pallas kernels  244 us (22%)
  matrix products  129 us (12%)
  starting transfers between devices  92.7 us (8%)
  local copies, waits for them, and re-layouts  73 us (7%)
  other arithmetic  71.5 us (6%)
    ppermute x32, waiting for transfers between devices, flip(): return lax.ppermute(values, 'dp', [(n, n ^ bit) for n in range(self.ways)])  260 us
    ppermute x30, waiting for transfers between devices, ring(): line.append(lax.ppermute(values, 'dp', pairs))  153 us
    pallas_call x13, Pallas kernels, call(): pl.pallas_call(body, grid=grid, scratch_shapes=scratch, in_specs=in_specs...  147 us
    dot_general x24, matrix products, outer_sum(): lax.dot_general(left, right, (((0,), (0,)), ((), ())), preferred_element_...  115 us
    all_to_all x4, waiting for transfers between devices, exchange(): lax.all_to_all(values, ('dp', 'tensor'), split_axis=0, concat_axis=0, til...  59.6 us
    pallas_call x2, Pallas kernels, mixer_backward(): pl.pallas_call(body, grid_spec=pltpu.PrefetchScalarGridSpec(num_scalar_pr...  58.4 us
    ppermute x32, starting transfers between devices, flip(): return lax.ppermute(values, 'dp', [(n, n ^ bit) for n in range(self.ways)])  40.7 us
    ppermute x30, starting transfers between devices, ring(): line.append(lax.ppermute(values, 'dp', pairs))  37.9 us
  transfers between devices with their start and end apart: 79, of which 36 were waited for; matrix products, arithmetic and copies ran while one was open for 22% of the time, Pallas kernels for 20%

profile of v4, /device:TPU:0, one launch (start us, length us, event | category | flops | bytes accessed | tf_op | source)
XLA Modules:
  0.0 1086.4 jit_solution(4290880601590382320)
XLA Ops:
  35.0 51.2 %collective-permute-done.5 = bf16[256,1664]{1,0:T(8,128)(2,1)} collective-permute-done((bf16[256,1664]{1,0:T(8,128)(2,1)}, bf16[256,1664]{1,0:T(8,128)(2,1)}, u32[]{:S(2)}, u32[]{:S(2)}) %collective-permute-start.5) | collective-permute-done | bytes 852000 | tf_op jit(solution)/shard_map/ppermute | solution.py:834
  97.5 13.3 %collective-permute-done.6 = bf16[128,1536]{1,0:T(8,128)(2,1)S(1)} collective-permute-done((bf16[128,1536]{1,0:T(8,128)(2,1)S(1)}, bf16[128,1536]{1,0:T(8,128)(2,1)S(1)}, u32[]{:S(2)}, u32[]{:S(2)}) %collective-permute-start.6) | collective-permute-done | bytes 393248 | tf_op jit(solution)/shard_map/ppermute | solution.py:834
  112.2 20.4 %collective-permute-done.11.refs_3_.refs_7_.refs_5_ = bf16[512,1664]{1,0:T(8,128)(2,1)} collective-permute-done((bf16[512,1664]{1,0:T(8,128)(2,1)}, bf16[512,1664]{1,0:T(8,128)(2,1)}, u32[]{:S(2)}, u32[]{:S(2)}) %collective-permute-start.11) | collective-permute-done | bytes 1703968 | tf_op jit(solution)/shard_map/ppermute | solution.py:830
  151.4 32.7 %collective-permute-done.15 = bf16[2432,128]{1,0:T(8,128)(2,1)} collective-permute-done((bf16[2432,128]{1,0:T(8,128)(2,1)}, bf16[2432,128]{1,0:T(8,128)(2,1)}, u32[]{:S(2)}, u32[]{:S(2)}) %collective-permute-start.15) | collective-permute-done | bytes 622624 | tf_op jit(solution)/shard_map/ppermute | solution.py:834
  189.6 21.4 %collective-permute-done.16 = bf16[1024,256]{1,0:T(8,128)(2,1)S(1)} collective-permute-done((bf16[1024,256]{1,0:T(8,128)(2,1)S(1)}, bf16[1024,256]{1,0:T(8,128)(2,1)S(1)}, u32[]{:S(2)}, u32[]{:S(2)}) %collective-permute-start.16) | collective-permute-done | bytes 524320 | tf_op jit(solution)/shard_map/ppermute | solution.py:834
  218.6 12.8 %project.3 = (bf16[1024,1536]{1,0:T(8,128)(2,1)}, f32[1024,128]{1,0:T(8,128)}) custom-call(bf16[1024,2048]{1,0:T(8,128)(2,1)} %pad_maximum_fusion.rows_ref, bf16[512,1664]{1,0:T(8,128)(2,1)} %pad_maximum_fusion.5.refs_0_.refs_4_.refs_2_, bf16[512,1664]{1,0:T(8,128)(2,1)} %collective-permute-done.8.refs_1_.refs_5_.refs_3_, ...), custom_call_target="tpu_custom_call" | custom-call | flops 6442450944 | bytes 13631488 | tf_op jit(solution)/shard_map/project/pallas_call | solution.py:581
  231.4 16.2 %collective-permute-done.13.refs_3_.refs_9_ = bf16[512,1536]{1,0:T(8,128)(2,1)} collective-permute-done((bf16[512,1536]{1,0:T(8,128)(2,1)}, bf16[512,1536]{1,0:T(8,128)(2,1)}, u32[]{:S(2)}, u32[]{:S(2)}) %collective-permute-start.13) | collective-permute-done | bytes 1572896 | tf_op jit(solution)/shard_map/ppermute | solution.py:830
  248.5 17.0 %mixer_forward.2 = (bf16[2,2,2,128,1024]{4,3,2,1,0:T(8,128)(2,1)}, bf16[4,4,128,256]{3,2,1,0:T(8,128)(2,1)}, bf16[4,4,128,128]{3,2,1,0:T(8,128)(2,1)}) custom-call(s32[1]{0:T(128)} %bitcast.3.refs_0_.core_ref, bf16[2,2,2,128,1536]{4,3,2,1,0:T(8,128)(2,1)} %bitcast.129, f32[2,2,2,128,128]{4,3,2,1,0:T(8,128)} %bitcast.134, ...), custom_call_target="tpu_custom_call" | custom-call | flops 16000000000 | bytes 16777216 | tf_op jit(solution)/shard_map/mixer_forward/pallas_call | solution.py:382
  266.7 11.4 %project.2 = bf16[1024,1536]{1,0:T(8,128)(2,1)} custom-call(bf16[1024,2048]{1,0:T(8,128)(2,1)} %pad_maximum_fusion.rows_ref, bf16[512,1536]{1,0:T(8,128)(2,1)} %pad_maximum_fusion.6.refs_0_.refs_6_, bf16[512,1536]{1,0:T(8,128)(2,1)} %collective-permute-done.9.refs_1_.refs_7_, bf16[512,1536]{1,0:T(8,128)(2,1)} %collective-permute-done.10.refs_2_.refs_8_, ...), custom_call_target="tpu_custom_call" | custom-call | flops 6442450944 | bytes 13631488 | tf_op jit(solution)/shard_map/project/pallas_call | solution.py:581
  279.3 16.6 %mixer_forward.3 = (bf16[2,2,2,128,1024]{4,3,2,1,0:T(8,128)(2,1)}, bf16[4,4,128,256]{3,2,1,0:T(8,128)(2,1)}, bf16[4,4,128,128]{3,2,1,0:T(8,128)(2,1)}) custom-call(s32[1]{0:T(128)} %bitcast.3.refs_0_.core_ref, bf16[2,2,2,128,1536]{4,3,2,1,0:T(8,128)(2,1)} %bitcast.126, f32[2,2,2,128,128]{4,3,2,1,0:T(8,128)} %bitcast.135, ...), custom_call_target="tpu_custom_call", output_to_operand_aliasing={{0}: (8, {})} | custom-call | flops 16000000000 | bytes 16777216 | tf_op jit(solution)/shard_map/mixer_forward/pallas_call | solution.py:382
  330.5 33.8 %all-to-all-done.1 = bf16[32,10,2048]{2,1,0:T(8,128)(2,1)S(1)} async-done(((bf16[32,10,2048]{2,1,0:T(8,128)(2,1)}), bf16[32,10,2048]{2,1,0:T(8,128)(2,1)S(1)}, u32[]{:S(2)}, u32[]{:S(2)}) %all-to-all-start.1) | async-done | bytes 1310752 | tf_op jit(solution)/shard_map/all_to_all | solution.py:974
  365.6 20.1 %collective-permute-done.22 = bf16[256,2048]{1,0:T(8,128)(2,1)} collective-permute-done((bf16[256,2048]{1,0:T(8,128)(2,1)}, bf16[256,2048]{1,0:T(8,128)(2,1)}, u32[]{:S(2)}, u32[]{:S(2)}) %collective-permute-start.22) | collective-permute-done | bytes 1048608 | tf_op jit(solution)/shard_map/ppermute | solution.py:834
  417.3 22.3 %collective-permute-done.29 = bf16[256,2048]{1,0:T(8,128)(2,1)S(1)} collective-permute-done((bf16[256,2048]{1,0:T(8,128)(2,1)}, bf16[256,2048]{1,0:T(8,128)(2,1)S(1)}, u32[]{:S(2)}, u32[]{:S(2)}) %collective-permute-start.29) | collective-permute-done | bytes 1048608 | tf_op jit(solution)/shard_map/ppermute | solution.py:834
  445.2 22.6 %collective-permute-done.27.refs_2_.refs_3_ = bf16[512,2816]{1,0:T(8,128)(2,1)} collective-permute-done((bf16[512,2816]{1,0:T(8,128)(2,1)}, bf16[512,2816]{1,0:T(8,128)(2,1)}, u32[]{:S(2)}, u32[]{:S(2)}) %collective-permute-start.27) | collective-permute-done | bytes 2883616 | tf_op jit(solution)/shard_map/ppermute | solution.py:830
  468.1 18.7 %feed_forward.1 = (bf16[1024,2816]{1,0:T(8,128)(2,1)}, bf16[1024,1408]{1,0:T(8,128)(2,1)}) custom-call(bf16[1024,2048]{1,0:T(8,128)(2,1)} %pad_maximum_fusion.1.rows_ref, bf16[512,2816]{1,0:T(8,128)(2,1)} %pad_maximum_fusion.4.refs_0_.refs_1_, bf16[512,2816]{1,0:T(8,128)(2,1)} %collective-permute-done.26.refs_1_.refs_2_, ...), custom_call_target="tpu_custom_call" | custom-call | flops 11811160064 | bytes 27262976 | tf_op jit(solution)/shard_map/feed_forward/pallas_call | solution.py:581
  500.5 13.8 %feed_backward.1.refs_0_ = bf16[1024,2816]{1,0:T(8,128)(2,1)} custom-call(bf16[1024,2048]{1,0:T(8,128)(2,1)} %copy-done.20, bf16[1408,512]{1,0:T(8,128)(2,1)} %pad_maximum_fusion.7.refs_0_.refs_1_, bf16[1408,512]{1,0:T(8,128)(2,1)} %collective-permute-done.33.refs_1_.refs_2_, bf16[1408,512]{1,0:T(8,128)(2,1)} %collective-permute-done.35.refs_2_.refs_3_, ...), custom_call_target="tpu_custom_call" | custom-call | flops 5905580032 | bytes 21495808 | tf_op jit(solution)/shard_map/feed_backward/pallas_call | solution.py:581
  514.3 11.8 %wide_given.5 = bf16[512,2048]{1,0:T(8,128)(2,1)} custom-call(bf16[1024,2816]{1,0:T(8,128)(2,1)} %feed_backward.1.refs_0_, bf16[512,2816]{1,0:T(8,128)(2,1)} %pad_maximum_fusion.4.refs_0_.refs_1_, bf16[512,2816]{1,0:T(8,128)(2,1)} %collective-permute-done.26.refs_1_.refs_2_, bf16[512,2816]{1,0:T(8,128)(2,1)} %collective-permute-done.27.refs_2_.refs_3_, ...), custom_call_target="tpu_custom_call" | custom-call | flops 5905580032 | bytes 24117248 | tf_op jit(solution)/shard_map/wide_given/pallas_call | solution.py:581
  530.7 12.1 %wide_kept.5 = (bf16[256,2048]{1,0:T(8,128)(2,1)}, f32[256,2048]{1,0:T(8,128)}) custom-call(bf16[1024,2816]{1,0:T(8,128)(2,1)} %feed_backward.1.refs_0_, bf16[512,2816]{1,0:T(8,128)(2,1)} %pad_maximum_fusion.4.refs_0_.refs_1_, bf16[512,2816]{1,0:T(8,128)(2,1)} %collective-permute-done.26.refs_1_.refs_2_, ...), custom_call_target="tpu_custom_call" | custom-call | flops 5905580032 | bytes 24117248 | tf_op jit(solution)/shard_map/wide_kept/pallas_call | solution.py:581
  551.6 8.9 collective-permute-done.43
  588.9 9.5 collective-permute-done.44
  606.4 23.2 %collective-permute-done.48 = bf16[512,2816]{1,0:T(8,128)(2,1)} collective-permute-done((bf16[512,2816]{1,0:T(8,128)(2,1)}, bf16[512,2816]{1,0:T(8,128)(2,1)}, u32[]{:S(2)}, u32[]{:S(2)}) %collective-permute-start.48) | collective-permute-done | bytes 2883616 | tf_op jit(solution)/shard_map/ppermute | solution.py:830
  662.6 29.0 %mixer_backward.2 = (bf16[2,2,2,128,1664]{4,3,2,1,0:T(8,128)(2,1)}, f32[4,1024]{1,0:T(4,128)}, f32[8,128]{1,0:T(8,128)}, f32[8,256]{1,0:T(8,128)}) custom-call(s32[1]{0:T(128)} %bitcast.3.refs_0_.core_ref, bf16[2,2,2,128,1536]{4,3,2,1,0:T(8,128)(2,1)} %bitcast.130, bf16[2,2,2,128,1536]{4,3,2,1,0:T(8,128)(2,1)} %bitcast.131, ...), custom_call_target="tpu_custom_call" | custom-call | flops 30000001024 | bytes 31457280 | tf_op jit(solution)/shard_map/mixer_backward/pallas_call | solution.py:468
  701.6 29.4 %mixer_backward.3 = (bf16[2,2,2,128,1664]{4,3,2,1,0:T(8,128)(2,1)}, f32[4,1024]{1,0:T(4,128)}, f32[8,128]{1,0:T(8,128)}, f32[8,256]{1,0:T(8,128)}) custom-call(s32[1]{0:T(128)} %bitcast.3.refs_0_.core_ref, bf16[2,2,2,128,1536]{4,3,2,1,0:T(8,128)(2,1)} %bitcast.127, bf16[2,2,2,128,1536]{4,3,2,1,0:T(8,128)(2,1)} %bitcast.128, ...), custom_call_target="tpu_custom_call" | custom-call | flops 30000001024 | bytes 31457280 | tf_op jit(solution)/shard_map/mixer_backward/pallas_call | solution.py:468
  745.1 13.3 %wide_given.7 = bf16[512,2048]{1,0:T(8,128)(2,1)} custom-call(bf16[1024,1664]{1,0:T(8,128)(2,1)} %bitcast.121, bf16[1024,1664]{1,0:T(8,128)(2,1)} %bitcast.77, bf16[512,1664]{1,0:T(8,128)(2,1)} %pad_maximum_fusion.5.refs_0_.refs_4_.refs_2_, bf16[512,1664]{1,0:T(8,128)(2,1)} %collective-permute-done.8.refs_1_.refs_5_.refs_3_, ...), custom_call_target="tpu_custom_call" | custom-call | flops 6710886400 | bytes 25690112 | tf_op jit(solution)/shard_map/wide_given/pallas_call | solution.py:581
  784.2 9.4 collective-permute-done.49
  802.5 13.4 %wide_kept.7 = (bf16[256,2048]{1,0:T(8,128)(2,1)}, f32[256,2048]{1,0:T(8,128)}) custom-call(bf16[1024,1664]{1,0:T(8,128)(2,1)} %bitcast.122, bf16[1024,1664]{1,0:T(8,128)(2,1)} %bitcast.78, bf16[512,1664]{1,0:T(8,128)(2,1)} %pad_maximum_fusion.5.refs_0_.refs_4_.refs_2_, bf16[512,1664]{1,0:T(8,128)(2,1)} %collective-permute-done.8.refs_1_.refs_5_.refs_3_, ...), custom_call_target="tpu_custom_call" | custom-call | flops 6710886400 | bytes 25690112 | tf_op jit(solution)/shard_map/wide_kept/pallas_call | solution.py:581
  824.7 20.1 %collective-permute-done.57 = bf16[512,1536]{1,0:T(8,128)(2,1)} collective-permute-done((bf16[512,1536]{1,0:T(8,128)(2,1)}, bf16[512,1536]{1,0:T(8,128)(2,1)}, u32[]{:S(2)}, u32[]{:S(2)}) %collective-permute-start.57) | collective-permute-done | bytes 1572896 | tf_op jit(solution)/shard_map/ppermute | solution.py:830
  852.0 13.3 %collective-permute-done.54 = bf16[256,2048]{1,0:T(8,128)(2,1)S(1)} collective-permute-done((bf16[256,2048]{1,0:T(8,128)(2,1)}, bf16[256,2048]{1,0:T(8,128)(2,1)S(1)}, u32[]{:S(2)}, u32[]{:S(2)}) %collective-permute-start.54) | collective-permute-done | bytes 1048608 | tf_op jit(solution)/shard_map/ppermute | solution.py:834
  921.4 25.8 %all-to-all-done.3 = bf16[32,10,2048]{2,1,0:T(8,128)(2,1)S(1)} async-done(((bf16[32,10,2048]{2,1,0:T(8,128)(2,1)}), bf16[32,10,2048]{2,1,0:T(8,128)(2,1)S(1)}, u32[]{:S(2)}, u32[]{:S(2)}) %all-to-all-start.3) | async-done | bytes 1310752 | tf_op jit(solution)/shard_map/all_to_all | solution.py:974
  951.4 27.2 %collective-permute-done.69 = bf16[1024,256]{1,0:T(8,128)(2,1)} collective-permute-done((bf16[1024,256]{1,0:T(8,128)(2,1)S(1)}, bf16[1024,256]{1,0:T(8,128)(2,1)}, u32[]{:S(2)}, u32[]{:S(2)}) %collective-permute-start.69) | collective-permute-done | bytes 524320 | tf_op jit(solution)/shard_map/ppermute | solution.py:834
  982.7 14.8 %collective-permute-done.65 = bf16[256,1536]{1,0:T(8,128)(2,1)S(1)} collective-permute-done((bf16[256,1536]{1,0:T(8,128)(2,1)}, bf16[256,1536]{1,0:T(8,128)(2,1)S(1)}, u32[]{:S(2)}, u32[]{:S(2)}) %collective-permute-start.65) | collective-permute-done | bytes 786464 | tf_op jit(solution)/shard_map/ppermute | solution.py:834
  1025.9 12.9 %collective-permute-done.61 = f32[296,128]{1,0:T(8,128)S(1)} collective-permute-done((f32[296,128]{1,0:T(8,128)S(1)}, f32[296,128]{1,0:T(8,128)S(1)}, u32[]{:S(2)}, u32[]{:S(2)}) %collective-permute-start.61) | collective-permute-done | bytes 151584 | tf_op jit(solution)/shard_map/ppermute | solution.py:834
  (541 shorter events, 465.5 us)
Async XLA Ops:
  0.7 94.8 %collective-permute-start.1 = (s32[1,4]{1,0:T(1,128)}, s32[1,4]{1,0:T(1,128)}, u32[]{:S(2)}, u32[]{:S(2)}) collective-permute-start(s32[1,4]{1,0:T(1,128)} %param.21), channel_id=1, source_target_pairs={{0,8},{2,10},{4,12},{6,14},{8,0},{10,2},{12,4},{14,6},{16,24},{18,... | collective-permute-start | bytes 56 | tf_op jit(solution)/shard_map/ppermute | solution.py:834
  23.2 63.0 %collective-permute-start.5 = (bf16[256,1664]{1,0:T(8,128)(2,1)}, bf16[256,1664]{1,0:T(8,128)(2,1)}, u32[]{:S(2)}, u32[]{:S(2)}) collective-permute-start(bf16[256,1664]{1,0:T(8,128)(2,1)} %maximum_select_fusion.7), channel_id=1, source_target_pairs={{0,16},{2,18},{4,20},{6,22},{8,24},{10,26},{12,28},{14,30},{16,0},... | collective-permute-start | bytes 2555912 | tf_op jit(solution)/shard_map/ppermute | solution.py:834
  28.6 106.3 %all-to-all-start = ((bf16[32,10,2176]{2,1,0:T(8,128)(2,1)}), bf16[32,10,2176]{2,1,0:T(8,128)(2,1)S(1)}, u32[]{:S(2)}, u32[]{:S(2)}) async-start(bf16[32,10,2176]{2,1,0:T(8,128)(2,1)} %all_to_all.32), calls=%async_computation | async-start | bytes 4456448 | tf_op jit(solution)/shard_map/all_to_all | solution.py:974
  96.9 54.0 %collective-permute-start.8 = (bf16[512,1664]{1,0:T(8,128)(2,1)}, bf16[512,1664]{1,0:T(8,128)(2,1)}, u32[]{:S(2)}, u32[]{:S(2)}) collective-permute-start(bf16[512,1664]{1,0:T(8,128)(2,1)} %pad_maximum_fusion.5.refs_0_.refs_4_.refs_2_), channel_id=1, source_target_pairs={{0,4},{2,0},{4,6},{6,2},{8,12},{10,8},{12,14},{14,10},{16,20},{18,... | collective-permute-start | bytes 5111816 | tf_op jit(solution)/shard_map/ppermute | solution.py:830
  132.6 56.1 %collective-permute-start.12 = (bf16[512,1664]{1,0:T(8,128)(2,1)}, bf16[512,1664]{1,0:T(8,128)(2,1)}, u32[]{:S(2)}, u32[]{:S(2)}) collective-permute-start(bf16[512,1664]{1,0:T(8,128)(2,1)} %collective-permute-done.11.refs_3_.refs_7_.refs_5_), channel_id=1, source_target_pairs={{0,2},{2,6},{4,0},{6,4},{8,10},{10,14},{12,8},{14,12},{16,18},{18,... | collective-permute-start | bytes 5111816 | tf_op jit(solution)/shard_map/ppermute | solution.py:830
  151.0 61.7 %collective-permute-start.9 = (bf16[512,1536]{1,0:T(8,128)(2,1)}, bf16[512,1536]{1,0:T(8,128)(2,1)}, u32[]{:S(2)}, u32[]{:S(2)}) collective-permute-start(bf16[512,1536]{1,0:T(8,128)(2,1)} %pad_maximum_fusion.6.refs_0_.refs_6_), channel_id=1, source_target_pairs={{0,4},{2,0},{4,6},{6,2},{8,12},{10,8},{12,14},{14,10},{16,20},{18,... | collective-permute-start | bytes 4718600 | tf_op jit(solution)/shard_map/ppermute | solution.py:830
  212.7 52.8 %collective-permute-start.10 = (bf16[512,1536]{1,0:T(8,128)(2,1)}, bf16[512,1536]{1,0:T(8,128)(2,1)}, u32[]{:S(2)}, u32[]{:S(2)}) collective-permute-start(bf16[512,1536]{1,0:T(8,128)(2,1)} %collective-permute-done.9.refs_1_.refs_7_), channel_id=1, source_target_pairs={{0,4},{2,0},{4,6},{6,2},{8,12},{10,8},{12,14},{14,10},{16,20},{18,... | collective-permute-start | bytes 4718600 | tf_op jit(solution)/shard_map/ppermute | solution.py:830
  218.5 77.4 %collective-permute-start.17 = (bf16[256,2816]{1,0:T(8,128)(2,1)S(1)}, bf16[256,2816]{1,0:T(8,128)(2,1)S(1)}, u32[]{:S(2)}, u32[]{:S(2)}) collective-permute-start(bf16[256,2816]{1,0:T(8,128)(2,1)S(1)} %maximum_select_fusion), channel_id=1, source_target_pairs={{0,16},{2,18},{4,20},{6,22},{8,24},{10,26},{12,28},{14,30},{16,0},... | collective-permute-start | bytes 4325384 | tf_op jit(solution)/shard_map/ppermute | solution.py:834
  311.8 52.5 %all-to-all-start.1 = ((bf16[32,10,2048]{2,1,0:T(8,128)(2,1)}), bf16[32,10,2048]{2,1,0:T(8,128)(2,1)S(1)}, u32[]{:S(2)}, u32[]{:S(2)}) async-start(bf16[32,10,2048]{2,1,0:T(8,128)(2,1)} %all_to_all.35), calls=%async_computation.1 | async-start | bytes 4194304 | tf_op jit(solution)/shard_map/all_to_all | solution.py:974
  314.5 87.1 %collective-permute-start.28 = (bf16[512,2816]{1,0:T(8,128)(2,1)}, bf16[512,2816]{1,0:T(8,128)(2,1)}, u32[]{:S(2)}, u32[]{:S(2)}) collective-permute-start(bf16[512,2816]{1,0:T(8,128)(2,1)} %pad_maximum_fusion.4.refs_0_.refs_1_), channel_id=1, source_target_pairs={{0,2},{2,6},{4,0},{6,4},{8,10},{10,14},{12,8},{14,12},{16,18},{18,... | collective-permute-start | bytes 8650760 | tf_op jit(solution)/shard_map/ppermute | solution.py:830
  316.2 85.4 %collective-permute-start.26 = (bf16[512,2816]{1,0:T(8,128)(2,1)}, bf16[512,2816]{1,0:T(8,128)(2,1)}, u32[]{:S(2)}, u32[]{:S(2)}) collective-permute-start(bf16[512,2816]{1,0:T(8,128)(2,1)} %pad_maximum_fusion.4.refs_0_.refs_1_), channel_id=1, source_target_pairs={{0,4},{2,0},{4,6},{6,2},{8,12},{10,8},{12,14},{14,10},{16,20},{18,... | collective-permute-start | bytes 8650760 | tf_op jit(solution)/shard_map/ppermute | solution.py:830
  324.0 61.6 %collective-permute-start.22 = (bf16[256,2048]{1,0:T(8,128)(2,1)}, bf16[256,2048]{1,0:T(8,128)(2,1)}, u32[]{:S(2)}, u32[]{:S(2)}) collective-permute-start(bf16[256,2048]{1,0:T(8,128)(2,1)} %get-tuple-element.141), channel_id=1, source_target_pairs={{0,8},{2,10},{4,12},{6,14},{8,0},{10,2},{12,4},{14,6},{16,24},{18,... | collective-permute-start | bytes 3145736 | tf_op jit(solution)/shard_map/ppermute | solution.py:834
  328.0 66.9 %collective-permute-start.32 = (bf16[1408,256]{1,0:T(8,128)(2,1)}, bf16[1408,256]{1,0:T(8,128)(2,1)}, u32[]{:S(2)}, u32[]{:S(2)}) collective-permute-start(bf16[1408,256]{1,0:T(8,128)(2,1)} %maximum_select_fusion.9), channel_id=1, source_target_pairs={{0,16},{2,18},{4,20},{6,22},{8,24},{10,26},{12,28},{14,30},{16,0},... | collective-permute-start | bytes 2162696 | tf_op jit(solution)/shard_map/ppermute | solution.py:834
  403.1 64.7 %collective-permute-start.27 = (bf16[512,2816]{1,0:T(8,128)(2,1)}, bf16[512,2816]{1,0:T(8,128)(2,1)}, u32[]{:S(2)}, u32[]{:S(2)}) collective-permute-start(bf16[512,2816]{1,0:T(8,128)(2,1)} %collective-permute-done.26.refs_1_.refs_2_), channel_id=1, source_target_pairs={{0,4},{2,0},{4,6},{6,2},{8,12},{10,8},{12,14},{14,10},{16,20},{18,... | collective-permute-start | bytes 8650760 | tf_op jit(solution)/shard_map/ppermute | solution.py:830
  440.1 54.3 %collective-permute-start.35 = (bf16[1408,512]{1,0:T(8,128)(2,1)}, bf16[1408,512]{1,0:T(8,128)(2,1)}, u32[]{:S(2)}, u32[]{:S(2)}) collective-permute-start(bf16[1408,512]{1,0:T(8,128)(2,1)} %collective-permute-done.34.refs_3_.refs_4_), channel_id=1, source_target_pairs={{0,2},{2,6},{4,0},{6,4},{8,10},{10,14},{12,8},{14,12},{16,18},{18,... | collective-permute-start | bytes 4325384 | tf_op jit(solution)/shard_map/ppermute | solution.py:830
  565.3 64.4 %collective-permute-start.48 = (bf16[512,2816]{1,0:T(8,128)(2,1)}, bf16[512,2816]{1,0:T(8,128)(2,1)}, u32[]{:S(2)}, u32[]{:S(2)}) collective-permute-start(bf16[512,2816]{1,0:T(8,128)(2,1)} %convolution_convert_fusion.1), channel_id=1, source_target_pairs={{0,4},{2,0},{4,6},{6,2},{8,12},{10,8},{12,14},{14,10},{16,20},{18,... | collective-permute-start | bytes 8650760 | tf_op jit(solution)/shard_map/ppermute | solution.py:830
  581.4 54.8 %collective-permute-start.38 = (bf16[512,2048]{1,0:T(8,128)(2,1)}, bf16[512,2048]{1,0:T(8,128)(2,1)}, u32[]{:S(2)}, u32[]{:S(2)}) collective-permute-start(bf16[512,2048]{1,0:T(8,128)(2,1)} %wide_given.6), channel_id=1, source_target_pairs={{0,1},{1,0},{2,3},{3,2},{4,5},{5,4},{6,7},{7,6},{8,9},{9,8},{10,11... | collective-permute-start | bytes 6291464 | tf_op jit(solution)/shard_map/ppermute | solution.py:840
  603.5 175.4 %collective-permute-start.73 = (bf16[1408,256]{1,0:T(8,128)(2,1)}, bf16[1408,256]{1,0:T(8,128)(2,1)}, u32[]{:S(2)}, u32[]{:S(2)}) collective-permute-start(bf16[1408,256]{1,0:T(8,128)(2,1)} %slice.551), channel_id=1, source_target_pairs={{0,16},{2,18},{4,20},{6,22},{8,24},{10,26},{12,28},{14,30},{16,0},... | collective-permute-start | bytes 2162696 | tf_op jit(solution)/shard_map/ppermute | solution.py:834
  605.9 95.3 %collective-permute-start.45 = (bf16[512,2816]{1,0:T(8,128)(2,1)}, bf16[512,2816]{1,0:T(8,128)(2,1)S(1)}, u32[]{:S(2)}, u32[]{:S(2)}) collective-permute-start(bf16[512,2816]{1,0:T(8,128)(2,1)} %convolution_convert_fusion), channel_id=1, source_target_pairs={{0,2},{2,6},{4,0},{6,4},{8,10},{10,14},{12,8},{14,12},{16,18},{18,... | collective-permute-start | bytes 8650760 | tf_op jit(solution)/shard_map/ppermute | solution.py:830
  636.2 108.9 %collective-permute-start.52 = (bf16[512,2816]{1,0:T(8,128)(2,1)}, bf16[512,2816]{1,0:T(8,128)(2,1)}, u32[]{:S(2)}, u32[]{:S(2)}) collective-permute-start(bf16[512,2816]{1,0:T(8,128)(2,1)} %add_convert_fusion), channel_id=1, source_target_pairs={{0,4},{2,0},{4,6},{6,2},{8,12},{10,8},{12,14},{14,10},{16,20},{18,... | collective-permute-start | bytes 8650760 | tf_op jit(solution)/shard_map/ppermute | solution.py:830
  646.7 118.0 %collective-permute-start.39 = (bf16[256,2048]{1,0:T(8,128)(2,1)}, bf16[256,2048]{1,0:T(8,128)(2,1)}, u32[]{:S(2)}, u32[]{:S(2)}) collective-permute-start(bf16[256,2048]{1,0:T(8,128)(2,1)} %get-tuple-element.160), channel_id=1, source_target_pairs={{0,8},{2,10},{4,12},{6,14},{8,0},{10,2},{12,4},{14,6},{16,24},{18,... | collective-permute-start | bytes 3145736 | tf_op jit(solution)/shard_map/ppermute | solution.py:834
  775.1 102.1 %all-to-all-start.2 = ((bf16[32,10,2048]{2,1,0:T(8,128)(2,1)}), bf16[32,10,2048]{2,1,0:T(8,128)(2,1)}, u32[]{:S(2)}, u32[]{:S(2)}) async-start(bf16[32,10,2048]{2,1,0:T(8,128)(2,1)} %all_to_all.38), calls=%async_computation.2 | async-start | bytes 4194304 | tf_op jit(solution)/shard_map/all_to_all | solution.py:974
  782.5 227.3 %collective-permute-start.74 = (bf16[1408,128]{1,0:T(8,128)(2,1)}, bf16[1408,128]{1,0:T(8,128)(2,1)}, u32[]{:S(2)}, u32[]{:S(2)}) collective-permute-start(bf16[1408,128]{1,0:T(8,128)(2,1)} %dynamic-slice_convert_fusion.3), channel_id=1, source_target_pairs={{0,8},{2,10},{4,12},{6,14},{8,0},{10,2},{12,4},{14,6},{16,24},{18,... | collective-permute-start | bytes 1081352 | tf_op jit(solution)/shard_map/ppermute | solution.py:834
  793.6 52.9 %collective-permute-start.50 = (bf16[512,1536]{1,0:T(8,128)(2,1)}, bf16[512,1536]{1,0:T(8,128)(2,1)}, u32[]{:S(2)}, u32[]{:S(2)}) collective-permute-start(bf16[512,1536]{1,0:T(8,128)(2,1)} %convolution_convert_fusion.6), channel_id=1, source_target_pairs={{0,2},{2,6},{4,0},{6,4},{8,10},{10,14},{12,8},{14,12},{16,18},{18,... | collective-permute-start | bytes 4718600 | tf_op jit(solution)/shard_map/ppermute | solution.py:830
  815.9 49.4 %collective-permute-start.54 = (bf16[256,2048]{1,0:T(8,128)(2,1)}, bf16[256,2048]{1,0:T(8,128)(2,1)S(1)}, u32[]{:S(2)}, u32[]{:S(2)}) collective-permute-start(bf16[256,2048]{1,0:T(8,128)(2,1)} %get-tuple-element.183), channel_id=1, source_target_pairs={{0,8},{2,10},{4,12},{6,14},{8,0},{10,2},{12,4},{14,6},{16,24},{18,... | collective-permute-start | bytes 3145736 | tf_op jit(solution)/shard_map/ppermute | solution.py:834
  824.3 124.2 %collective-permute-start.71 = (bf16[256,2816]{1,0:T(8,128)(2,1)}, bf16[256,2816]{1,0:T(8,128)(2,1)}, u32[]{:S(2)}, u32[]{:S(2)}) collective-permute-start(bf16[256,2816]{1,0:T(8,128)(2,1)} %slice.548), channel_id=1, source_target_pairs={{0,16},{2,18},{4,20},{6,22},{8,24},{10,26},{12,28},{14,30},{16,0},... | collective-permute-start | bytes 4325384 | tf_op jit(solution)/shard_map/ppermute | solution.py:834
  877.2 70.0 %all-to-all-start.3 = ((bf16[32,10,2048]{2,1,0:T(8,128)(2,1)}), bf16[32,10,2048]{2,1,0:T(8,128)(2,1)S(1)}, u32[]{:S(2)}, u32[]{:S(2)}) async-start(bf16[32,10,2048]{2,1,0:T(8,128)(2,1)} %all_to_all.41), calls=%async_computation.3 | async-start | bytes 4194304 | tf_op jit(solution)/shard_map/all_to_all | solution.py:974
  889.4 59.1 %collective-permute-start.55 = (bf16[512,1664]{1,0:T(8,128)(2,1)}, bf16[512,1664]{1,0:T(8,128)(2,1)}, u32[]{:S(2)}, u32[]{:S(2)}) collective-permute-start(bf16[512,1664]{1,0:T(8,128)(2,1)} %convolution_convert_fusion.3), channel_id=1, source_target_pairs={{0,2},{2,6},{4,0},{6,4},{8,10},{10,14},{12,8},{14,12},{16,18},{18,... | collective-permute-start | bytes 5111816 | tf_op jit(solution)/shard_map/ppermute | solution.py:830
  896.5 54.9 %collective-permute-start.59 = (bf16[512,1664]{1,0:T(8,128)(2,1)}, bf16[512,1664]{1,0:T(8,128)(2,1)}, u32[]{:S(2)}, u32[]{:S(2)}) collective-permute-start(bf16[512,1664]{1,0:T(8,128)(2,1)} %add_convert_fusion.1), channel_id=1, source_target_pairs={{0,4},{2,0},{4,6},{6,2},{8,12},{10,8},{12,14},{14,10},{16,20},{18,... | collective-permute-start | bytes 5111816 | tf_op jit(solution)/shard_map/ppermute | solution.py:830
  901.8 76.9 %collective-permute-start.69 = (bf16[1024,256]{1,0:T(8,128)(2,1)S(1)}, bf16[1024,256]{1,0:T(8,128)(2,1)}, u32[]{:S(2)}, u32[]{:S(2)}) collective-permute-start(bf16[1024,256]{1,0:T(8,128)(2,1)S(1)} %slice.552), channel_id=1, source_target_pairs={{0,16},{2,18},{4,20},{6,22},{8,24},{10,26},{12,28},{14,30},{16,0},... | collective-permute-start | bytes 1572872 | tf_op jit(solution)/shard_map/ppermute | solution.py:834
  948.5 69.1 %collective-permute-start.60 = (f32[296,128]{1,0:T(8,128)}, f32[296,128]{1,0:T(8,128)S(1)}, u32[]{:S(2)}, u32[]{:S(2)}) collective-permute-start(f32[296,128]{1,0:T(8,128)} %pad_bitcast_fusion), channel_id=1, source_target_pairs={{0,16},{2,18},{4,20},{6,22},{8,24},{10,26},{12,28},{14,30},{16,0},... | collective-permute-start | bytes 454664 | tf_op jit(solution)/shard_map/ppermute | solution.py:834
  1015.3 52.3 %collective-permute-start.66 = (bf16[256,1664]{1,0:T(8,128)(2,1)}, bf16[256,1664]{1,0:T(8,128)(2,1)}, u32[]{:S(2)}, u32[]{:S(2)}) collective-permute-start(bf16[256,1664]{1,0:T(8,128)(2,1)} %slice.549), channel_id=1, source_target_pairs={{0,16},{2,18},{4,20},{6,22},{8,24},{10,26},{12,28},{14,30},{16,0},... | collective-permute-start | bytes 2555912 | tf_op jit(solution)/shard_map/ppermute | solution.py:834
  (146 other events, 3330.5 us)

commit v5 on v3

--- a/solution.py
+++ b/solution.py
@@ -1125,7 +1125,7 @@
     def sent_home(back, *others):
         return outer_sum(sending, lay.tie(back, *others)).astype(bf)
 
-    branch_own = lay.own_of([(0, 0, 0, 0, hidden_here)], [lay.tie(hidden, feed_terms[0], grad_second)], [down_pieces], nn, features)
+    branch_own = lay.own_of([(0, 0, 0, 0, hidden_here)], [lay.tie(hidden, grad_proj_first)], [down_pieces], nn, features)
     output = sent_home(sent_out((middle + live_own * branch_own).astype(bf), out_sent[0]), first_sent[2])
     tokens_grad = sent_home(sent_out(grad_tokens), *second_sent[1:])
 

time: 1100 us -> 1120 us (1.018)
  waiting for transfers between devices: 475 us -> 497 us
    ppermute x32, waiting for transfers between devices: 260 us -> 311 us  [flip(): return lax.ppermute(values, 'dp', [(n, n ^ bit) for n in range(self.ways)])]
    ppermute x30, waiting for transfers between devices: 154 us -> 129 us  [ring(): line.append(lax.ppermute(values, 'dp', pairs))]
  transfers between devices with their start and end apart: 79 -> 79, of which waited for: 36 -> 33; matrix products, arithmetic and copies ran while one was open for 22% -> 21% of each run, Pallas kernels for 19% -> 19%
where the time goes in v5:
time: 1120 us; the launch traced here: 1110 us
  waiting for transfers between devices  497 us (44%)
  Pallas kernels  241 us (22%)
  matrix products  130 us (12%)
  starting transfers between devices  99.9 us (9%)
  local copies, waits for them, and re-layouts  73.6 us (7%)
  other arithmetic  70.1 us (6%)
    ppermute x32, waiting for transfers between devices, flip(): return lax.ppermute(values, 'dp', [(n, n ^ bit) for n in range(self.ways)])  311 us
    pallas_call x13, Pallas kernels, call(): pl.pallas_call(body, grid=grid, scratch_shapes=scratch, in_specs=in_specs...  147 us
    ppermute x30, waiting for transfers between devices, ring(): line.append(lax.ppermute(values, 'dp', pairs))  129 us
    dot_general x24, matrix products, outer_sum(): lax.dot_general(left, right, (((0,), (0,)), ((), ())), preferred_element_...  116 us
    pallas_call x2, Pallas kernels, mixer_backward(): pl.pallas_call(body, grid_spec=pltpu.PrefetchScalarGridSpec(num_scalar_pr...  57.5 us
    all_to_all x4, waiting for transfers between devices, exchange(): lax.all_to_all(values, ('dp', 'tensor'), split_axis=0, concat_axis=0, til...  54.9 us
    ppermute x32, starting transfers between devices, flip(): return lax.ppermute(values, 'dp', [(n, n ^ bit) for n in range(self.ways)])  45.1 us
    ppermute x30, starting transfers between devices, ring(): line.append(lax.ppermute(values, 'dp', pairs))  34.3 us
  transfers between devices with their start and end apart: 79, of which 33 were waited for; matrix products, arithmetic and copies ran while one was open for 21% of the time, Pallas kernels for 19%

profile of v5, /device:TPU:0, one launch (start us, length us, event | category | flops | bytes accessed | tf_op | source)
XLA Modules:
  0.0 1114.3 jit_solution(687121588628486397)
XLA Ops:
  34.8 51.5 %collective-permute-done.5 = bf16[256,1664]{1,0:T(8,128)(2,1)} collective-permute-done((bf16[256,1664]{1,0:T(8,128)(2,1)}, bf16[256,1664]{1,0:T(8,128)(2,1)}, u32[]{:S(2)}, u32[]{:S(2)}) %collective-permute-start.5) | collective-permute-done | bytes 852000 | tf_op jit(solution)/shard_map/ppermute | solution.py:834
  96.9 12.9 %collective-permute-done.6 = bf16[128,1536]{1,0:T(8,128)(2,1)S(1)} collective-permute-done((bf16[128,1536]{1,0:T(8,128)(2,1)S(1)}, bf16[128,1536]{1,0:T(8,128)(2,1)S(1)}, u32[]{:S(2)}, u32[]{:S(2)}) %collective-permute-start.6) | collective-permute-done | bytes 393248 | tf_op jit(solution)/shard_map/ppermute | solution.py:834
  112.6 18.4 %collective-permute-done.11.refs_3_.refs_7_.refs_5_ = bf16[512,1664]{1,0:T(8,128)(2,1)} collective-permute-done((bf16[512,1664]{1,0:T(8,128)(2,1)}, bf16[512,1664]{1,0:T(8,128)(2,1)}, u32[]{:S(2)}, u32[]{:S(2)}) %collective-permute-start.11) | collective-permute-done | bytes 1703968 | tf_op jit(solution)/shard_map/ppermute | solution.py:830
  150.4 32.7 %collective-permute-done.15 = bf16[2432,128]{1,0:T(8,128)(2,1)} collective-permute-done((bf16[2432,128]{1,0:T(8,128)(2,1)}, bf16[2432,128]{1,0:T(8,128)(2,1)}, u32[]{:S(2)}, u32[]{:S(2)}) %collective-permute-start.15) | collective-permute-done | bytes 622624 | tf_op jit(solution)/shard_map/ppermute | solution.py:834
  191.9 19.2 %collective-permute-done.16 = bf16[1024,256]{1,0:T(8,128)(2,1)S(1)} collective-permute-done((bf16[1024,256]{1,0:T(8,128)(2,1)S(1)}, bf16[1024,256]{1,0:T(8,128)(2,1)S(1)}, u32[]{:S(2)}, u32[]{:S(2)}) %collective-permute-start.16) | collective-permute-done | bytes 524320 | tf_op jit(solution)/shard_map/ppermute | solution.py:834
  219.4 12.7 %project.3 = (bf16[1024,1536]{1,0:T(8,128)(2,1)}, f32[1024,128]{1,0:T(8,128)}) custom-call(bf16[1024,2048]{1,0:T(8,128)(2,1)} %pad_maximum_fusion.rows_ref, bf16[512,1664]{1,0:T(8,128)(2,1)} %pad_maximum_fusion.5.refs_0_.refs_4_.refs_2_, bf16[512,1664]{1,0:T(8,128)(2,1)} %collective-permute-done.8.refs_1_.refs_5_.refs_3_, ...), custom_call_target="tpu_custom_call" | custom-call | flops 6442450944 | bytes 13631488 | tf_op jit(solution)/shard_map/project/pallas_call | solution.py:581
  232.1 14.8 %collective-permute-done.13.refs_3_.refs_9_ = bf16[512,1536]{1,0:T(8,128)(2,1)} collective-permute-done((bf16[512,1536]{1,0:T(8,128)(2,1)}, bf16[512,1536]{1,0:T(8,128)(2,1)}, u32[]{:S(2)}, u32[]{:S(2)}) %collective-permute-start.13) | collective-permute-done | bytes 1572896 | tf_op jit(solution)/shard_map/ppermute | solution.py:830
  248.2 16.1 %mixer_forward.2 = (bf16[2,2,2,128,1024]{4,3,2,1,0:T(8,128)(2,1)}, bf16[4,4,128,256]{3,2,1,0:T(8,128)(2,1)}, bf16[4,4,128,128]{3,2,1,0:T(8,128)(2,1)}) custom-call(s32[1]{0:T(128)} %bitcast.3.refs_0_.core_ref, bf16[2,2,2,128,1536]{4,3,2,1,0:T(8,128)(2,1)} %bitcast.129, f32[2,2,2,128,128]{4,3,2,1,0:T(8,128)} %bitcast.134, ...), custom_call_target="tpu_custom_call" | custom-call | flops 16000000000 | bytes 16777216 | tf_op jit(solution)/shard_map/mixer_forward/pallas_call | solution.py:382
  265.0 11.4 %project.2 = bf16[1024,1536]{1,0:T(8,128)(2,1)} custom-call(bf16[1024,2048]{1,0:T(8,128)(2,1)} %pad_maximum_fusion.rows_ref, bf16[512,1536]{1,0:T(8,128)(2,1)} %pad_maximum_fusion.6.refs_0_.refs_6_, bf16[512,1536]{1,0:T(8,128)(2,1)} %collective-permute-done.9.refs_1_.refs_7_, bf16[512,1536]{1,0:T(8,128)(2,1)} %collective-permute-done.10.refs_2_.refs_8_, ...), custom_call_target="tpu_custom_call" | custom-call | flops 6442450944 | bytes 13631488 | tf_op jit(solution)/shard_map/project/pallas_call | solution.py:581
  278.0 15.8 %mixer_forward.3 = (bf16[2,2,2,128,1024]{4,3,2,1,0:T(8,128)(2,1)}, bf16[4,4,128,256]{3,2,1,0:T(8,128)(2,1)}, bf16[4,4,128,128]{3,2,1,0:T(8,128)(2,1)}) custom-call(s32[1]{0:T(128)} %bitcast.3.refs_0_.core_ref, bf16[2,2,2,128,1536]{4,3,2,1,0:T(8,128)(2,1)} %bitcast.126, f32[2,2,2,128,128]{4,3,2,1,0:T(8,128)} %bitcast.135, ...), custom_call_target="tpu_custom_call", output_to_operand_aliasing={{0}: (8, {})} | custom-call | flops 16000000000 | bytes 16777216 | tf_op jit(solution)/shard_map/mixer_forward/pallas_call | solution.py:382
  330.6 33.8 %all-to-all-done.1 = bf16[32,10,2048]{2,1,0:T(8,128)(2,1)S(1)} async-done(((bf16[32,10,2048]{2,1,0:T(8,128)(2,1)}), bf16[32,10,2048]{2,1,0:T(8,128)(2,1)S(1)}, u32[]{:S(2)}, u32[]{:S(2)}) %all-to-all-start.1) | async-done | bytes 1310752 | tf_op jit(solution)/shard_map/all_to_all | solution.py:974
  365.7 20.2 %collective-permute-done.22 = bf16[256,2048]{1,0:T(8,128)(2,1)} collective-permute-done((bf16[256,2048]{1,0:T(8,128)(2,1)}, bf16[256,2048]{1,0:T(8,128)(2,1)}, u32[]{:S(2)}, u32[]{:S(2)}) %collective-permute-start.22) | collective-permute-done | bytes 1048608 | tf_op jit(solution)/shard_map/ppermute | solution.py:834
  389.3 12.6 %collective-permute-done.26.refs_1_.refs_2_ = bf16[512,2816]{1,0:T(8,128)(2,1)} collective-permute-done((bf16[512,2816]{1,0:T(8,128)(2,1)}, bf16[512,2816]{1,0:T(8,128)(2,1)}, u32[]{:S(2)}, u32[]{:S(2)}) %collective-permute-start.26) | collective-permute-done | bytes 2883616 | tf_op jit(solution)/shard_map/ppermute | solution.py:830
  417.4 22.3 %collective-permute-done.29 = bf16[256,2048]{1,0:T(8,128)(2,1)S(1)} collective-permute-done((bf16[256,2048]{1,0:T(8,128)(2,1)}, bf16[256,2048]{1,0:T(8,128)(2,1)S(1)}, u32[]{:S(2)}, u32[]{:S(2)}) %collective-permute-start.29) | collective-permute-done | bytes 1048608 | tf_op jit(solution)/shard_map/ppermute | solution.py:834
  445.4 21.0 %collective-permute-done.27.refs_2_.refs_3_ = bf16[512,2816]{1,0:T(8,128)(2,1)} collective-permute-done((bf16[512,2816]{1,0:T(8,128)(2,1)}, bf16[512,2816]{1,0:T(8,128)(2,1)}, u32[]{:S(2)}, u32[]{:S(2)}) %collective-permute-start.27) | collective-permute-done | bytes 2883616 | tf_op jit(solution)/shard_map/ppermute | solution.py:830
  466.8 18.8 %feed_forward.1 = (bf16[1024,2816]{1,0:T(8,128)(2,1)}, bf16[1024,1408]{1,0:T(8,128)(2,1)}) custom-call(bf16[1024,2048]{1,0:T(8,128)(2,1)} %pad_maximum_fusion.1.rows_ref, bf16[512,2816]{1,0:T(8,128)(2,1)} %pad_maximum_fusion.4.refs_0_.refs_1_, bf16[512,2816]{1,0:T(8,128)(2,1)} %collective-permute-done.26.refs_1_.refs_2_, ...), custom_call_target="tpu_custom_call" | custom-call | flops 11811160064 | bytes 27262976 | tf_op jit(solution)/shard_map/feed_forward/pallas_call | solution.py:581
  499.4 13.7 %feed_backward.1.refs_0_ = bf16[1024,2816]{1,0:T(8,128)(2,1)} custom-call(bf16[1024,2048]{1,0:T(8,128)(2,1)} %copy-done.22, bf16[1408,512]{1,0:T(8,128)(2,1)} %pad_maximum_fusion.7.refs_0_.refs_1_, bf16[1408,512]{1,0:T(8,128)(2,1)} %collective-permute-done.33.refs_1_.refs_2_, bf16[1408,512]{1,0:T(8,128)(2,1)} %collective-permute-done.35.refs_2_.refs_3_, ...), custom_call_target="tpu_custom_call" | custom-call | flops 5905580032 | bytes 21495808 | tf_op jit(solution)/shard_map/feed_backward/pallas_call | solution.py:581
  513.1 11.8 %wide_given.5 = bf16[512,2048]{1,0:T(8,128)(2,1)} custom-call(bf16[1024,2816]{1,0:T(8,128)(2,1)} %feed_backward.1.refs_0_, bf16[512,2816]{1,0:T(8,128)(2,1)} %pad_maximum_fusion.4.refs_0_.refs_1_, bf16[512,2816]{1,0:T(8,128)(2,1)} %collective-permute-done.26.refs_1_.refs_2_, bf16[512,2816]{1,0:T(8,128)(2,1)} %collective-permute-done.27.refs_2_.refs_3_, ...), custom_call_target="tpu_custom_call" | custom-call | flops 5905580032 | bytes 24117248 | tf_op jit(solution)/shard_map/wide_given/pallas_call | solution.py:581
  530.6 12.0 %wide_kept.5 = (bf16[256,2048]{1,0:T(8,128)(2,1)}, f32[256,2048]{1,0:T(8,128)}) custom-call(bf16[1024,2816]{1,0:T(8,128)(2,1)} %feed_backward.1.refs_0_, bf16[512,2816]{1,0:T(8,128)(2,1)} %pad_maximum_fusion.4.refs_0_.refs_1_, bf16[512,2816]{1,0:T(8,128)(2,1)} %collective-permute-done.26.refs_1_.refs_2_, ...), custom_call_target="tpu_custom_call" | custom-call | flops 5905580032 | bytes 24117248 | tf_op jit(solution)/shard_map/wide_kept/pallas_call | solution.py:581
  581.8 15.4 %collective-permute-done.46 = bf16[1408,512]{1,0:T(8,128)(2,1)} collective-permute-done((bf16[1408,512]{1,0:T(8,128)(2,1)}, bf16[1408,512]{1,0:T(8,128)(2,1)}, u32[]{:S(2)}, u32[]{:S(2)}) %collective-permute-start.46) | collective-permute-done | bytes 1441824 | tf_op jit(solution)/shard_map/ppermute | solution.py:830
  607.2 22.6 %collective-permute-done.42 = bf16[512,2816]{1,0:T(8,128)(2,1)} collective-permute-done((bf16[512,2816]{1,0:T(8,128)(2,1)}, bf16[512,2816]{1,0:T(8,128)(2,1)}, u32[]{:S(2)}, u32[]{:S(2)}) %collective-permute-start.42) | collective-permute-done | bytes 2883616 | tf_op jit(solution)/shard_map/ppermute | solution.py:830
  642.0 8.9 heads_backward.1
  650.9 28.7 %mixer_backward.2 = (bf16[2,2,2,128,1664]{4,3,2,1,0:T(8,128)(2,1)}, f32[4,1024]{1,0:T(4,128)}, f32[8,128]{1,0:T(8,128)}, f32[8,256]{1,0:T(8,128)}) custom-call(s32[1]{0:T(128)} %bitcast.3.refs_0_.core_ref, bf16[2,2,2,128,1536]{4,3,2,1,0:T(8,128)(2,1)} %bitcast.130, bf16[2,2,2,128,1536]{4,3,2,1,0:T(8,128)(2,1)} %bitcast.131, ...), custom_call_target="tpu_custom_call" | custom-call | flops 30000001024 | bytes 31457280 | tf_op jit(solution)/shard_map/mixer_backward/pallas_call | solution.py:468
  699.1 28.8 %mixer_backward.3 = (bf16[2,2,2,128,1664]{4,3,2,1,0:T(8,128)(2,1)}, f32[4,1024]{1,0:T(4,128)}, f32[8,128]{1,0:T(8,128)}, f32[8,256]{1,0:T(8,128)}) custom-call(s32[1]{0:T(128)} %bitcast.3.refs_0_.core_ref, bf16[2,2,2,128,1536]{4,3,2,1,0:T(8,128)(2,1)} %bitcast.127, bf16[2,2,2,128,1536]{4,3,2,1,0:T(8,128)(2,1)} %bitcast.128, ...), custom_call_target="tpu_custom_call" | custom-call | flops 30000001024 | bytes 31457280 | tf_op jit(solution)/shard_map/mixer_backward/pallas_call | solution.py:468
  742.3 13.3 %wide_given.7 = bf16[512,2048]{1,0:T(8,128)(2,1)} custom-call(bf16[1024,1664]{1,0:T(8,128)(2,1)} %bitcast.121, bf16[1024,1664]{1,0:T(8,128)(2,1)} %bitcast.77, bf16[512,1664]{1,0:T(8,128)(2,1)} %pad_maximum_fusion.5.refs_0_.refs_4_.refs_2_, bf16[512,1664]{1,0:T(8,128)(2,1)} %collective-permute-done.8.refs_1_.refs_5_.refs_3_, ...), custom_call_target="tpu_custom_call" | custom-call | flops 6710886400 | bytes 25690112 | tf_op jit(solution)/shard_map/wide_given/pallas_call | solution.py:581
  761.9 8.7 wide_kept.6
  787.9 19.0 %collective-permute-done.44 = bf16[256,2048]{1,0:T(8,128)(2,1)} collective-permute-done((bf16[256,2048]{1,0:T(8,128)(2,1)}, bf16[256,2048]{1,0:T(8,128)(2,1)}, u32[]{:S(2)}, u32[]{:S(2)}) %collective-permute-start.44) | collective-permute-done | bytes 1048608 | tf_op jit(solution)/shard_map/ppermute | solution.py:834
  821.0 13.6 %wide_kept.7 = (bf16[256,2048]{1,0:T(8,128)(2,1)}, f32[256,2048]{1,0:T(8,128)}) custom-call(bf16[1024,1664]{1,0:T(8,128)(2,1)} %bitcast.122, bf16[1024,1664]{1,0:T(8,128)(2,1)} %bitcast.78, bf16[512,1664]{1,0:T(8,128)(2,1)} %pad_maximum_fusion.5.refs_0_.refs_4_.refs_2_, bf16[512,1664]{1,0:T(8,128)(2,1)} %collective-permute-done.8.refs_1_.refs_5_.refs_3_, ...), custom_call_target="tpu_custom_call" | custom-call | flops 6710886400 | bytes 25690112 | tf_op jit(solution)/shard_map/wide_kept/pallas_call | solution.py:581
  847.4 52.8 %collective-permute-done.54 = bf16[256,2048]{1,0:T(8,128)(2,1)S(1)} collective-permute-done((bf16[256,2048]{1,0:T(8,128)(2,1)}, bf16[256,2048]{1,0:T(8,128)(2,1)S(1)}, u32[]{:S(2)}, u32[]{:S(2)}) %collective-permute-start.54) | collective-permute-done | bytes 1048608 | tf_op jit(solution)/shard_map/ppermute | solution.py:834
  949.4 21.1 %all-to-all-done.3 = bf16[32,10,2048]{2,1,0:T(8,128)(2,1)S(1)} async-done(((bf16[32,10,2048]{2,1,0:T(8,128)(2,1)}), bf16[32,10,2048]{2,1,0:T(8,128)(2,1)S(1)}, u32[]{:S(2)}, u32[]{:S(2)}) %all-to-all-start.3) | async-done | bytes 1310752 | tf_op jit(solution)/shard_map/all_to_all | solution.py:974
  990.4 41.8 %collective-permute-done.65 = bf16[256,1536]{1,0:T(8,128)(2,1)S(1)} collective-permute-done((bf16[256,1536]{1,0:T(8,128)(2,1)S(1)}, bf16[256,1536]{1,0:T(8,128)(2,1)S(1)}, u32[]{:S(2)}, u32[]{:S(2)}) %collective-permute-start.65) | collective-permute-done | bytes 786464 | tf_op jit(solution)/shard_map/ppermute | solution.py:834
  1054.7 11.2 %collective-permute-done.70 = bf16[1024,128]{1,0:T(8,128)(2,1)} collective-permute-done((bf16[1024,128]{1,0:T(8,128)(2,1)}, bf16[1024,128]{1,0:T(8,128)(2,1)}, u32[]{:S(2)}, u32[]{:S(2)}) %collective-permute-start.70) | collective-permute-done | bytes 262176 | tf_op jit(solution)/shard_map/ppermute | solution.py:834
  (545 shorter events, 454.2 us)
Async XLA Ops:
  9.2 85.8 %collective-permute-start.1 = (s32[1,4]{1,0:T(1,128)}, s32[1,4]{1,0:T(1,128)}, u32[]{:S(2)}, u32[]{:S(2)}) collective-permute-start(s32[1,4]{1,0:T(1,128)} %param.21), channel_id=1, source_target_pairs={{0,8},{2,10},{4,12},{6,14},{8,0},{10,2},{12,4},{14,6},{16,24},{18,... | collective-permute-start | bytes 56 | tf_op jit(solution)/shard_map/ppermute | solution.py:834
  21.8 64.5 %collective-permute-start.5 = (bf16[256,1664]{1,0:T(8,128)(2,1)}, bf16[256,1664]{1,0:T(8,128)(2,1)}, u32[]{:S(2)}, u32[]{:S(2)}) collective-permute-start(bf16[256,1664]{1,0:T(8,128)(2,1)} %maximum_select_fusion.7), channel_id=1, source_target_pairs={{0,16},{2,18},{4,20},{6,22},{8,24},{10,26},{12,28},{14,30},{16,0},... | collective-permute-start | bytes 2555912 | tf_op jit(solution)/shard_map/ppermute | solution.py:834
  27.4 106.1 %all-to-all-start = ((bf16[32,10,2176]{2,1,0:T(8,128)(2,1)}), bf16[32,10,2176]{2,1,0:T(8,128)(2,1)S(1)}, u32[]{:S(2)}, u32[]{:S(2)}) async-start(bf16[32,10,2176]{2,1,0:T(8,128)(2,1)} %all_to_all.32), calls=%async_computation | async-start | bytes 4456448 | tf_op jit(solution)/shard_map/all_to_all | solution.py:974
  96.3 53.7 %collective-permute-start.8 = (bf16[512,1664]{1,0:T(8,128)(2,1)}, bf16[512,1664]{1,0:T(8,128)(2,1)}, u32[]{:S(2)}, u32[]{:S(2)}) collective-permute-start(bf16[512,1664]{1,0:T(8,128)(2,1)} %pad_maximum_fusion.5.refs_0_.refs_4_.refs_2_), channel_id=1, source_target_pairs={{0,4},{2,0},{4,6},{6,2},{8,12},{10,8},{12,14},{14,10},{16,20},{18,... | collective-permute-start | bytes 5111816 | tf_op jit(solution)/shard_map/ppermute | solution.py:830
  131.0 58.4 %collective-permute-start.12 = (bf16[512,1664]{1,0:T(8,128)(2,1)}, bf16[512,1664]{1,0:T(8,128)(2,1)}, u32[]{:S(2)}, u32[]{:S(2)}) collective-permute-start(bf16[512,1664]{1,0:T(8,128)(2,1)} %collective-permute-done.11.refs_3_.refs_7_.refs_5_), channel_id=1, source_target_pairs={{0,2},{2,6},{4,0},{6,4},{8,10},{10,14},{12,8},{14,12},{16,18},{18,... | collective-permute-start | bytes 5111816 | tf_op jit(solution)/shard_map/ppermute | solution.py:830
  150.0 63.2 %collective-permute-start.9 = (bf16[512,1536]{1,0:T(8,128)(2,1)}, bf16[512,1536]{1,0:T(8,128)(2,1)}, u32[]{:S(2)}, u32[]{:S(2)}) collective-permute-start(bf16[512,1536]{1,0:T(8,128)(2,1)} %pad_maximum_fusion.6.refs_0_.refs_6_), channel_id=1, source_target_pairs={{0,4},{2,0},{4,6},{6,2},{8,12},{10,8},{12,14},{14,10},{16,20},{18,... | collective-permute-start | bytes 4718600 | tf_op jit(solution)/shard_map/ppermute | solution.py:830
  218.7 75.0 %collective-permute-start.17 = (bf16[256,2816]{1,0:T(8,128)(2,1)S(1)}, bf16[256,2816]{1,0:T(8,128)(2,1)S(1)}, u32[]{:S(2)}, u32[]{:S(2)}) collective-permute-start(bf16[256,2816]{1,0:T(8,128)(2,1)S(1)} %maximum_select_fusion), channel_id=1, source_target_pairs={{0,16},{2,18},{4,20},{6,22},{8,24},{10,26},{12,28},{14,30},{16,0},... | collective-permute-start | bytes 4325384 | tf_op jit(solution)/shard_map/ppermute | solution.py:834
  309.3 55.1 %all-to-all-start.1 = ((bf16[32,10,2048]{2,1,0:T(8,128)(2,1)}), bf16[32,10,2048]{2,1,0:T(8,128)(2,1)S(1)}, u32[]{:S(2)}, u32[]{:S(2)}) async-start(bf16[32,10,2048]{2,1,0:T(8,128)(2,1)} %all_to_all.35), calls=%async_computation.1 | async-start | bytes 4194304 | tf_op jit(solution)/shard_map/all_to_all | solution.py:974
  314.7 87.2 %collective-permute-start.26 = (bf16[512,2816]{1,0:T(8,128)(2,1)}, bf16[512,2816]{1,0:T(8,128)(2,1)}, u32[]{:S(2)}, u32[]{:S(2)}) collective-permute-start(bf16[512,2816]{1,0:T(8,128)(2,1)} %pad_maximum_fusion.4.refs_0_.refs_1_), channel_id=1, source_target_pairs={{0,4},{2,0},{4,6},{6,2},{8,12},{10,8},{12,14},{14,10},{16,20},{18,... | collective-permute-start | bytes 8650760 | tf_op jit(solution)/shard_map/ppermute | solution.py:830
  316.5 88.3 %collective-permute-start.28 = (bf16[512,2816]{1,0:T(8,128)(2,1)}, bf16[512,2816]{1,0:T(8,128)(2,1)}, u32[]{:S(2)}, u32[]{:S(2)}) collective-permute-start(bf16[512,2816]{1,0:T(8,128)(2,1)} %pad_maximum_fusion.4.refs_0_.refs_1_), channel_id=1, source_target_pairs={{0,2},{2,6},{4,0},{6,4},{8,10},{10,14},{12,8},{14,12},{16,18},{18,... | collective-permute-start | bytes 8650760 | tf_op jit(solution)/shard_map/ppermute | solution.py:830
  324.2 61.7 %collective-permute-start.22 = (bf16[256,2048]{1,0:T(8,128)(2,1)}, bf16[256,2048]{1,0:T(8,128)(2,1)}, u32[]{:S(2)}, u32[]{:S(2)}) collective-permute-start(bf16[256,2048]{1,0:T(8,128)(2,1)} %get-tuple-element.142), channel_id=1, source_target_pairs={{0,8},{2,10},{4,12},{6,14},{8,0},{10,2},{12,4},{14,6},{16,24},{18,... | collective-permute-start | bytes 3145736 | tf_op jit(solution)/shard_map/ppermute | solution.py:834
  328.2 74.1 %collective-permute-start.32 = (bf16[1408,256]{1,0:T(8,128)(2,1)}, bf16[1408,256]{1,0:T(8,128)(2,1)}, u32[]{:S(2)}, u32[]{:S(2)}) collective-permute-start(bf16[1408,256]{1,0:T(8,128)(2,1)} %maximum_select_fusion.9), channel_id=1, source_target_pairs={{0,16},{2,18},{4,20},{6,22},{8,24},{10,26},{12,28},{14,30},{16,0},... | collective-permute-start | bytes 2162696 | tf_op jit(solution)/shard_map/ppermute | solution.py:834
  401.9 64.5 %collective-permute-start.27 = (bf16[512,2816]{1,0:T(8,128)(2,1)}, bf16[512,2816]{1,0:T(8,128)(2,1)}, u32[]{:S(2)}, u32[]{:S(2)}) collective-permute-start(bf16[512,2816]{1,0:T(8,128)(2,1)} %collective-permute-done.26.refs_1_.refs_2_), channel_id=1, source_target_pairs={{0,4},{2,0},{4,6},{6,2},{8,12},{10,8},{12,14},{14,10},{16,20},{18,... | collective-permute-start | bytes 8650760 | tf_op jit(solution)/shard_map/ppermute | solution.py:830
  565.5 64.3 %collective-permute-start.42 = (bf16[512,2816]{1,0:T(8,128)(2,1)}, bf16[512,2816]{1,0:T(8,128)(2,1)}, u32[]{:S(2)}, u32[]{:S(2)}) collective-permute-start(bf16[512,2816]{1,0:T(8,128)(2,1)} %convolution_convert_fusion.1), channel_id=1, source_target_pairs={{0,4},{2,0},{4,6},{6,2},{8,12},{10,8},{12,14},{14,10},{16,20},{18,... | collective-permute-start | bytes 8650760 | tf_op jit(solution)/shard_map/ppermute | solution.py:830
  597.2 100.2 %collective-permute-start.47 = (bf16[512,2816]{1,0:T(8,128)(2,1)}, bf16[512,2816]{1,0:T(8,128)(2,1)S(1)}, u32[]{:S(2)}, u32[]{:S(2)}) collective-permute-start(bf16[512,2816]{1,0:T(8,128)(2,1)} %convolution_convert_fusion), channel_id=1, source_target_pairs={{0,2},{2,6},{4,0},{6,4},{8,10},{10,14},{12,8},{14,12},{16,18},{18,... | collective-permute-start | bytes 8650760 | tf_op jit(solution)/shard_map/ppermute | solution.py:830
  604.8 178.7 %collective-permute-start.73 = (bf16[1408,256]{1,0:T(8,128)(2,1)S(1)}, bf16[1408,256]{1,0:T(8,128)(2,1)}, u32[]{:S(2)}, u32[]{:S(2)}) collective-permute-start(bf16[1408,256]{1,0:T(8,128)(2,1)S(1)} %slice.551), channel_id=1, source_target_pairs={{0,16},{2,18},{4,20},{6,22},{8,24},{10,26},{12,28},{14,30},{16,0},... | collective-permute-start | bytes 2162696 | tf_op jit(solution)/shard_map/ppermute | solution.py:834
  636.3 105.9 %collective-permute-start.52 = (bf16[512,2816]{1,0:T(8,128)(2,1)}, bf16[512,2816]{1,0:T(8,128)(2,1)}, u32[]{:S(2)}, u32[]{:S(2)}) collective-permute-start(bf16[512,2816]{1,0:T(8,128)(2,1)} %add_convert_fusion), channel_id=1, source_target_pairs={{0,4},{2,0},{4,6},{6,2},{8,12},{10,8},{12,14},{14,10},{16,20},{18,... | collective-permute-start | bytes 8650760 | tf_op jit(solution)/shard_map/ppermute | solution.py:830
  687.7 74.2 %collective-permute-start.43 = (bf16[512,2048]{1,0:T(8,128)(2,1)}, bf16[512,2048]{1,0:T(8,128)(2,1)}, u32[]{:S(2)}, u32[]{:S(2)}) collective-permute-start(bf16[512,2048]{1,0:T(8,128)(2,1)} %wide_given.6), channel_id=1, source_target_pairs={{0,1},{1,0},{2,3},{3,2},{4,5},{5,4},{6,7},{7,6},{8,9},{9,8},{10,11... | collective-permute-start | bytes 6291464 | tf_op jit(solution)/shard_map/ppermute | solution.py:840
  755.6 65.4 %collective-permute-start.53 = (bf16[512,2048]{1,0:T(8,128)(2,1)}, bf16[512,2048]{1,0:T(8,128)(2,1)}, u32[]{:S(2)}, u32[]{:S(2)}) collective-permute-start(bf16[512,2048]{1,0:T(8,128)(2,1)} %wide_given.7), channel_id=1, source_target_pairs={{0,1},{1,0},{2,3},{3,2},{4,5},{5,4},{6,7},{7,6},{8,9},{9,8},{10,11... | collective-permute-start | bytes 6291464 | tf_op jit(solution)/shard_map/ppermute | solution.py:840
  783.5 254.8 %collective-permute-start.71 = (bf16[256,2816]{1,0:T(8,128)(2,1)}, bf16[256,2816]{1,0:T(8,128)(2,1)}, u32[]{:S(2)}, u32[]{:S(2)}) collective-permute-start(bf16[256,2816]{1,0:T(8,128)(2,1)} %slice.548), channel_id=1, source_target_pairs={{0,16},{2,18},{4,20},{6,22},{8,24},{10,26},{12,28},{14,30},{16,0},... | collective-permute-start | bytes 4325384 | tf_op jit(solution)/shard_map/ppermute | solution.py:834
  785.9 56.1 %collective-permute-start.50 = (bf16[512,1536]{1,0:T(8,128)(2,1)}, bf16[512,1536]{1,0:T(8,128)(2,1)}, u32[]{:S(2)}, u32[]{:S(2)}) collective-permute-start(bf16[512,1536]{1,0:T(8,128)(2,1)} %convolution_convert_fusion.6), channel_id=1, source_target_pairs={{0,2},{2,6},{4,0},{6,4},{8,10},{10,14},{12,8},{14,12},{16,18},{18,... | collective-permute-start | bytes 4718600 | tf_op jit(solution)/shard_map/ppermute | solution.py:830
  817.3 94.7 %all-to-all-start.2 = ((bf16[32,10,2048]{2,1,0:T(8,128)(2,1)}), bf16[32,10,2048]{2,1,0:T(8,128)(2,1)}, u32[]{:S(2)}, u32[]{:S(2)}) async-start(bf16[32,10,2048]{2,1,0:T(8,128)(2,1)} %all_to_all.38), calls=%async_computation.2 | async-start | bytes 4194304 | tf_op jit(solution)/shard_map/all_to_all | solution.py:974
  834.5 65.6 %collective-permute-start.54 = (bf16[256,2048]{1,0:T(8,128)(2,1)}, bf16[256,2048]{1,0:T(8,128)(2,1)S(1)}, u32[]{:S(2)}, u32[]{:S(2)}) collective-permute-start(bf16[256,2048]{1,0:T(8,128)(2,1)} %get-tuple-element.185), channel_id=1, source_target_pairs={{0,8},{2,10},{4,12},{6,14},{8,0},{10,2},{12,4},{14,6},{16,24},{18,... | collective-permute-start | bytes 3145736 | tf_op jit(solution)/shard_map/ppermute | solution.py:834
  839.6 208.0 %collective-permute-start.74 = (bf16[1408,128]{1,0:T(8,128)(2,1)}, bf16[1408,128]{1,0:T(8,128)(2,1)}, u32[]{:S(2)}, u32[]{:S(2)}) collective-permute-start(bf16[1408,128]{1,0:T(8,128)(2,1)} %dynamic-slice_convert_fusion.3), channel_id=1, source_target_pairs={{0,8},{2,10},{4,12},{6,14},{8,0},{10,2},{12,4},{14,6},{16,24},{18,... | collective-permute-start | bytes 1081352 | tf_op jit(solution)/shard_map/ppermute | solution.py:834
  840.1 81.4 %collective-permute-start.58 = (bf16[512,1664]{1,0:T(8,128)(2,1)}, bf16[512,1664]{1,0:T(8,128)(2,1)}, u32[]{:S(2)}, u32[]{:S(2)}) collective-permute-start(bf16[512,1664]{1,0:T(8,128)(2,1)} %convolution_convert_fusion.4), channel_id=1, source_target_pairs={{0,4},{2,0},{4,6},{6,2},{8,12},{10,8},{12,14},{14,10},{16,20},{18,... | collective-permute-start | bytes 5111816 | tf_op jit(solution)/shard_map/ppermute | solution.py:830
  846.8 72.9 %collective-permute-start.51 = (bf16[512,1536]{1,0:T(8,128)(2,1)}, bf16[512,1536]{1,0:T(8,128)(2,1)}, u32[]{:S(2)}, u32[]{:S(2)}) collective-permute-start(bf16[512,1536]{1,0:T(8,128)(2,1)} %fusion.10), channel_id=1, source_target_pairs={{0,2},{2,6},{4,0},{6,4},{8,10},{10,14},{12,8},{14,12},{16,18},{18,... | collective-permute-start | bytes 4718600 | tf_op jit(solution)/shard_map/ppermute | solution.py:830
  912.0 58.5 %all-to-all-start.3 = ((bf16[32,10,2048]{2,1,0:T(8,128)(2,1)}), bf16[32,10,2048]{2,1,0:T(8,128)(2,1)S(1)}, u32[]{:S(2)}, u32[]{:S(2)}) async-start(bf16[32,10,2048]{2,1,0:T(8,128)(2,1)} %all_to_all.41), calls=%async_computation.3 | async-start | bytes 4194304 | tf_op jit(solution)/shard_map/all_to_all | solution.py:974
  919.7 59.9 %collective-permute-start.55 = (bf16[512,1664]{1,0:T(8,128)(2,1)}, bf16[512,1664]{1,0:T(8,128)(2,1)}, u32[]{:S(2)}, u32[]{:S(2)}) collective-permute-start(bf16[512,1664]{1,0:T(8,128)(2,1)} %convolution_convert_fusion.3), channel_id=1, source_target_pairs={{0,2},{2,6},{4,0},{6,4},{8,10},{10,14},{12,8},{14,12},{16,18},{18,... | collective-permute-start | bytes 5111816 | tf_op jit(solution)/shard_map/ppermute | solution.py:830
  927.6 54.4 %collective-permute-start.59 = (bf16[512,1664]{1,0:T(8,128)(2,1)}, bf16[512,1664]{1,0:T(8,128)(2,1)}, u32[]{:S(2)}, u32[]{:S(2)}) collective-permute-start(bf16[512,1664]{1,0:T(8,128)(2,1)} %add_convert_fusion.1), channel_id=1, source_target_pairs={{0,4},{2,0},{4,6},{6,2},{8,12},{10,8},{12,14},{14,10},{16,20},{18,... | collective-permute-start | bytes 5111816 | tf_op jit(solution)/shard_map/ppermute | solution.py:830
  973.3 60.0 %collective-permute-start.69 = (bf16[1024,256]{1,0:T(8,128)(2,1)}, bf16[1024,256]{1,0:T(8,128)(2,1)S(1)}, u32[]{:S(2)}, u32[]{:S(2)}) collective-permute-start(bf16[1024,256]{1,0:T(8,128)(2,1)} %slice.552), channel_id=1, source_target_pairs={{0,16},{2,18},{4,20},{6,22},{8,24},{10,26},{12,28},{14,30},{16,0},... | collective-permute-start | bytes 1572872 | tf_op jit(solution)/shard_map/ppermute | solution.py:834
  982.0 70.6 %collective-permute-start.61 = (f32[296,128]{1,0:T(8,128)S(1)}, f32[296,128]{1,0:T(8,128)}, u32[]{:S(2)}, u32[]{:S(2)}) collective-permute-start(f32[296,128]{1,0:T(8,128)S(1)} %fusion.102), channel_id=1, source_target_pairs={{0,8},{2,10},{4,12},{6,14},{8,0},{10,2},{12,4},{14,6},{16,24},{18,... | collective-permute-start | bytes 454664 | tf_op jit(solution)/shard_map/ppermute | solution.py:834
  1032.2 60.9 %collective-permute-start.66 = (bf16[256,1664]{1,0:T(8,128)(2,1)}, bf16[256,1664]{1,0:T(8,128)(2,1)}, u32[]{:S(2)}, u32[]{:S(2)}) collective-permute-start(bf16[256,1664]{1,0:T(8,128)(2,1)} %slice.549), channel_id=1, source_target_pairs={{0,16},{2,18},{4,20},{6,22},{8,24},{10,26},{12,28},{14,30},{16,0},... | collective-permute-start | bytes 2555912 | tf_op jit(solution)/shard_map/ppermute | solution.py:834
  (148 other events, 3620.6 us)
